TPU v7x, 32 devices: a whole 2x2x4 slice. The times are simulated.
32 devices in a mesh: ctx: 8 (over z, y), fsdp: 4 (over x, core).
Axes of the slice: x: 2, y: 2, z: 4, core: 2. Of those that a mesh axis runs over, the one named last changes fastest.
Arguments:
- block_in: bfloat16 [4, 1024, 2304], P('fsdp', 'ctx'), may hold values from -6 to 6
- stretch_order: int32 [8, 2], replicated, may hold values from 0 to 15, as said below
- weight_query: bfloat16 [2304, 2048], P(None, ('fsdp', 'ctx')), may hold values from -0.625 to 0.625
- weight_key: bfloat16 [2304, 1024], P(None, ('fsdp', 'ctx')), may hold values from -0.125 to 0.125
- weight_value: bfloat16 [2304, 1024], P(None, ('fsdp', 'ctx')), may hold values from -0.125 to 0.125
- weight_output: bfloat16 [2048, 2304], P(('fsdp', 'ctx')), may hold values from -0.125 to 0.125
- weight_gate: bfloat16 [2304, 9216], P(None, ('fsdp', 'ctx')), may hold values from -0.125 to 0.125
- weight_up: bfloat16 [2304, 9216], P(None, ('fsdp', 'ctx')), may hold values from -0.125 to 0.125
- weight_down: bfloat16 [9216, 2304], P(('fsdp', 'ctx')), may hold values from -0.0625 to 0.0625
- gain_preattn: float32 [2304], P(('ctx', 'fsdp')), may hold values from 0.1 to 1.9
- gain_postattn: float32 [2304], P(('ctx', 'fsdp')), may hold values from 0.1 to 1.9
- gain_premlp: float32 [2304], P(('ctx', 'fsdp')), may hold values from 0.1 to 1.9
- gain_postmlp: float32 [2304], P(('ctx', 'fsdp')), may hold values from 0.1 to 1.9
- grad_out: bfloat16 [4, 1024, 2304], P('fsdp', 'ctx'), may hold values from -6 to 6
Outputs:
- block_out: bfloat16 [4, 1024, 2304], P('fsdp', 'ctx')
- grad_in: float32 [4, 1024, 2304], P('fsdp', 'ctx')
- grad_query: float32 [2304, 2048], P(None, ('fsdp', 'ctx'))
- grad_key: float32 [2304, 1024], P(None, ('fsdp', 'ctx'))
- grad_value: float32 [2304, 1024], P(None, ('fsdp', 'ctx'))
- grad_output: float32 [2048, 2304], P(('fsdp', 'ctx'))
- grad_gate: float32 [2304, 9216], P(None, ('fsdp', 'ctx'))
- grad_up: float32 [2304, 9216], P(None, ('fsdp', 'ctx'))
- grad_down: float32 [9216, 2304], P(('fsdp', 'ctx'))
- grad_preattn: float32 [2304], P(('ctx', 'fsdp'))
- grad_postattn: float32 [2304], P(('ctx', 'fsdp'))
- grad_premlp: float32 [2304], P(('ctx', 'fsdp'))
- grad_postmlp: float32 [2304], P(('ctx', 'fsdp'))
Inputs may be any that keep to these rules, and one draw needn't show every extreme that they name: `stretch_order`: row c holds the stretch numbers p and 15 - p, where p runs over a permutation of 0 to 7.
All inputs are finite; a program needn't handle non-finite values.
Results may differ from a plain program's by a relative error of at most 0.028.
The roundings to bfloat16 on the way count: a program that leaves them out, or rounds other values in their place, can miss the bound.
Values may be sent and summed in bfloat16 or wider, within the bound.
No kernel may reach another device: no remote copies, remote signals or barrier semaphores. Data moves between devices by JAX's collectives and lax.ppermute only.
A program may use at most 192 MiB of HBM per device.

v0:
```python
import functools
import math

import jax
import jax.numpy as jnp
from jax import lax
from jax.sharding import PartitionSpec as P

HEAD_DIM = 256


EPS = 1e-06
CAP = 50.0
NEGATIVE = -1e30


def passed_along(block, axis, distance):
    devices = range(lax.axis_size(axis))
    route = [((i - distance) % len(devices), i) for i in devices]
    return lax.ppermute(block, axis, route)


def rms_norm(values, gain):
    return values * lax.rsqrt(jnp.mean(values * values, axis=-1, keepdims=True) + EPS) * gain


def norm_back(values, gain, cotangent):
    _, pullback = jax.vjp(rms_norm, values, gain)
    return pullback(cotangent)


def rotate(values, cosine, sine):
    middle = values.shape[-1] // 2
    first = values[..., :middle]
    second = values[..., middle:]
    return jnp.concatenate(
        [first * cosine - second * sine, second * cosine + first * sine], axis=-1
    )


def angles(positions, width):
    steps = jnp.arange(width // 2, dtype=jnp.float32)
    inverse = jnp.exp(steps * (-2.0 * math.log(10000.0) / width))
    return positions.astype(jnp.float32)[:, None] * inverse[None, :]


def place(order, start, number, half):
    storage = start + jnp.arange(number, dtype=jnp.int32)
    stretch_index = storage // half
    table = jnp.arange(order.shape[0], dtype=jnp.int32)
    picked = jnp.sum(jnp.where(stretch_index[:, None] == table[None, :], order[None, :], 0), axis=1)
    return picked * half + storage % half


def capped_scores(queries, keys):
    raw = jnp.einsum("sjgqd,skjd->sjgqk", queries, keys, preferred_element_type=jnp.float32)
    return CAP * jnp.tanh(raw / CAP)


def spread(normed):
    return lax.all_gather(normed[None], "fsdp", axis=0, tiled=True)


def collect(partial_sum):
    return lax.psum_scatter(
        partial_sum.astype(jnp.bfloat16), "fsdp", scatter_dimension=0, tiled=True
    ).astype(jnp.float32)[0]


def spread_back(cotangent):
    return lax.all_gather(cotangent.astype(jnp.bfloat16)[None], "fsdp", axis=0, tiled=True)


def collect_back(partial_sum):
    return lax.psum_scatter(
        partial_sum.astype(jnp.bfloat16), "fsdp", scatter_dimension=0, tiled=True
    ).astype(jnp.float32)[0]


def body(
    block_in,
    stretch_order,
    weight_query,
    weight_key,
    weight_value,
    weight_output,
    weight_gate,
    weight_up,
    weight_down,
    gain_preattn,
    gain_postattn,
    gain_premlp,
    gain_postmlp,
    grad_out,
):
    rows_in = block_in[0].astype(jnp.float32)
    local_rows = rows_in.shape[0]
    half = local_rows // 2
    order = stretch_order.reshape(-1)
    query_pos = place(order, lax.axis_index("ctx") * local_rows, local_rows, half)
    angle = angles(query_pos, HEAD_DIM)
    cos_query = jnp.cos(angle)[:, None, None, :]
    sin_query = jnp.sin(angle)[:, None, None, :]
    cos_key = jnp.cos(angle)[:, None, :]
    sin_key = jnp.sin(angle)[:, None, :]
    scale = HEAD_DIM ** (-0.5)
    gathered = (
        lax.all_gather(weight_query, "ctx", axis=1, tiled=True),
        lax.all_gather(weight_key, "ctx", axis=1, tiled=True),
        lax.all_gather(weight_value, "ctx", axis=1, tiled=True),
        lax.all_gather(weight_output, "ctx", axis=0, tiled=True),
        lax.all_gather(weight_gate, "ctx", axis=1, tiled=True),
        lax.all_gather(weight_up, "ctx", axis=1, tiled=True),
        lax.all_gather(weight_down, "ctx", axis=0, tiled=True),
    )
    query_full, key_full, value_full, output_full, gate_full, up_full, down_full = gathered
    gain_one, gain_two, gain_three, gain_four = (
        lax.all_gather(gain_preattn, ("ctx", "fsdp"), axis=0, tiled=True),
        lax.all_gather(gain_postattn, ("ctx", "fsdp"), axis=0, tiled=True),
        lax.all_gather(gain_premlp, ("ctx", "fsdp"), axis=0, tiled=True),
        lax.all_gather(gain_postmlp, ("ctx", "fsdp"), axis=0, tiled=True),
    )
    kv_local = key_full.shape[1] // HEAD_DIM
    group = query_full.shape[1] // (kv_local * HEAD_DIM)
    normed_one = spread(rms_norm(rows_in, gain_one).astype(jnp.bfloat16))
    sequences = normed_one.shape[0]
    query_raw = jnp.einsum(
        "std,dc->stc", normed_one, query_full, preferred_element_type=jnp.float32
    )
    query_raw = query_raw.reshape(sequences, local_rows, kv_local, group, HEAD_DIM)
    query_heads = (
        (rotate(query_raw, cos_query, sin_query) * scale)
        .astype(jnp.bfloat16)
        .transpose(0, 2, 3, 1, 4)
    )
    key_raw = jnp.einsum("std,dc->stc", normed_one, key_full, preferred_element_type=jnp.float32)
    key_local = rotate(
        key_raw.reshape(sequences, local_rows, kv_local, HEAD_DIM), cos_key, sin_key
    ).astype(jnp.bfloat16)
    value_local = jnp.einsum(
        "std,dc->stc", normed_one, value_full, preferred_element_type=jnp.float32
    )
    value_local = value_local.astype(jnp.bfloat16).reshape(
        sequences, local_rows, kv_local, HEAD_DIM
    )
    best = jnp.full((sequences, kv_local, group, local_rows), NEGATIVE, jnp.float32)
    keys = lax.all_gather(key_local, "ctx", axis=1, tiled=True)
    values = lax.all_gather(value_local, "ctx", axis=1, tiled=True)
    key_pos = place(order, jnp.int32(0), keys.shape[1], half)
    capped = capped_scores(query_heads, keys)
    allowed = key_pos[None, None, None, None, :] <= query_pos[None, None, None, :, None]
    new_best = jnp.maximum(best, jnp.max(jnp.where(allowed, capped, NEGATIVE), axis=-1))
    probs = jnp.where(allowed, jnp.exp(capped - new_best[..., None]), 0.0)
    total = jnp.sum(probs, axis=-1)
    weighted = jnp.einsum(
        "sjgqk,skjd->sjgqd", probs.astype(jnp.bfloat16), values, preferred_element_type=jnp.float32
    )
    best, total, weighted = (new_best, total, weighted)
    attn_exact = weighted / total[..., None]
    log_total = best + jnp.log(total)
    mixed = (
        attn_exact.astype(jnp.bfloat16).transpose(0, 3, 1, 2, 4).reshape(sequences, local_rows, -1)
    )
    attn_out = collect(
        jnp.einsum("stc,cd->std", mixed, output_full, preferred_element_type=jnp.float32)
    )
    resid = rows_in + rms_norm(attn_out, gain_two)
    normed_two = spread(rms_norm(resid, gain_three).astype(jnp.bfloat16))
    gate = jnp.einsum("std,dc->stc", normed_two, gate_full, preferred_element_type=jnp.float32)
    up_proj = jnp.einsum("std,dc->stc", normed_two, up_full, preferred_element_type=jnp.float32)
    gelu_tanh = functools.partial(jax.nn.gelu, approximate=True)
    activated, gelu_pull = jax.vjp(gelu_tanh, gate)
    hidden = (activated * up_proj).astype(jnp.bfloat16)
    mlp_out = collect(
        jnp.einsum("stc,cd->std", hidden, down_full, preferred_element_type=jnp.float32)
    )
    block_out = resid + rms_norm(mlp_out, gain_four)
    cotangent = grad_out[0].astype(jnp.float32)
    d_mlp_out, grad_four = norm_back(mlp_out, gain_four, cotangent)
    d_mlp_all = spread_back(d_mlp_out)
    d_hidden = jnp.einsum("std,cd->stc", d_mlp_all, down_full, preferred_element_type=jnp.float32)
    d_gate = gelu_pull(d_hidden * up_proj)[0].astype(jnp.bfloat16)
    d_up = (d_hidden * activated).astype(jnp.bfloat16)
    grad_down_full = jnp.einsum(
        "stc,std->cd", hidden, d_mlp_all, preferred_element_type=jnp.float32
    )
    grad_gate_full = jnp.einsum(
        "std,stc->dc", normed_two, d_gate, preferred_element_type=jnp.float32
    )
    grad_up_full = jnp.einsum("std,stc->dc", normed_two, d_up, preferred_element_type=jnp.float32)
    d_normed_two = collect_back(
        jnp.einsum("stc,dc->std", d_gate, gate_full, preferred_element_type=jnp.float32)
        + jnp.einsum("stc,dc->std", d_up, up_full, preferred_element_type=jnp.float32)
    )
    d_resid_mlp, grad_three = norm_back(resid, gain_three, d_normed_two)
    d_resid = cotangent + d_resid_mlp
    d_attn_out, grad_two = norm_back(attn_out, gain_two, d_resid)
    d_attn_all = spread_back(d_attn_out)
    grad_output_full = jnp.einsum(
        "stc,std->cd", mixed, d_attn_all, preferred_element_type=jnp.float32
    )
    d_mixed = jnp.einsum("std,cd->stc", d_attn_all, output_full, preferred_element_type=jnp.float32)
    d_mixed_heads = d_mixed.astype(jnp.bfloat16).reshape(
        sequences, local_rows, kv_local, group, HEAD_DIM
    )
    d_mixed_heads = d_mixed_heads.transpose(0, 2, 3, 1, 4)
    delta = jnp.sum(d_mixed_heads.astype(jnp.float32) * attn_exact, axis=-1)

    def block_back(d_queries, keys, values, start):
        key_pos = place(order, start, keys.shape[1], half)
        capped = capped_scores(query_heads, keys)
        allowed = key_pos[None, None, None, None, :] <= query_pos[None, None, None, :, None]
        probs = jnp.where(allowed, jnp.exp(capped - log_total[..., None]), 0.0)
        d_values = jnp.einsum(
            "sjgqk,sjgqd->skjd",
            probs.astype(jnp.bfloat16),
            d_mixed_heads,
            preferred_element_type=jnp.float32,
        )
        d_probs = jnp.einsum(
            "sjgqd,skjd->sjgqk", d_mixed_heads, values, preferred_element_type=jnp.float32
        )
        d_scores = (probs * (d_probs - delta[..., None]) * (1.0 - (capped / CAP) ** 2)).astype(
            jnp.bfloat16
        )
        d_queries = d_queries + jnp.einsum(
            "sjgqk,skjd->sjgqd", d_scores, keys, preferred_element_type=jnp.float32
        )
        d_keys = jnp.einsum(
            "sjgqk,sjgqd->skjd", d_scores, query_heads, preferred_element_type=jnp.float32
        )
        return (d_queries, d_keys, d_values)

    query_zeros = jnp.zeros((sequences, kv_local, group, local_rows, HEAD_DIM), jnp.float32)
    own_index = lax.axis_index("ctx")
    members = lax.axis_size("ctx")
    grad_zeros = jnp.zeros(key_local.shape, jnp.float32)
    bundle = jnp.stack(
        [key_local.astype(jnp.float32), value_local.astype(jnp.float32), grad_zeros, grad_zeros]
    )

    def travel_step(turn_index, carry):
        d_queries, bundle = carry
        source = (own_index - turn_index) % members
        d_queries, d_keys, d_values = block_back(
            d_queries,
            bundle[0].astype(jnp.bfloat16),
            bundle[1].astype(jnp.bfloat16),
            source * local_rows,
        )
        bundle = jnp.concatenate([bundle[:2], bundle[2:] + jnp.stack([d_keys, d_values])], axis=0)
        bundle = passed_along(bundle.astype(jnp.bfloat16), "ctx", 1).astype(bundle.dtype)
        return (d_queries, bundle)

    d_queries, bundle = lax.fori_loop(0, members, travel_step, (query_zeros, bundle))
    d_keys = bundle[2]
    d_values = bundle[3]
    d_query_raw = rotate(d_queries.transpose(0, 3, 1, 2, 4) * scale, cos_query, -sin_query)
    d_query_raw = d_query_raw.astype(jnp.bfloat16).reshape(sequences, local_rows, -1)
    d_key_raw = (
        rotate(d_keys, cos_key, -sin_key).astype(jnp.bfloat16).reshape(sequences, local_rows, -1)
    )
    d_value_raw = d_values.astype(jnp.bfloat16).reshape(sequences, local_rows, -1)
    grad_query_full = jnp.einsum(
        "std,stc->dc", normed_one, d_query_raw, preferred_element_type=jnp.float32
    )
    grad_key_full = jnp.einsum(
        "std,stc->dc", normed_one, d_key_raw, preferred_element_type=jnp.float32
    )
    grad_value_full = jnp.einsum(
        "std,stc->dc", normed_one, d_value_raw, preferred_element_type=jnp.float32
    )
    d_normed_one = collect_back(
        jnp.einsum("stc,dc->std", d_query_raw, query_full, preferred_element_type=jnp.float32)
        + jnp.einsum("stc,dc->std", d_key_raw, key_full, preferred_element_type=jnp.float32)
        + jnp.einsum("stc,dc->std", d_value_raw, value_full, preferred_element_type=jnp.float32)
    )
    d_rows_attn, grad_one = norm_back(rows_in, gain_one, d_normed_one)
    grad_in = d_resid + d_rows_attn
    query_sum, key_sum, value_sum, output_sum, gate_sum, up_sum, down_sum = (
        lax.psum_scatter(
            grad_query_full.astype(jnp.bfloat16), "ctx", scatter_dimension=1, tiled=True
        ).astype(jnp.float32),
        lax.psum_scatter(
            grad_key_full.astype(jnp.bfloat16), "ctx", scatter_dimension=1, tiled=True
        ).astype(jnp.float32),
        lax.psum_scatter(
            grad_value_full.astype(jnp.bfloat16), "ctx", scatter_dimension=1, tiled=True
        ).astype(jnp.float32),
        lax.psum_scatter(
            grad_output_full.astype(jnp.bfloat16), "ctx", scatter_dimension=0, tiled=True
        ).astype(jnp.float32),
        lax.psum_scatter(
            grad_gate_full.astype(jnp.bfloat16), "ctx", scatter_dimension=1, tiled=True
        ).astype(jnp.float32),
        lax.psum_scatter(
            grad_up_full.astype(jnp.bfloat16), "ctx", scatter_dimension=1, tiled=True
        ).astype(jnp.float32),
        lax.psum_scatter(
            grad_down_full.astype(jnp.bfloat16), "ctx", scatter_dimension=0, tiled=True
        ).astype(jnp.float32),
    )
    gain_terms = (
        lax.psum_scatter(grad_one, ("ctx", "fsdp"), scatter_dimension=0, tiled=True),
        lax.psum_scatter(grad_two, ("ctx", "fsdp"), scatter_dimension=0, tiled=True),
        lax.psum_scatter(grad_three, ("ctx", "fsdp"), scatter_dimension=0, tiled=True),
        lax.psum_scatter(grad_four, ("ctx", "fsdp"), scatter_dimension=0, tiled=True),
    )
    return (
        block_out[None].astype(jnp.bfloat16),
        grad_in[None],
        query_sum,
        key_sum,
        value_sum,
        output_sum,
        gate_sum,
        up_sum,
        down_sum,
        gain_terms[0],
        gain_terms[1],
        gain_terms[2],
        gain_terms[3],
    )


def solution(mesh):
    placed = (
        P("fsdp", "ctx", None),
        P(),
        P(None, ("fsdp", "ctx")),
        P(None, ("fsdp", "ctx")),
        P(None, ("fsdp", "ctx")),
        P(("fsdp", "ctx"), None),
        P(None, ("fsdp", "ctx")),
        P(None, ("fsdp", "ctx")),
        P(("fsdp", "ctx"), None),
        P(("ctx", "fsdp")),
        P(("ctx", "fsdp")),
        P(("ctx", "fsdp")),
        P(("ctx", "fsdp")),
        P("fsdp", "ctx", None),
    )
    return jax.shard_map(
        body,
        mesh=mesh,
        in_specs=placed,
        out_specs=(
            P("fsdp", "ctx", None),
            P("fsdp", "ctx", None),
            P(None, ("fsdp", "ctx")),
            P(None, ("fsdp", "ctx")),
            P(None, ("fsdp", "ctx")),
            P(("fsdp", "ctx"), None),
            P(None, ("fsdp", "ctx")),
            P(None, ("fsdp", "ctx")),
            P(("fsdp", "ctx"), None),
            P(("ctx", "fsdp")),
            P(("ctx", "fsdp")),
            P(("ctx", "fsdp")),
            P(("ctx", "fsdp")),
        ),
        check_vma=False,
    )
```

profile of v0, /device:TPU:0, one launch (start us, length us, event | category | flops | bytes accessed | tf_op | source)
XLA Modules:
  0.0 2158.7 jit_solution(16452350625945222529)
XLA Ops:
  11.4 43.6 %all-reduce.9 = (f32[2304]{0:T(1024)S(1)}, f32[2304]{0:T(1024)}, f32[2304]{0:T(1024)S(1)}, f32[2304]{0:T(1024)}) all-reduce(f32[2304]{0:T(1024)S(1)} %dynamic-update-slice, f32[2304]{0:T(1024)S(1)} %dynamic-update-slice.2, f32[2304]{0:T(1024)S(1)} %dynamic-update-slice.1, ...), channel_id=1, replica_groups=mesh['ctx'=8,'fsdp'=4] {'ctx','fsdp'}, use_global_device_ids=true, to_apply=%add | all-reduce | flops 9216 | bytes 73728
  60.4 22.0 %all-gather.15.cloned.1.call-done = bf16[4,128,2304]{2,1,0:T(8,128)(2,1)} async-done(((bf16[1,128,2304]{2,1,0:T(8,128)(2,1)}), bf16[4,128,2304]{2,1,0:T(8,128)(2,1)}) %all-gather.15.cloned.1.call-update) | async-done | bytes 2359312 | tf_op jit(solution)/shard_map/all_gather | solution.py:61
  82.5 2.9 convolution_bitcast_fusion.7
  86.3 39.4 %all-gather.23.cloned.1.call-done = bf16[2304,256]{0,1:T(8,128)(2,1)} async-done(((bf16[2304,32]{0,1:T(8,128)(2,1)}), bf16[2304,256]{0,1:T(8,128)(2,1)}) %all-gather.23.cloned.1.call-update) | async-done | bytes 1179664 | tf_op jit(solution)/shard_map/all_gather | solution.py:110
  125.7 3.0 bitcast_convert_fusion.3
  129.8 48.9 %all-gather.17.cloned.1.call-done = bf16[2304,512]{0,1:T(8,128)(2,1)} async-done(((bf16[2304,64]{0,1:T(8,128)(2,1)}), bf16[2304,512]{0,1:T(8,128)(2,1)}) %all-gather.17.cloned.1.call-update) | async-done | bytes 2359312 | tf_op jit(solution)/shard_map/all_gather | solution.py:108
  178.7 4.0 fusion.58
  185.1 44.0 %all-gather.21.cloned.1.call-done = bf16[4,1024,1,256]{3,1,0,2:T(8,128)(2,1)} async-done(((bf16[4,128,1,256]{3,1,0,2:T(8,128)(2,1)}), bf16[4,1024,1,256]{3,1,0,2:T(8,128)(2,1)}) %all-gather.21.cloned.1.call-update) | async-done | bytes 2097168 | tf_op jit(solution)/shard_map/all_gather | solution.py:147
  229.1 3.0 select_reduce_fusion.1
  235.6 43.9 %all-gather.39.cloned.1.call-done = bf16[4,1024,256]{2,1,0:T(8,128)(2,1)} async-done(((bf16[4,128,256]{2,1,0:T(8,128)(2,1)}), bf16[4,1024,256]{2,1,0:T(8,128)(2,1)}) %all-gather.39.cloned.1.call-update) | async-done | bytes 2097168 | tf_op jit(solution)/shard_map/all_gather | solution.py:148
  279.5 3.9 fusion.124
  283.8 48.5 %all-gather.25.cloned.1.call-done = bf16[512,2304]{1,0:T(8,128)(2,1)} async-done(((bf16[64,2304]{1,0:T(8,128)(2,1)}), bf16[512,2304]{1,0:T(8,128)(2,1)}) %all-gather.25.cloned.1.call-update) | async-done | bytes 2359312 | tf_op jit(solution)/shard_map/all_gather | solution.py:111
  332.3 4.5 convolution_convert_fusion
  337.3 31.2 %reduce-scatter.12.cloned.1.call-done = bf16[1,128,2304]{2,1,0:T(8,128)(2,1)} async-done(((bf16[4,128,2304]{2,1,0:T(8,128)(2,1)}), bf16[1,128,2304]{2,1,0:T(8,128)(2,1)}) %reduce-scatter.12.cloned.1.call-update) | async-done | bytes 589840 | tf_op jit(solution)/shard_map/reduce_scatter | solution.py:65
  371.4 2.3 multiply_convert_fusion.2
  375.6 22.3 %all-gather.27.cloned.1.call-done = bf16[4,128,2304]{2,1,0:T(8,128)(2,1)} async-done(((bf16[1,128,2304]{2,1,0:T(8,128)(2,1)}), bf16[4,128,2304]{2,1,0:T(8,128)(2,1)}) %all-gather.27.cloned.1.call-update) | async-done | bytes 2359312 | tf_op jit(solution)/shard_map/all_gather | solution.py:61
  397.9 154.8 %all-gather.29.cloned.1.call-done = bf16[2304,2304]{0,1:T(8,128)(2,1)} async-done(((bf16[2304,288]{0,1:T(8,128)(2,1)}), bf16[2304,2304]{0,1:T(8,128)(2,1)}) %all-gather.29.cloned.1.call-update) | async-done | bytes 10616848 | tf_op jit(solution)/shard_map/all_gather | solution.py:112
  552.6 11.7 fusion.29
  564.4 141.3 %all-gather.31.cloned.1.call-done = bf16[2304,2304]{0,1:T(8,128)(2,1)} async-done(((bf16[2304,288]{0,1:T(8,128)(2,1)}), bf16[2304,2304]{0,1:T(8,128)(2,1)}) %all-gather.31.cloned.1.call-update) | async-done | bytes 10616848 | tf_op jit(solution)/shard_map/all_gather | solution.py:113
  705.7 12.9 multiply_convert_fusion.1
  718.6 140.1 %all-gather.33.cloned.1.call-done = bf16[2304,2304]{1,0:T(8,128)(2,1)} async-done(((bf16[288,2304]{1,0:T(8,128)(2,1)}), bf16[2304,2304]{1,0:T(8,128)(2,1)}) %all-gather.33.cloned.1.call-update) | async-done | bytes 10616848 | tf_op jit(solution)/shard_map/all_gather | solution.py:114
  858.7 11.2 fusion.47
  870.0 31.4 %reduce-scatter.14.cloned.1.call-done = bf16[1,128,2304]{2,1,0:T(8,128)(2,1)} async-done(((bf16[4,128,2304]{2,1,0:T(8,128)(2,1)}), bf16[1,128,2304]{2,1,0:T(8,128)(2,1)}) %reduce-scatter.14.cloned.1.call-update) | async-done | bytes 589840 | tf_op jit(solution)/shard_map/reduce_scatter | solution.py:65
  902.6 2.3 fusion.108
  905.0 2.2 fusion.110
  907.4 24.0 %all-gather.35.cloned.1.call-done = bf16[4,128,2304]{2,1,0:T(8,128)(2,1)} async-done(((bf16[1,128,2304]{2,1,0:T(8,128)(2,1)}), bf16[4,128,2304]{2,1,0:T(8,128)(2,1)}) %all-gather.35.cloned.1.call-update) | async-done | bytes 2359312 | tf_op jit(solution)/shard_map/all_gather | solution.py:71
  931.4 14.4 fusion.40
  945.8 9.8 fusion.23
  955.6 11.0 fusion.44
  966.7 33.2 %reduce-scatter.16.cloned.1.call-done = bf16[1,128,2304]{2,1,0:T(8,128)(2,1)} async-done(((bf16[4,128,2304]{2,1,0:T(8,128)(2,1)}), bf16[1,128,2304]{2,1,0:T(8,128)(2,1)}) %reduce-scatter.16.cloned.1.call-update) | async-done | bytes 589840 | tf_op jit(solution)/shard_map/reduce_scatter | solution.py:75
  1001.5 2.7 fusion.94
  1010.6 19.9 all-gather.37.cloned.1.call-done
  1030.4 4.6 fusion.91
  1040.4 248.8 %while.20 = (s32[]{:T(128)}, f32[4,1,2,128,256]{4,3,2,0,1:T(8,128)}, f32[4,4,128,1,256]{4,2,1,3,0:T(8,128)S(1)}, s32[]{:T(128)}, s32[8,2]{1,0:T(8,128)}, /*index...) while((s32[]{:T(128)}, ...), condition=%wide.wide.region_17.18_spmd.clone, body=%wide.wide.region_15.17_spmd.clone.sunk | while | flops 340289152 | bytes 39946652 | solution.py:255
  1050.2 24.2 %collective-permute-done = bf16[4,4,128,1,256]{4,2,1,3,0:T(8,128)(2,1)S(1)} collective-permute-done((bf16[4,4,128,1,256]{4,2,1,3,0:T(8,128)(2,1)S(1)}, bf16[4,4,128,1,256]{4,2,1,3,0:T(8,128)(2,1)S(1)}, u32[]{:S(2)}, u32[]{:S(2)}) %collective-permute-start) | collective-permute-done | bytes 1048608 | tf_op jit(solution)/shard_map/while/body/eval_jaxpr/ppermute | solution.py:20
  1084.0 23.8 %collective-permute-done = bf16[4,4,128,1,256]{4,2,1,3,0:T(8,128)(2,1)S(1)} collective-permute-done((bf16[4,4,128,1,256]{4,2,1,3,0:T(8,128)(2,1)S(1)}, bf16[4,4,128,1,256]{4,2,1,3,0:T(8,128)(2,1)S(1)}, u32[]{:S(2)}, u32[]{:S(2)}) %collective-permute-start) | collective-permute-done | bytes 1048608 | tf_op jit(solution)/shard_map/while/body/eval_jaxpr/ppermute | solution.py:20
  1117.4 22.8 %collective-permute-done = bf16[4,4,128,1,256]{4,2,1,3,0:T(8,128)(2,1)S(1)} collective-permute-done((bf16[4,4,128,1,256]{4,2,1,3,0:T(8,128)(2,1)S(1)}, bf16[4,4,128,1,256]{4,2,1,3,0:T(8,128)(2,1)S(1)}, u32[]{:S(2)}, u32[]{:S(2)}) %collective-permute-start) | collective-permute-done | bytes 1048608 | tf_op jit(solution)/shard_map/while/body/eval_jaxpr/ppermute | solution.py:20
  1149.9 21.9 %collective-permute-done = bf16[4,4,128,1,256]{4,2,1,3,0:T(8,128)(2,1)S(1)} collective-permute-done((bf16[4,4,128,1,256]{4,2,1,3,0:T(8,128)(2,1)S(1)}, bf16[4,4,128,1,256]{4,2,1,3,0:T(8,128)(2,1)S(1)}, u32[]{:S(2)}, u32[]{:S(2)}) %collective-permute-start) | collective-permute-done | bytes 1048608 | tf_op jit(solution)/shard_map/while/body/eval_jaxpr/ppermute | solution.py:20
  1181.5 21.0 collective-permute-done
  1212.2 20.1 collective-permute-done
  1241.9 19.1 collective-permute-done
  1270.7 18.2 collective-permute-done
  1289.3 3.6 fusion.50
  1293.0 3.6 fusion.51
  1297.3 2.3 fusion.119
  1304.4 4.3 fusion.41
  1310.4 2.7 fusion.42
  1314.8 9.6 bitcast_convert_fusion
  1326.1 9.7 bitcast_convert_fusion.2
  1335.9 9.7 bitcast_convert_fusion.1
  1345.7 7.9 reduce-scatter.22.cloned.1.call-done
  1355.2 65.0 %reduce-scatter.24.cloned.1.call-done = bf16[2304,32]{0,1:T(8,128)(2,1)} async-done(((bf16[2304,256]{0,1:T(8,128)(2,1)}), bf16[2304,32]{0,1:T(8,128)(2,1)}) %reduce-scatter.24.cloned.1.call-update) | async-done | bytes 147472 | tf_op jit(solution)/shard_map/reduce_scatter | solution.py:287
  1421.8 33.7 %reduce-scatter.18.cloned.1.call-done = bf16[1,128,2304]{2,1,0:T(8,128)(2,1)} async-done(((bf16[4,128,2304]{2,1,0:T(8,128)(2,1)}), bf16[1,128,2304]{2,1,0:T(8,128)(2,1)}) %reduce-scatter.18.cloned.1.call-update) | async-done | bytes 589840 | tf_op jit(solution)/shard_map/reduce_scatter | solution.py:75
  1455.5 2.4 fusion.98
  1457.9 41.8 %all-reduce.8 = (f32[2304]{0:T(1024)}, f32[2304]{0:T(1024)}, f32[2304]{0:T(1024)}, f32[2304]{0:T(1024)}) all-reduce(f32[2304]{0:T(1024)} %get-tuple-element.377, f32[2304]{0:T(1024)} %get-tuple-element.372, f32[2304]{0:T(1024)} %get-tuple-element.374, ...), channel_id=14, replica_groups=mesh['ctx'=8,'fsdp'=4] {'ctx','fsdp'}, use_global_device_ids=true, to_apply=%region_28.29.clone | all-reduce | flops 9216 | bytes 73728
  1504.8 23.5 %reduce-scatter.26.cloned.1.call-done = bf16[64,2304]{1,0:T(8,128)(2,1)} async-done(((bf16[512,2304]{1,0:T(8,128)(2,1)}), bf16[64,2304]{1,0:T(8,128)(2,1)}) %reduce-scatter.26.cloned.1.call-update) | async-done | bytes 294928 | tf_op jit(solution)/shard_map/reduce_scatter | solution.py:290
  1530.2 70.2 %reduce-scatter.20.cloned.1.call-done = bf16[2304,64]{0,1:T(8,128)(2,1)} async-done(((bf16[2304,512]{0,1:T(8,128)(2,1)}), bf16[2304,64]{0,1:T(8,128)(2,1)}) %reduce-scatter.20.cloned.1.call-update) | async-done | bytes 294928 | tf_op jit(solution)/shard_map/reduce_scatter | solution.py:281
  1603.0 3.1 fusion.112
  1606.0 177.0 %reduce-scatter.32.cloned.1.call-done = bf16[288,2304]{1,0:T(8,128)(2,1)} async-done(((bf16[2304,2304]{1,0:T(8,128)(2,1)}), bf16[288,2304]{1,0:T(8,128)(2,1)}) %reduce-scatter.32.cloned.1.call-update) | async-done | bytes 1327120 | tf_op jit(solution)/shard_map/reduce_scatter | solution.py:299
  1783.1 3.0 convert_element_type.338
  1786.1 179.9 %reduce-scatter.28.cloned.1.call-done = bf16[2304,288]{0,1:T(8,128)(2,1)} async-done(((bf16[2304,2304]{0,1:T(8,128)(2,1)}), bf16[2304,288]{0,1:T(8,128)(2,1)}) %reduce-scatter.28.cloned.1.call-update) | async-done | bytes 1327120 | tf_op jit(solution)/shard_map/reduce_scatter | solution.py:293
  1966.0 3.0 convert_element_type.334
  1969.0 179.4 %reduce-scatter.30.cloned.1.call-done = bf16[2304,288]{0,1:T(8,128)(2,1)} async-done(((bf16[2304,2304]{0,1:T(8,128)(2,1)}), bf16[2304,288]{0,1:T(8,128)(2,1)}) %reduce-scatter.30.cloned.1.call-update) | async-done | bytes 1327120 | tf_op jit(solution)/shard_map/reduce_scatter | solution.py:296
  2148.4 3.0 convert_element_type.336
  (467 shorter events, 137.0 us)
Async XLA Ops:
  7.2 52.6 %copy-start.46 = (s32[8,2]{0,1:T(2,128)S(1)}, s32[8,2]{0,1:T(2,128)}, u32[]{:S(2)}) copy-start(s32[8,2]{0,1:T(2,128)} %param.17) | copy-start | bytes 196
  7.2 53.2 %all-gather.19.cloned.1.call-start = ((), (), s32[]{:S(2)}) async-start(), calls=%async_computation.13 | async-start | bytes 1327104 | tf_op jit(solution)/shard_map/all_gather | solution.py:109
  7.9 74.5 %all-gather.15.cloned.1.call-start = ((), (), s32[]{:S(2)}) async-start(), calls=%async_computation.11 | async-start | bytes 2949120 | tf_op jit(solution)/shard_map/all_gather | solution.py:61
  58.4 67.4 %all-gather.23.cloned.1.call-start = ((), (), s32[]{:S(2)}) async-start(), calls=%async_computation.15 | async-start | bytes 1327104 | tf_op jit(solution)/shard_map/all_gather | solution.py:110
  59.1 119.5 %all-gather.17.cloned.1.call-start = ((), (), s32[]{:S(2)}) async-start(), calls=%async_computation.12 | async-start | bytes 2654208 | tf_op jit(solution)/shard_map/all_gather | solution.py:108
  59.7 169.4 %all-gather.21.cloned.1.call-start = ((), (), s32[]{:S(2)}) async-start(), calls=%async_computation.14 | async-start | bytes 2359296 | tf_op jit(solution)/shard_map/all_gather | solution.py:147
  59.8 946.6 %copy-start.30 = (s32[8,2]{1,0:T(8,128)}, s32[8,2]{1,0:T(8,128)S(1)}, u32[]{:S(2)}) copy-start(s32[8,2]{1,0:T(8,128)S(1)} %copy.76) | copy-start | bytes 196
  60.1 69.6 %copy-start.31 = (s32[128]{0:T(128)}, s32[128]{0:T(128)S(1)}, u32[]{:S(2)}) copy-start(s32[128]{0:T(128)S(1)} %get-tuple-element.544) | copy-start | bytes 1540
  82.5 43.3 %copy-start.14 = (bf16[4,128,2304]{2,1,0:T(8,128)(2,1)S(1)}, bf16[4,128,2304]{2,1,0:T(8,128)(2,1)}, u32[]{:S(2)}) copy-start(bf16[4,128,2304]{2,1,0:T(8,128)(2,1)} %all-gather.15.cloned.1.call-done) | copy-start | bytes 7077892
  86.2 193.3 %all-gather.39.cloned.1.call-start = ((), (), s32[]{:S(2)}) async-start(), calls=%async_computation.34 | async-start | bytes 2359296 | tf_op jit(solution)/shard_map/all_gather | solution.py:148
  128.7 203.6 %all-gather.25.cloned.1.call-start = ((), (), s32[]{:S(2)}) async-start(), calls=%async_computation.16 | async-start | bytes 2654208 | tf_op jit(solution)/shard_map/all_gather | solution.py:111
  129.5 239.1 %reduce-scatter.12.cloned.1.call-start = ((), (), s32[]{:S(2)}) async-start(), calls=%async_computation.17 | async-start | bytes 2949120 | tf_op jit(solution)/shard_map/reduce_scatter | solution.py:65
  129.8 102.3 %copy-start.26 = (pred[128,1024]{1,0:T(8,128)(4,1)}, pred[128,1024]{1,0:T(8,128)(4,1)S(1)}, u32[]{:S(2)}) copy-start(pred[128,1024]{1,0:T(8,128)(4,1)S(1)} %broadcast_compare_fusion.1) | copy-start | bytes 393220
  185.1 46.9 %copy-start.19 = (f32[4,128,1,2,128]{4,1,3,0,2:T(8,128)}, f32[4,128,1,2,128]{4,1,3,0,2:T(8,128)S(1)}, u32[]{:S(2)}) copy-start(f32[4,128,1,2,128]{4,1,3,0,2:T(8,128)S(1)} %get-tuple-element.415) | copy-start | bytes 1572868
  185.1 46.9 %copy-start.20 = (f32[4,128,1,2,128]{4,1,3,0,2:T(8,128)}, f32[4,128,1,2,128]{4,1,3,0,2:T(8,128)S(1)}, u32[]{:S(2)}) copy-start(f32[4,128,1,2,128]{4,1,3,0,2:T(8,128)S(1)} %get-tuple-element.416) | copy-start | bytes 1572868
  235.6 47.8 %copy-start.38 = (f32[4,2,128]{2,1,0:T(2,128)}, f32[4,2,128]{2,1,0:T(2,128)S(1)}, u32[]{:S(2)}) copy-start(f32[4,2,128]{2,1,0:T(2,128)S(1)} %fusion.52) | copy-start | bytes 12292
  283.7 48.5 %copy-start.21 = (bf16[4,128,1,2,256]{1,4,3,0,2:T(8,128)(2,1)}, bf16[4,128,1,2,256]{1,4,3,0,2:T(8,128)(2,1)S(1)}, u32[]{:S(2)}) copy-start(bf16[4,128,1,2,256]{1,4,3,0,2:T(8,128)(2,1)S(1)} %copy.79) | copy-start | bytes 1572868
  336.8 33.1 %copy-start.2 = (bf16[1,128,2304]{2,1,0:T(8,128)(2,1)S(1)}, bf16[1,128,2304]{2,1,0:T(8,128)(2,1)}, u32[]{:S(2)}) copy-start(bf16[1,128,2304]{2,1,0:T(8,128)(2,1)} %param.16) | copy-start | bytes 1769476
  336.8 34.6 %copy-start.27 = (f32[2304]{0:T(1024)S(1)}, f32[2304]{0:T(1024)}, u32[]{:S(2)}) copy-start(f32[2304]{0:T(1024)} %get-tuple-element.404) | copy-start | bytes 27652
  336.8 61.1 %all-gather.27.cloned.1.call-start = ((), (), s32[]{:S(2)}) async-start(), calls=%async_computation.18 | async-start | bytes 2949120 | tf_op jit(solution)/shard_map/all_gather | solution.py:61
  369.8 634.5 %copy-start.34 = (f32[128]{0:T(128)}, f32[128]{0:T(128)S(1)}, u32[]{:S(2)}) copy-start(f32[128]{0:T(128)S(1)} %fusion.148) | copy-start | bytes 1540
  371.3 633.0 %copy-start.40 = (f32[128]{0:T(128)}, f32[128]{0:T(128)S(1)}, u32[]{:S(2)}) copy-start(f32[128]{0:T(128)S(1)} %fusion.149) | copy-start | bytes 1540
  373.7 179.0 %all-gather.29.cloned.1.call-start = ((), (), s32[]{:S(2)}) async-start(), calls=%async_computation.19 | async-start | bytes 11943936 | tf_op jit(solution)/shard_map/all_gather | solution.py:112
  374.2 331.5 %all-gather.31.cloned.1.call-start = ((), (), s32[]{:S(2)}) async-start(), calls=%async_computation.20 | async-start | bytes 11943936 | tf_op jit(solution)/shard_map/all_gather | solution.py:113
  375.0 483.7 %all-gather.33.cloned.1.call-start = ((), (), s32[]{:S(2)}) async-start(), calls=%async_computation.21 | async-start | bytes 11943936 | tf_op jit(solution)/shard_map/all_gather | solution.py:114
  375.6 525.8 %reduce-scatter.14.cloned.1.call-start = ((), (), s32[]{:S(2)}) async-start(), calls=%async_computation.22 | async-start | bytes 2949120 | tf_op jit(solution)/shard_map/reduce_scatter | solution.py:65
  869.9 32.7 %copy-start.9 = (bf16[1,128,2304]{2,1,0:T(8,128)(2,1)S(1)}, bf16[1,128,2304]{2,1,0:T(8,128)(2,1)}, u32[]{:S(2)}) copy-start(bf16[1,128,2304]{2,1,0:T(8,128)(2,1)} %param.29) | copy-start | bytes 1769476
  869.9 32.7 %copy-start.29 = (f32[2304]{0:T(1024)S(1)}, f32[2304]{0:T(1024)}, u32[]{:S(2)}) copy-start(f32[2304]{0:T(1024)} %get-tuple-element.406) | copy-start | bytes 27652
  869.9 61.5 %all-gather.35.cloned.1.call-start = ((), (), s32[]{:S(2)}) async-start(), calls=%async_computation.23 | async-start | bytes 2949120 | tf_op jit(solution)/shard_map/all_gather | solution.py:71
  902.6 43.2 %copy-start.42 = (f32[128]{0:T(128)}, f32[128]{0:T(128)S(1)}, u32[]{:S(2)}) copy-start(f32[128]{0:T(128)S(1)} %fusion.150) | copy-start | bytes 1540
  907.2 92.7 %reduce-scatter.16.cloned.1.call-start = ((), (), s32[]{:S(2)}) async-start(), calls=%async_computation.24 | async-start | bytes 2949120 | tf_op jit(solution)/shard_map/reduce_scatter | solution.py:75
  966.7 33.2 %copy-start.7 = (bf16[1,128,2304]{2,1,0:T(8,128)(2,1)S(1)}, bf16[1,128,2304]{2,1,0:T(8,128)(2,1)}, u32[]{:S(2)}) copy-start(bf16[1,128,2304]{2,1,0:T(8,128)(2,1)} %reduce-scatter.12.cloned.1.call-done) | copy-start | bytes 1769476
  966.7 63.7 %all-gather.37.cloned.1.call-start = ((), (), s32[]{:S(2)}) async-start(), calls=%async_computation.25 | async-start | bytes 2949120 | tf_op jit(solution)/shard_map/all_gather | solution.py:71
  1006.2 347.3 %reduce-scatter.22.cloned.1.call-start = ((), (), s32[]{:S(2)}) async-start(), calls=%async_computation.28 | async-start | bytes 1327104 | tf_op jit(solution)/shard_map/reduce_scatter | solution.py:284
  1046.3 28.1 %collective-permute-start = (bf16[4,4,128,1,256]{4,2,1,3,0:T(8,128)(2,1)S(1)}, bf16[4,4,128,1,256]{4,2,1,3,0:T(8,128)(2,1)S(1)}, u32[]{:S(2)}, u32[]{:S(2)}) collective-permute-start(bf16[4,4,128,1,256]{4,2,1,3,0:T(8,128)(2,1)S(1)} %pad_maximum_fusion.8), channel_id=1, source_target_pairs={{28,0},{0,4},{4,8},{8,12},{12,16},{16,20},{20,24},{24,28},{29,1},{... | collective-permute-start | bytes 3145736 | tf_op jit(solution)/shard_map/while/body/eval_jaxpr/ppermute | solution.py:20
  1050.2 24.4 %copy-start.33 = (s32[128]{0:T(128)S(1)}, s32[128]{0:T(128)}, u32[]{:S(2)}) copy-start(s32[128]{0:T(128)} %get-tuple-element.693) | copy-start | bytes 1540 | tf_op jit(solution)/shard_map/while
  1050.2 24.4 %copy-start.45 = (f32[4,1,2,128]{3,2,0,1:T(2,128)S(1)}, f32[4,1,2,128]{3,2,0,1:T(2,128)}, u32[]{:S(2)}) copy-start(f32[4,1,2,128]{3,2,0,1:T(2,128)} %copy-done.44) | copy-start | bytes 12292 | tf_op jit(solution)/shard_map/while
  1050.2 24.4 %copy-start.48 = (s32[16]{0:T(128)S(1)}, s32[16]{0:T(128)}, u32[]{:S(2)}) copy-start(s32[16]{0:T(128)} %get-tuple-element.711) | copy-start | bytes 196 | tf_op jit(solution)/shard_map/while
  1080.6 27.2 %collective-permute-start = (bf16[4,4,128,1,256]{4,2,1,3,0:T(8,128)(2,1)S(1)}, bf16[4,4,128,1,256]{4,2,1,3,0:T(8,128)(2,1)S(1)}, u32[]{:S(2)}, u32[]{:S(2)}) collective-permute-start(bf16[4,4,128,1,256]{4,2,1,3,0:T(8,128)(2,1)S(1)} %pad_maximum_fusion.8), channel_id=1, source_target_pairs={{28,0},{0,4},{4,8},{8,12},{12,16},{16,20},{20,24},{24,28},{29,1},{... | collective-permute-start | bytes 3145736 | tf_op jit(solution)/shard_map/while/body/eval_jaxpr/ppermute | solution.py:20
  1084.0 24.0 %copy-start.33 = (s32[128]{0:T(128)S(1)}, s32[128]{0:T(128)}, u32[]{:S(2)}) copy-start(s32[128]{0:T(128)} %get-tuple-element.693) | copy-start | bytes 1540 | tf_op jit(solution)/shard_map/while
  1084.0 24.0 %copy-start.45 = (f32[4,1,2,128]{3,2,0,1:T(2,128)S(1)}, f32[4,1,2,128]{3,2,0,1:T(2,128)}, u32[]{:S(2)}) copy-start(f32[4,1,2,128]{3,2,0,1:T(2,128)} %copy-done.44) | copy-start | bytes 12292 | tf_op jit(solution)/shard_map/while
  1084.0 24.0 %copy-start.48 = (s32[16]{0:T(128)S(1)}, s32[16]{0:T(128)}, u32[]{:S(2)}) copy-start(s32[16]{0:T(128)} %get-tuple-element.711) | copy-start | bytes 196 | tf_op jit(solution)/shard_map/while
  1114.0 26.3 %collective-permute-start = (bf16[4,4,128,1,256]{4,2,1,3,0:T(8,128)(2,1)S(1)}, bf16[4,4,128,1,256]{4,2,1,3,0:T(8,128)(2,1)S(1)}, u32[]{:S(2)}, u32[]{:S(2)}) collective-permute-start(bf16[4,4,128,1,256]{4,2,1,3,0:T(8,128)(2,1)S(1)} %pad_maximum_fusion.8), channel_id=1, source_target_pairs={{28,0},{0,4},{4,8},{8,12},{12,16},{16,20},{20,24},{24,28},{29,1},{... | collective-permute-start | bytes 3145736 | tf_op jit(solution)/shard_map/while/body/eval_jaxpr/ppermute | solution.py:20
  1117.4 23.1 %copy-start.45 = (f32[4,1,2,128]{3,2,0,1:T(2,128)S(1)}, f32[4,1,2,128]{3,2,0,1:T(2,128)}, u32[]{:S(2)}) copy-start(f32[4,1,2,128]{3,2,0,1:T(2,128)} %copy-done.44) | copy-start | bytes 12292 | tf_op jit(solution)/shard_map/while
  1117.4 23.1 %copy-start.48 = (s32[16]{0:T(128)S(1)}, s32[16]{0:T(128)}, u32[]{:S(2)}) copy-start(s32[16]{0:T(128)} %get-tuple-element.711) | copy-start | bytes 196 | tf_op jit(solution)/shard_map/while
  1146.5 25.4 %collective-permute-start = (bf16[4,4,128,1,256]{4,2,1,3,0:T(8,128)(2,1)S(1)}, bf16[4,4,128,1,256]{4,2,1,3,0:T(8,128)(2,1)S(1)}, u32[]{:S(2)}, u32[]{:S(2)}) collective-permute-start(bf16[4,4,128,1,256]{4,2,1,3,0:T(8,128)(2,1)S(1)} %pad_maximum_fusion.8), channel_id=1, source_target_pairs={{28,0},{0,4},{4,8},{8,12},{12,16},{16,20},{20,24},{24,28},{29,1},{... | collective-permute-start | bytes 3145736 | tf_op jit(solution)/shard_map/while/body/eval_jaxpr/ppermute | solution.py:20
  1178.0 24.5 %collective-permute-start = (bf16[4,4,128,1,256]{4,2,1,3,0:T(8,128)(2,1)S(1)}, bf16[4,4,128,1,256]{4,2,1,3,0:T(8,128)(2,1)S(1)}, u32[]{:S(2)}, u32[]{:S(2)}) collective-permute-start(bf16[4,4,128,1,256]{4,2,1,3,0:T(8,128)(2,1)S(1)} %pad_maximum_fusion.8), channel_id=1, source_target_pairs={{28,0},{0,4},{4,8},{8,12},{12,16},{16,20},{20,24},{24,28},{29,1},{... | collective-permute-start | bytes 3145736 | tf_op jit(solution)/shard_map/while/body/eval_jaxpr/ppermute | solution.py:20
  1208.7 23.5 %collective-permute-start = (bf16[4,4,128,1,256]{4,2,1,3,0:T(8,128)(2,1)S(1)}, bf16[4,4,128,1,256]{4,2,1,3,0:T(8,128)(2,1)S(1)}, u32[]{:S(2)}, u32[]{:S(2)}) collective-permute-start(bf16[4,4,128,1,256]{4,2,1,3,0:T(8,128)(2,1)S(1)} %pad_maximum_fusion.8), channel_id=1, source_target_pairs={{28,0},{0,4},{4,8},{8,12},{12,16},{16,20},{20,24},{24,28},{29,1},{... | collective-permute-start | bytes 3145736 | tf_op jit(solution)/shard_map/while/body/eval_jaxpr/ppermute | solution.py:20
  1238.4 22.6 %collective-permute-start = (bf16[4,4,128,1,256]{4,2,1,3,0:T(8,128)(2,1)S(1)}, bf16[4,4,128,1,256]{4,2,1,3,0:T(8,128)(2,1)S(1)}, u32[]{:S(2)}, u32[]{:S(2)}) collective-permute-start(bf16[4,4,128,1,256]{4,2,1,3,0:T(8,128)(2,1)S(1)} %pad_maximum_fusion.8), channel_id=1, source_target_pairs={{28,0},{0,4},{4,8},{8,12},{12,16},{16,20},{20,24},{24,28},{29,1},{... | collective-permute-start | bytes 3145736 | tf_op jit(solution)/shard_map/while/body/eval_jaxpr/ppermute | solution.py:20
  1267.2 21.7 %collective-permute-start = (bf16[4,4,128,1,256]{4,2,1,3,0:T(8,128)(2,1)S(1)}, bf16[4,4,128,1,256]{4,2,1,3,0:T(8,128)(2,1)S(1)}, u32[]{:S(2)}, u32[]{:S(2)}) collective-permute-start(bf16[4,4,128,1,256]{4,2,1,3,0:T(8,128)(2,1)S(1)} %pad_maximum_fusion.8), channel_id=1, source_target_pairs={{28,0},{0,4},{4,8},{8,12},{12,16},{16,20},{20,24},{24,28},{29,1},{... | collective-permute-start | bytes 3145736 | tf_op jit(solution)/shard_map/while/body/eval_jaxpr/ppermute | solution.py:20
  1293.0 127.2 %reduce-scatter.24.cloned.1.call-start = ((), (), s32[]{:S(2)}) async-start(), calls=%async_computation.29 | async-start | bytes 1327104 | tf_op jit(solution)/shard_map/reduce_scatter | solution.py:287
  1296.6 158.9 %reduce-scatter.18.cloned.1.call-start = ((), (), s32[]{:S(2)}) async-start(), calls=%async_computation.26 | async-start | bytes 2949120 | tf_op jit(solution)/shard_map/reduce_scatter | solution.py:75
  1303.3 225.0 %reduce-scatter.26.cloned.1.call-start = ((), (), s32[]{:S(2)}) async-start(), calls=%async_computation.30 | async-start | bytes 2654208 | tf_op jit(solution)/shard_map/reduce_scatter | solution.py:290
  1308.7 291.7 %reduce-scatter.20.cloned.1.call-start = ((), (), s32[]{:S(2)}) async-start(), calls=%async_computation.27 | async-start | bytes 2654208 | tf_op jit(solution)/shard_map/reduce_scatter | solution.py:281
  1313.1 470.0 %reduce-scatter.32.cloned.1.call-start = ((), (), s32[]{:S(2)}) async-start(), calls=%async_computation.33 | async-start | bytes 11943936 | tf_op jit(solution)/shard_map/reduce_scatter | solution.py:299
  1324.4 641.6 %reduce-scatter.28.cloned.1.call-start = ((), (), s32[]{:S(2)}) async-start(), calls=%async_computation.31 | async-start | bytes 11943936 | tf_op jit(solution)/shard_map/reduce_scatter | solution.py:293
  1335.8 812.6 %reduce-scatter.30.cloned.1.call-start = ((), (), s32[]{:S(2)}) async-start(), calls=%async_computation.32 | async-start | bytes 11943936 | tf_op jit(solution)/shard_map/reduce_scatter | solution.py:296
  1345.6 109.9 %copy-start.3 = (bf16[1,128,2304]{2,1,0:T(8,128)(2,1)S(1)}, bf16[1,128,2304]{2,1,0:T(8,128)(2,1)}, u32[]{:S(2)}) copy-start(bf16[1,128,2304]{2,1,0:T(8,128)(2,1)} %param.16) | copy-start | bytes 1769476
  1345.6 257.3 %copy-start.8 = (bf16[1,128,2304]{2,1,0:T(8,128)(2,1)S(1)}, bf16[1,128,2304]{2,1,0:T(8,128)(2,1)}, u32[]{:S(2)}) copy-start(bf16[1,128,2304]{2,1,0:T(8,128)(2,1)} %reduce-scatter.12.cloned.1.call-done) | copy-start | bytes 1769476
  1345.6 257.3 %copy-start.10 = (bf16[1,128,2304]{2,1,0:T(8,128)(2,1)S(1)}, bf16[1,128,2304]{2,1,0:T(8,128)(2,1)}, u32[]{:S(2)}) copy-start(bf16[1,128,2304]{2,1,0:T(8,128)(2,1)} %param.29) | copy-start | bytes 1769476
  1345.7 257.3 %copy-start.11 = (bf16[1,128,2304]{2,1,0:T(8,128)(2,1)S(1)}, bf16[1,128,2304]{2,1,0:T(8,128)(2,1)}, u32[]{:S(2)}) copy-start(bf16[1,128,2304]{2,1,0:T(8,128)(2,1)} %reduce-scatter.14.cloned.1.call-done) | copy-start | bytes 1769476
  1345.7 257.3 %copy-start.13 = (bf16[1,128,2304]{2,1,0:T(8,128)(2,1)S(1)}, bf16[1,128,2304]{2,1,0:T(8,128)(2,1)}, u32[]{:S(2)}) copy-start(bf16[1,128,2304]{2,1,0:T(8,128)(2,1)} %reduce-scatter.16.cloned.1.call-done) | copy-start | bytes 1769476
  1345.7 257.3 %copy-start.35 = (f32[128]{0:T(128)S(1)}, f32[128]{0:T(128)}, u32[]{:S(2)}) copy-start(f32[128]{0:T(128)} %copy-done.34) | copy-start | bytes 1540
  1455.5 147.4 %copy-start.18 = (bf16[1,128,2304]{2,1,0:T(8,128)(2,1)S(1)}, bf16[1,128,2304]{2,1,0:T(8,128)(2,1)}, u32[]{:S(2)}) copy-start(bf16[1,128,2304]{2,1,0:T(8,128)(2,1)} %reduce-scatter.18.cloned.1.call-done) | copy-start | bytes 1769476
  (86 other events, 493.3 us)
Sparse Core Ops, SparseCore 0:
  10.2 43.7 all-gather.18
  58.5 23.8 all-gather.14
  84.6 41.0 all-gather.22
  127.8 50.8 all-gather.16
  181.3 47.7 all-gather.20
  231.7 47.7 all-gather.38
  281.7 50.5 all-gather.24
  336.9 31.5 reduce-scatter.11
  373.8 24.0 all-gather.26
  400.1 152.4 all-gather.28
  555.0 150.6 all-gather.30
  708.0 150.6 all-gather.32
  870.0 31.2 reduce-scatter.13
  907.3 24.0 all-gather.34
  966.8 33.0 reduce-scatter.15
  1006.3 24.0 all-gather.36
  1293.1 60.4 reduce-scatter.21
  1357.2 62.9 reduce-scatter.23
  1423.5 31.9 reduce-scatter.17
  1458.9 69.4 reduce-scatter.25
  1532.4 67.9 reduce-scatter.19
  1604.0 179.0 reduce-scatter.31
  1787.1 178.8 reduce-scatter.27
  1969.5 178.8 reduce-scatter.29
where the time goes:
time: 2170 us; the launch traced here: 2160 us
  waiting for transfers between devices  1760 us (81%)
  matrix products  185 us (9%)
  blocking collectives  85.4 us (4%)
  other arithmetic  57.2 us (3%)
  local copies, waits for them, and re-layouts  52.3 us (2%)
    reduce_scatter x1, waiting for transfers between devices, body(): lax.psum_scatter(grad_gate_full.astype(jnp.bfloat16), 'ctx', scatter_dime...  180 us
    reduce_scatter x1, waiting for transfers between devices, body(): lax.psum_scatter(grad_up_full.astype(jnp.bfloat16), 'ctx', scatter_dimens...  179 us
    reduce_scatter x1, waiting for transfers between devices, body(): lax.psum_scatter(grad_down_full.astype(jnp.bfloat16), 'ctx', scatter_dime...  177 us
    ppermute x8, waiting for transfers between devices, passed_along(): return lax.ppermute(block, axis, route)  171 us
    all_gather x1, waiting for transfers between devices, body(): lax.all_gather(weight_gate, 'ctx', axis=1, tiled=True)  155 us
    all_gather x1, waiting for transfers between devices, body(): lax.all_gather(weight_up, 'ctx', axis=1, tiled=True)  141 us
    all_gather x1, waiting for transfers between devices, body(): lax.all_gather(weight_down, 'ctx', axis=0, tiled=True)  140 us
    unnamed x2, blocking collectives  85.4 us
  transfers between devices with their start and end apart: 32, of which 31 were waited for; matrix products, arithmetic and copies ran while one was open for 6% of the time, Pallas kernels for 0%

commit v1 on v0

v1 whole, which is shorter than its diff:
```python
import math

import jax
import jax.numpy as jnp
from jax import lax
from jax.sharding import PartitionSpec as P

HEAD_DIM = 256
EPS = 1e-06
CAP = 50.0
NEGATIVE = -1e30
BF16 = jnp.bfloat16
F32 = jnp.float32


def ring_order(size):
    return list(range(0, size, 2)) + list(range(size - 1, 0, -2))


def ring_hop(block, step):
    order = ring_order(lax.axis_size("ctx"))
    size = len(order)
    return lax.ppermute(block, "ctx", [(order[i], order[(i + step) % size]) for i in range(size)])


def ring_member(offset):
    size = lax.axis_size("ctx")
    own = lax.axis_index("ctx")
    place = jnp.where(own % 2 == 0, own // 2, size - 1 - own // 2)
    place = (place + offset) % size
    return jnp.where(place < size // 2, 2 * place, 2 * (size - 1 - place) + 1)


def ring_offsets():
    half = lax.axis_size("ctx") // 2
    offsets = [0]
    for k in range(1, half):
        offsets += [-k, k]
    return offsets + [half]


def ring_gather(own):
    half = lax.axis_size("ctx") // 2
    blocks = [own]
    behind = ahead = own
    for _ in range(1, half):
        behind, ahead = ring_hop(behind, 1), ring_hop(ahead, -1)
        blocks += [behind, ahead]
    middle = own.shape[0] // 2
    far = [ring_hop(behind[:middle], 1), ring_hop(ahead[middle:], -1)]
    return blocks + [jnp.concatenate(far, axis=0)]


def ring_scatter(term):
    half = lax.axis_size("ctx") // 2
    far = term(half).astype(BF16)
    middle = far.shape[0] // 2
    behind, ahead = ring_hop(far[:middle], 1), ring_hop(far[middle:], -1)
    first = True
    for k in range(half - 1, -1, -1):
        if k == 0:
            return term(0) + (behind.astype(F32) + ahead.astype(F32))
        to_ahead, to_behind = term(k), term(-k)
        if first:
            zeros = jnp.zeros_like(behind)
            behind = jnp.concatenate([behind, zeros], axis=0)
            ahead = jnp.concatenate([zeros, ahead], axis=0)
            first = False
        behind = ring_hop((to_ahead + behind.astype(F32)).astype(BF16), 1)
        ahead = ring_hop((to_behind + ahead.astype(F32)).astype(BF16), -1)


def cube_hop(block, mask):
    size = lax.axis_size("fsdp")
    return lax.ppermute(block, "fsdp", [(i, i ^ mask) for i in range(size)])


def cube_gather(own):
    blocks = [own]
    mask = lax.axis_size("fsdp") // 2
    while mask:
        blocks += [cube_hop(block, mask) for block in blocks]
        mask //= 2
    return blocks


def cube_scatter(terms):
    mask = 1
    while len(terms) > 1:
        half = len(terms) // 2
        kept = terms[:half]
        moved = [cube_hop(term.astype(BF16), mask) for term in terms[half:]]
        terms = [a + b.astype(F32) for a, b in zip(kept, moved)]
        mask *= 2
    return terms[0]


def sum_over_all(block):
    for axis in ("fsdp", "ctx"):
        mask = 1
        size = lax.axis_size(axis)
        while mask < size:
            block = block + lax.ppermute(block, axis, [(i, i ^ mask) for i in range(size)])
            mask *= 2
    return block


def rms_norm(values, gain):
    return values * lax.rsqrt(jnp.mean(values * values, axis=-1, keepdims=True) + EPS) * gain


def norm_back(values, gain, cotangent):
    _, pullback = jax.vjp(rms_norm, values, gain)
    return pullback(cotangent)


def rotate(values, cosine, sine):
    middle = values.shape[-1] // 2
    first = values[..., :middle]
    second = values[..., middle:]
    return jnp.concatenate(
        [first * cosine - second * sine, second * cosine + first * sine], axis=-1
    )


def dot(a, b, dims):
    return lax.dot_general(a, b, (dims, ((), ())), preferred_element_type=F32)


def nn(a, b):
    return dot(a, b, ((1,), (0,)))


def nt(a, b):
    return dot(a, b, ((1,), (1,)))


def tn(a, b):
    return dot(a, b, ((0,), (0,)))


def gelu_parts(gate):
    slope = math.sqrt(2.0 / math.pi)
    square = gate * gate
    tanh = jnp.tanh(slope * gate * (1.0 + 0.044715 * square))
    value = 0.5 * gate * (1.0 + tanh)
    inner = slope * (1.0 + 3.0 * 0.044715 * square)
    return value, 0.5 * (1.0 + tanh) + 0.5 * gate * (1.0 - tanh * tanh) * inner


def put_blocks(blocks, places):
    size = blocks[0].shape[0]
    whole = jnp.zeros((size * len(blocks),) + blocks[0].shape[1:], blocks[0].dtype)
    for block, at in zip(blocks, places):
        whole = lax.dynamic_update_slice_in_dim(whole, block, at * size, axis=0)
    return whole


def body(
    block_in,
    stretch_order,
    weight_query,
    weight_key,
    weight_value,
    weight_output,
    weight_gate,
    weight_up,
    weight_down,
    gain_preattn,
    gain_postattn,
    gain_premlp,
    gain_postmlp,
    grad_out,
):
    n_ctx, n_fsdp = lax.axis_size("ctx"), lax.axis_size("fsdp")
    own_ctx, own_fsdp = lax.axis_index("ctx"), lax.axis_index("fsdp")
    rows_in = block_in[0].astype(F32)
    tokens, width = rows_in.shape
    half = tokens // 2
    scale = HEAD_DIM ** (-0.5)
    offsets = ring_offsets()
    members = [ring_member(k) for k in offsets]

    steps = jnp.arange(HEAD_DIM // 2, dtype=F32)
    inverse = jnp.exp(steps * (-2.0 * math.log(10000.0) / HEAD_DIM))

    def positions(member):
        starts = lax.dynamic_slice_in_dim(stretch_order, member, 1, axis=0)[0]
        return (starts[:, None] * half + jnp.arange(half, dtype=jnp.int32)[None, :]).reshape(-1)

    query_pos = positions(own_ctx)
    key_pos = jnp.concatenate([positions(member) for member in members])
    angle = query_pos.astype(F32)[:, None] * inverse[None, :]
    cosine, sine = jnp.cos(angle), jnp.sin(angle)

    gains = jnp.stack([gain_preattn, gain_postattn, gain_premlp, gain_postmlp])
    share = gains.shape[1]
    own_place = (own_ctx * n_fsdp + own_fsdp) * share
    gains = sum_over_all(
        lax.dynamic_update_slice_in_dim(jnp.zeros((4, width), F32), gains, own_place, axis=1)
    )
    gain_one, gain_two, gain_three, gain_four = gains[0], gains[1], gains[2], gains[3]

    query_cols, key_cols = weight_query.shape[1], weight_key.shape[1]
    in_blocks = ring_gather(
        jnp.concatenate([weight_query.T, weight_key.T, weight_value.T], axis=0)
    )
    query_full = put_blocks([b[:query_cols] for b in in_blocks], members)
    key_full = put_blocks([b[query_cols : query_cols + key_cols] for b in in_blocks], members)
    value_full = put_blocks([b[query_cols + key_cols :] for b in in_blocks], members)
    output_full = put_blocks(ring_gather(weight_output), members)
    gate_full = jnp.concatenate(cube_gather(weight_gate.T), axis=0)
    up_full = jnp.concatenate(cube_gather(weight_up.T), axis=0)
    down_full = jnp.concatenate(cube_gather(weight_down), axis=0)

    normed_one = jnp.concatenate(cube_gather(rms_norm(rows_in, gain_one).astype(BF16)), axis=0)
    seqs = n_fsdp
    group = query_full.shape[0] // HEAD_DIM

    def by_head(flat, heads):
        return flat.reshape(seqs, tokens, heads, HEAD_DIM).transpose(0, 2, 1, 3)

    def flatten(heads):
        return heads.transpose(0, 2, 1, 3).reshape(seqs * tokens, -1)

    queries = (rotate(by_head(nt(normed_one, query_full), group), cosine, sine) * scale).astype(BF16)
    queries = queries.reshape(seqs, group * tokens, HEAD_DIM)
    keys_own = rotate(nt(normed_one, key_full).reshape(seqs, tokens, HEAD_DIM), cosine, sine)
    values_own = nt(normed_one, value_full).reshape(seqs, tokens, HEAD_DIM)
    own = jnp.stack([keys_own, values_own], axis=1).astype(BF16)
    both = jnp.concatenate(ring_gather(own), axis=2)
    keys, values = both[:, 0], both[:, 1]
    raw = jnp.einsum("sqd,skd->sqk", queries, keys, preferred_element_type=F32)
    capped = CAP * jnp.tanh(raw / CAP)
    allowed = key_pos[None, :] <= jnp.tile(query_pos, group)[:, None]
    masked = jnp.where(allowed, capped, NEGATIVE)
    best = jnp.max(masked, axis=-1, keepdims=True)
    weights = jnp.exp(masked - best)
    total = jnp.sum(weights, axis=-1, keepdims=True)
    weighted = jnp.einsum("sqk,skd->sqd", weights.astype(BF16), values, preferred_element_type=F32)
    attn_exact = weighted / total
    mixed = flatten(attn_exact.astype(BF16).reshape(seqs, group, tokens, HEAD_DIM))

    def by_seq(flat):
        return [flat[i * tokens : (i + 1) * tokens] for i in range(seqs)]

    attn_out = cube_scatter(by_seq(nn(mixed, output_full)))
    resid = rows_in + rms_norm(attn_out, gain_two)

    normed_two = ring_gather(rms_norm(resid, gain_three).astype(BF16))
    gates = [nt(rows, gate_full) for rows in normed_two]
    ups = [nt(rows, up_full) for rows in normed_two]
    parts = [gelu_parts(gate) for gate in gates]
    hidden = [(part[0] * up).astype(BF16) for part, up in zip(parts, ups)]
    at = {offset: i for i, offset in enumerate(offsets)}
    mlp_out = ring_scatter(lambda k: nn(hidden[at[k]], down_full))
    block_out = resid + rms_norm(mlp_out, gain_four)

    cotangent = grad_out[0].astype(F32)
    d_mlp_out, grad_four = norm_back(mlp_out, gain_four, cotangent)
    d_mlp = ring_gather(d_mlp_out.astype(BF16))
    d_hidden = [nt(rows, down_full) for rows in d_mlp]
    d_gate = [(d * up * part[1]).astype(BF16) for d, up, part in zip(d_hidden, ups, parts)]
    d_up = [(d * part[0]).astype(BF16) for d, part in zip(d_hidden, parts)]
    d_normed_two = ring_scatter(
        lambda k: nn(d_gate[at[k]], gate_full) + nn(d_up[at[k]], up_full)
    )
    d_resid_mlp, grad_three = norm_back(resid, gain_three, d_normed_two)
    d_resid = cotangent + d_resid_mlp
    d_attn_out, grad_two = norm_back(attn_out, gain_two, d_resid)

    normed_two_all = jnp.concatenate(normed_two, axis=0)
    d_mlp_all = jnp.concatenate(d_mlp, axis=0)
    grad_down_full = tn(jnp.concatenate(hidden, axis=0), d_mlp_all)
    grad_gate_full = tn(jnp.concatenate(d_gate, axis=0), normed_two_all)
    grad_up_full = tn(jnp.concatenate(d_up, axis=0), normed_two_all)

    def to_owners(full):
        size = full.shape[0] // n_fsdp
        return cube_scatter([full[i * size : (i + 1) * size] for i in range(n_fsdp)])

    grad_down = to_owners(grad_down_full)
    grad_gate = to_owners(grad_gate_full).T
    grad_up = to_owners(grad_up_full).T

    d_attn = jnp.concatenate(cube_gather(d_attn_out.astype(BF16)), axis=0)
    grad_output_full = tn(mixed, d_attn)
    d_mixed = by_head(nt(d_attn, output_full).astype(BF16), group)
    d_mixed = d_mixed.reshape(seqs, group * tokens, HEAD_DIM)
    delta = jnp.sum(d_mixed.astype(F32) * attn_exact, axis=-1, keepdims=True)
    probs = weights * (1.0 / total)
    d_values = jnp.einsum("sqk,sqd->skd", probs.astype(BF16), d_mixed, preferred_element_type=F32)
    d_probs = jnp.einsum("sqd,skd->sqk", d_mixed, values, preferred_element_type=F32)
    d_scores = (probs * (d_probs - delta) * (1.0 - (capped * (1.0 / CAP)) ** 2)).astype(BF16)
    d_queries = jnp.einsum("sqk,skd->sqd", d_scores, keys, preferred_element_type=F32)
    d_keys = jnp.einsum("sqk,sqd->skd", d_scores, queries, preferred_element_type=F32)
    d_both = jnp.stack([d_keys, d_values], axis=1)

    def both_term(k):
        return lax.slice_in_dim(d_both, at[k] * tokens, (at[k] + 1) * tokens, axis=2)

    d_both_own = ring_scatter(both_term)
    d_query_raw = rotate(
        d_queries.reshape(seqs, group, tokens, HEAD_DIM) * scale, cosine, -sine
    ).astype(BF16)
    d_query_raw = flatten(d_query_raw)
    d_key_raw = rotate(d_both_own[:, 0], cosine, -sine).astype(BF16).reshape(-1, HEAD_DIM)
    d_value_raw = d_both_own[:, 1].astype(BF16).reshape(-1, HEAD_DIM)
    d_normed_one = cube_scatter(
        by_seq(
            nn(d_query_raw, query_full) + nn(d_key_raw, key_full) + nn(d_value_raw, value_full)
        )
    )
    d_rows_attn, grad_one = norm_back(rows_in, gain_one, d_normed_one)
    grad_in = d_resid + d_rows_attn

    def cut(full, k):
        size = full.shape[0] // n_ctx
        return lax.dynamic_slice_in_dim(full, members[at[k]] * size, size, axis=0)

    grad_query_full = tn(d_query_raw, normed_one)
    grad_key_full = tn(d_key_raw, normed_one)
    grad_value_full = tn(d_value_raw, normed_one)
    grad_output = ring_scatter(lambda k: cut(grad_output_full, k))
    grad_ins = ring_scatter(
        lambda k: jnp.concatenate(
            [cut(grad_query_full, k), cut(grad_key_full, k), cut(grad_value_full, k)], axis=0
        )
    )
    grad_query = grad_ins[:query_cols].T
    grad_key = grad_ins[query_cols : query_cols + key_cols].T
    grad_value = grad_ins[query_cols + key_cols :].T

    grad_gains = sum_over_all(jnp.stack([grad_one, grad_two, grad_three, grad_four]))
    grad_gains = lax.dynamic_slice_in_dim(grad_gains, own_place, share, axis=1)
    return (
        block_out[None].astype(BF16),
        grad_in[None],
        grad_query,
        grad_key,
        grad_value,
        grad_output,
        grad_gate,
        grad_up,
        grad_down,
        grad_gains[0],
        grad_gains[1],
        grad_gains[2],
        grad_gains[3],
    )


def solution(mesh):
    rows = P("fsdp", "ctx", None)
    columns = P(None, ("fsdp", "ctx"))
    units = P(("fsdp", "ctx"), None)
    gain = P(("ctx", "fsdp"))
    weights = (columns, columns, columns, units, columns, columns, units)
    return jax.shard_map(
        body,
        mesh=mesh,
        in_specs=(rows, P()) + weights + (gain,) * 4 + (rows,),
        out_specs=(rows, rows) + weights + (gain,) * 4,
        check_vma=False,
    )
```

time: 2170 us -> 798 us (0.37)
  waiting for transfers between devices: 1760 us -> 380 us
  starting transfers between devices: 4.01 us -> 123 us
  blocking collectives: 85.4 us -> 0 us
    reduce_scatter x11 -> x0, waiting for transfers between devices: 832 us -> none  [the longest x1 180 us: body(): lax.psum_scatter(grad_gate_full.astype(jnp.bfloat16), 'ctx', scatter_dime...]
    all_gather x13 -> x0, waiting for transfers between devices: 749 us -> none  [the longest x1 155 us: body(): lax.all_gather(weight_gate, 'ctx', axis=1, tiled=True)]
    ppermute x8 -> x120, waiting for transfers between devices: 171 us -> 380 us  [the longest x80 257 us: ring_hop(): lax.ppermute(block, 'ctx', [(order[i], order[(i + step) % size]) for i in...]
    ppermute x8 -> x120, starting transfers between devices: 1.94 us -> 123 us  [the longest x80 95.3 us: ring_hop(): lax.ppermute(block, 'ctx', [(order[i], order[(i + step) % size]) for i in...]
    unnamed x2 -> x0, blocking collectives: 85.4 us -> none
    dot_general x63 -> x69, matrix products: 185 us -> 182 us  [the longest x63 170 us: dot(): return lax.dot_general(a, b, (dims, ((), ())), preferred_element_type=F32)]
  transfers between devices with their start and end apart: 32 -> 120, of which waited for: 31 -> 64; matrix products, arithmetic and copies ran while one was open for 6% -> 27% of each run, Pallas kernels for 0% -> 0%
where the time goes in v1:
time: 798 us; the launch traced here: 787 us
  waiting for transfers between devices  380 us (48%)
  matrix products  182 us (23%)
  starting transfers between devices  123 us (15%)
  local copies, waits for them, and re-layouts  54.9 us (7%)
  other arithmetic  42.8 us (5%)
    ppermute x80, waiting for transfers between devices, ring_hop(): lax.ppermute(block, 'ctx', [(order[i], order[(i + step) % size]) for i in...  257 us
    dot_general x63, matrix products, dot(): return lax.dot_general(a, b, (dims, ((), ())), preferred_element_type=F32)  170 us
    ppermute x30, waiting for transfers between devices, cube_hop(): return lax.ppermute(block, 'fsdp', [(i, i ^ mask) for i in range(size)])  105 us
    ppermute x80, starting transfers between devices, ring_hop(): lax.ppermute(block, 'ctx', [(order[i], order[(i + step) % size]) for i in...  95.3 us
    ppermute x10, waiting for transfers between devices, sum_over_all(): lax.ppermute(block, axis, [(i, i ^ mask) for i in range(size)])  19 us
    dynamic_update_slice x23, local copies, waits for them, and re-layouts, put_blocks(): whole = lax.dynamic_update_slice_in_dim(whole, block, at * size, axis=0)  17.7 us
    unnamed x214, local copies, waits for them, and re-layouts  16.4 us
  transfers between devices with their start and end apart: 120, of which 64 were waited for; matrix products, arithmetic and copies ran while one was open for 27% of the time, Pallas kernels for 0%

profile of v1, /device:TPU:0, one launch (start us, length us, event | category | flops | bytes accessed | tf_op | source)
XLA Modules:
  0.0 786.9 jit_solution(17416843396713390826)
XLA Ops:
  47.1 3.6 collective-permute-done.26
  59.5 9.6 %collective-permute-done.28 = bf16[64,2304]{1,0:T(8,128)(2,1)S(1)} collective-permute-done((bf16[64,2304]{1,0:T(8,128)(2,1)S(1)}, bf16[64,2304]{1,0:T(8,128)(2,1)S(1)}, u32[]{:S(2)}, u32[]{:S(2)}) %collective-permute-start.28) | collective-permute-done | bytes 294944 | tf_op jit(solution)/shard_map/ppermute | solution.py:23
  79.1 11.7 %collective-permute-done.11 = bf16[128,2304]{1,0:T(8,128)(2,1)S(1)} collective-permute-done((bf16[128,2304]{1,0:T(8,128)(2,1)}, bf16[128,2304]{1,0:T(8,128)(2,1)S(1)}, u32[]{:S(2)}, u32[]{:S(2)}) %collective-permute-start.11) | collective-permute-done | bytes 589856 | tf_op jit(solution)/shard_map/ppermute | solution.py:23
  93.9 10.0 %collective-permute-done.12 = bf16[128,2304]{1,0:T(8,128)(2,1)S(1)} collective-permute-done((bf16[128,2304]{1,0:T(8,128)(2,1)S(1)}, bf16[128,2304]{1,0:T(8,128)(2,1)S(1)}, u32[]{:S(2)}, u32[]{:S(2)}) %collective-permute-start.12) | collective-permute-done | bytes 589856 | tf_op jit(solution)/shard_map/ppermute | solution.py:23
  105.7 11.6 %collective-permute-done.13 = bf16[128,2304]{1,0:T(8,128)(2,1)S(1)} collective-permute-done((bf16[128,2304]{1,0:T(8,128)(2,1)S(1)}, bf16[128,2304]{1,0:T(8,128)(2,1)S(1)}, u32[]{:S(2)}, u32[]{:S(2)}) %collective-permute-start.13) | collective-permute-done | bytes 589856 | tf_op jit(solution)/shard_map/ppermute | solution.py:23
  120.6 3.5 collective-permute-done.15
  137.0 14.8 %collective-permute-done.14 = bf16[64,2304]{1,0:T(8,128)(2,1)S(1)} collective-permute-done((bf16[64,2304]{1,0:T(8,128)(2,1)S(1)}, bf16[64,2304]{1,0:T(8,128)(2,1)S(1)}, u32[]{:S(2)}, u32[]{:S(2)}) %collective-permute-start.14) | collective-permute-done | bytes 294944 | tf_op jit(solution)/shard_map/ppermute | solution.py:23
  160.0 5.8 collective-permute-done.18
  173.3 4.8 collective-permute-done.20
  192.5 3.2 fusion.155
  204.6 11.1 %collective-permute-done.34 = bf16[128,2304]{1,0:T(8,128)(2,1)S(1)} collective-permute-done((bf16[128,2304]{1,0:T(8,128)(2,1)S(1)}, bf16[128,2304]{1,0:T(8,128)(2,1)S(1)}, u32[]{:S(2)}, u32[]{:S(2)}) %collective-permute-start.34) | collective-permute-done | bytes 589856 | tf_op jit(solution)/shard_map/ppermute | solution.py:75
  222.8 8.8 %collective-permute-done.47 = bf16[128,2304]{1,0:T(8,128)(2,1)S(1)} collective-permute-done((bf16[128,2304]{1,0:T(8,128)(2,1)S(1)}, bf16[128,2304]{1,0:T(8,128)(2,1)S(1)}, u32[]{:S(2)}, u32[]{:S(2)}) %collective-permute-start.47) | collective-permute-done | bytes 589856 | tf_op jit(solution)/shard_map/ppermute | solution.py:23
  241.1 3.9 collective-permute-done.48
  254.5 3.9 collective-permute-done.49
  273.8 3.4 convolution_convert_fusion
  279.4 4.7 collective-permute-done.52
  284.1 3.5 fusion.17
  289.3 3.5 fusion.20
  293.2 5.0 collective-permute-done.53
  298.2 3.5 fusion.16
  303.4 3.5 fusion.19
  307.3 5.8 collective-permute-done.54
  313.1 3.5 fusion.15
  318.5 3.5 fusion.18
  322.5 4.3 collective-permute-done.55
  326.8 5.2 collective-permute-done.59
  332.0 3.6 multiply_reduce_fusion.4
  339.7 5.1 constant_dynamic-update-slice_fusion.21
  347.5 5.1 constant_dynamic-update-slice_fusion.20
  352.6 5.2 constant_dynamic-update-slice_fusion.19
  362.1 7.6 collective-permute-done.64
  369.7 5.2 constant_dynamic-update-slice_fusion.18
  374.9 5.2 constant_dynamic-update-slice_fusion.17
  384.2 7.8 collective-permute-done.65
  392.0 5.2 constant_dynamic-update-slice_fusion.16
  397.2 5.2 constant_dynamic-update-slice_fusion.15
  406.6 4.8 collective-permute-done.66
  413.9 5.1 constant_dynamic-update-slice_fusion.14
  424.8 8.2 %fusion.159 = (bf16[1152,2304]{1,0:T(8,128)(2,1)S(1)}, f32[1152,2304]{1,0:T(8,128)}) fusion(bf16[1024,1152]{1,0:T(8,128)(2,1)S(1)} %get-tuple-element.36, bf16[1024,2304]{1,0:T(8,128)(2,1)S(1)} %constant_dynamic-update-slice_fusion.47), kind=kOutput, calls=%fused_computation.472 | convolution fusion | flops 5438472192 | bytes 23003136 | tf_op jit(solution)/shard_map/dot_general | solution.py:127
  435.1 8.9 %fusion.158 = (bf16[1152,2304]{1,0:T(8,128)(2,1)S(1)}, f32[1152,2304]{1,0:T(8,128)S(1)}) fusion(bf16[1024,1152]{1,0:T(8,128)(2,1)} %get-tuple-element.137, bf16[1024,2304]{1,0:T(8,128)(2,1)} %copy-done.52), kind=kOutput, calls=%fused_computation.471 | convolution fusion | flops 5438472192 | bytes 23003136 | tf_op jit(solution)/shard_map/dot_general | solution.py:127
  445.8 14.3 %fusion.157 = (bf16[1152,2304]{1,0:T(8,128)(2,1)S(1)}, f32[1152,2304]{1,0:T(8,128)}) fusion(bf16[1024,1152]{1,0:T(8,128)(2,1)} %copy-done.87, bf16[1024,2304]{1,0:T(8,128)(2,1)} %copy-done.52), kind=kOutput, calls=%fused_computation.470 | convolution fusion | flops 5438472192 | bytes 23003136 | tf_op jit(solution)/shard_map/dot_general | solution.py:127
  466.5 11.0 %collective-permute-done.69 = bf16[128,2304]{1,0:T(8,128)(2,1)S(1)} collective-permute-done((bf16[128,2304]{1,0:T(8,128)(2,1)S(1)}, bf16[128,2304]{1,0:T(8,128)(2,1)S(1)}, u32[]{:S(2)}, u32[]{:S(2)}) %collective-permute-start.69) | collective-permute-done | bytes 589856 | tf_op jit(solution)/shard_map/ppermute | solution.py:23
  487.4 9.5 %collective-permute-done.70 = bf16[128,2304]{1,0:T(8,128)(2,1)S(1)} collective-permute-done((bf16[128,2304]{1,0:T(8,128)(2,1)S(1)}, bf16[128,2304]{1,0:T(8,128)(2,1)S(1)}, u32[]{:S(2)}, u32[]{:S(2)}) %collective-permute-start.70) | collective-permute-done | bytes 589856 | tf_op jit(solution)/shard_map/ppermute | solution.py:23
  502.8 11.2 %collective-permute-done.71 = bf16[128,2304]{1,0:T(8,128)(2,1)S(1)} collective-permute-done((bf16[128,2304]{1,0:T(8,128)(2,1)S(1)}, bf16[128,2304]{1,0:T(8,128)(2,1)S(1)}, u32[]{:S(2)}, u32[]{:S(2)}) %collective-permute-start.71) | collective-permute-done | bytes 589856 | tf_op jit(solution)/shard_map/ppermute | solution.py:23
  521.3 24.7 %collective-permute-done.114 = bf16[288,2304]{1,0:T(8,128)(2,1)S(1)} collective-permute-done((bf16[288,2304]{1,0:T(8,128)(2,1)S(1)}, bf16[288,2304]{1,0:T(8,128)(2,1)S(1)}, u32[]{:S(2)}, u32[]{:S(2)}) %collective-permute-start.114) | collective-permute-done | bytes 1327136 | tf_op jit(solution)/shard_map/ppermute | solution.py:75
  547.7 4.1 fusion.24
  551.9 61.2 %collective-permute-done.76 = bf16[128,2304]{1,0:T(8,128)(2,1)S(1)} collective-permute-done((bf16[128,2304]{1,0:T(8,128)(2,1)S(1)}, bf16[128,2304]{1,0:T(8,128)(2,1)S(1)}, u32[]{:S(2)}, u32[]{:S(2)}) %collective-permute-start.76) | collective-permute-done | bytes 589856 | tf_op jit(solution)/shard_map/ppermute | solution.py:75
  613.0 4.0 fusion.27
  625.1 4.1 convolution_bitcast_fusion
  638.2 3.6 collective-permute-done.98
  645.6 4.7 collective-permute-done.99
  654.8 5.5 collective-permute-done.100
  666.0 3.6 collective-permute-done.103
  673.3 5.1 collective-permute-done.80
  683.8 3.4 collective-permute-done.104
  690.7 5.2 collective-permute-done.81
  701.3 3.4 collective-permute-done.105
  705.6 4.7 collective-permute-done.82
  710.3 3.2 collective-permute-done.86
  727.4 3.9 collective-permute-done.94
  733.1 6.3 collective-permute-done.89
  748.1 8.4 %collective-permute-done.92 = bf16[128,2304]{1,0:T(8,128)(2,1)S(1)} collective-permute-done((bf16[128,2304]{1,0:T(8,128)(2,1)S(1)}, bf16[128,2304]{1,0:T(8,128)(2,1)S(1)}, u32[]{:S(2)}, u32[]{:S(2)}) %collective-permute-start.92) | collective-permute-done | bytes 589856 | tf_op jit(solution)/shard_map/ppermute | solution.py:23
  758.3 11.4 %collective-permute-done.118 = f32[4,2304]{1,0:T(4,128)S(1)} collective-permute-done((f32[4,2304]{1,0:T(4,128)S(1)}, f32[4,2304]{1,0:T(4,128)S(1)}, u32[]{:S(2)}, u32[]{:S(2)}) %collective-permute-start.118) | collective-permute-done | bytes 36896 | tf_op jit(solution)/shard_map/ppermute | solution.py:103
  775.8 8.8 %collective-permute-done.97 = bf16[128,2304]{1,0:T(8,128)(2,1)S(1)} collective-permute-done((bf16[128,2304]{1,0:T(8,128)(2,1)S(1)}, bf16[128,2304]{1,0:T(8,128)(2,1)S(1)}, u32[]{:S(2)}, u32[]{:S(2)}) %collective-permute-start.97) | collective-permute-done | bytes 589856 | tf_op jit(solution)/shard_map/ppermute | solution.py:23
  (630 shorter events, 320.2 us)
Async XLA Ops:
  2.7 41.3 %collective-permute-start.8 = (bf16[128,2304]{1,0:T(8,128)(2,1)}, bf16[128,2304]{1,0:T(8,128)(2,1)}, u32[]{:S(2)}, u32[]{:S(2)}) collective-permute-start(bf16[128,2304]{1,0:T(8,128)(2,1)} %pad_maximum_fusion.5), channel_id=1, source_target_pairs={{0,8},{8,16},{16,24},{24,28},{28,20},{20,12},{12,4},{4,0},{1,9},{9... | collective-permute-start | bytes 1769480 | tf_op jit(solution)/shard_map/ppermute | solution.py:23
  5.7 39.7 %collective-permute-start.9 = (bf16[128,2304]{1,0:T(8,128)(2,1)}, bf16[128,2304]{1,0:T(8,128)(2,1)}, u32[]{:S(2)}, u32[]{:S(2)}) collective-permute-start(bf16[128,2304]{1,0:T(8,128)(2,1)} %pad_maximum_fusion.5), channel_id=1, source_target_pairs={{0,4},{8,0},{16,8},{24,16},{28,24},{20,28},{12,20},{4,12},{1,5},{9... | collective-permute-start | bytes 1769480 | tf_op jit(solution)/shard_map/ppermute | solution.py:23
  5.7 33.0 %collective-permute-start.24 = (bf16[64,2304]{1,0:T(8,128)(2,1)}, bf16[64,2304]{1,0:T(8,128)(2,1)}, u32[]{:S(2)}, u32[]{:S(2)}) collective-permute-start(bf16[64,2304]{1,0:T(8,128)(2,1)} %param.19), channel_id=1, source_target_pairs={{0,8},{8,16},{16,24},{24,28},{28,20},{20,12},{12,4},{4,0},{1,9},{9... | collective-permute-start | bytes 884744 | tf_op jit(solution)/shard_map/ppermute | solution.py:23
  7.7 32.9 %collective-permute-start.25 = (bf16[64,2304]{1,0:T(8,128)(2,1)}, bf16[64,2304]{1,0:T(8,128)(2,1)}, u32[]{:S(2)}, u32[]{:S(2)}) collective-permute-start(bf16[64,2304]{1,0:T(8,128)(2,1)} %param.19), channel_id=1, source_target_pairs={{0,4},{8,0},{16,8},{24,16},{28,24},{20,28},{12,20},{4,12},{1,5},{9... | collective-permute-start | bytes 884744 | tf_op jit(solution)/shard_map/ppermute | solution.py:23
  36.5 145.1 %collective-permute-start.35 = (bf16[288,2304]{1,0:T(8,128)(2,1)}, bf16[288,2304]{1,0:T(8,128)(2,1)}, u32[]{:S(2)}, u32[]{:S(2)}) collective-permute-start(bf16[288,2304]{1,0:T(8,128)(2,1)} %bitcast.235), channel_id=1, source_target_pairs={{0,2},{1,3},{2,0},{3,1},{4,6},{5,7},{6,4},{7,5},{8,10},{9,11},{10,... | collective-permute-start | bytes 3981320 | tf_op jit(solution)/shard_map/ppermute | solution.py:75
  38.7 157.1 %collective-permute-start.36 = (bf16[288,2304]{1,0:T(8,128)(2,1)}, bf16[288,2304]{1,0:T(8,128)(2,1)}, u32[]{:S(2)}, u32[]{:S(2)}) collective-permute-start(bf16[288,2304]{1,0:T(8,128)(2,1)} %bitcast.236), channel_id=1, source_target_pairs={{0,1},{1,0},{2,3},{3,2},{4,5},{5,4},{6,7},{7,6},{8,9},{9,8},{10,11... | collective-permute-start | bytes 3981320 | tf_op jit(solution)/shard_map/ppermute | solution.py:75
  45.4 31.9 %collective-permute-start.10 = (bf16[128,2304]{1,0:T(8,128)(2,1)}, bf16[128,2304]{1,0:T(8,128)(2,1)S(1)}, u32[]{:S(2)}, u32[]{:S(2)}) collective-permute-start(bf16[128,2304]{1,0:T(8,128)(2,1)} %collective-permute-done.8), channel_id=1, source_target_pairs={{0,8},{8,16},{16,24},{24,28},{28,20},{20,12},{12,4},{4,0},{1,9},{9... | collective-permute-start | bytes 1769480 | tf_op jit(solution)/shard_map/ppermute | solution.py:23
  50.7 18.4 %collective-permute-start.28 = (bf16[64,2304]{1,0:T(8,128)(2,1)S(1)}, bf16[64,2304]{1,0:T(8,128)(2,1)S(1)}, u32[]{:S(2)}, u32[]{:S(2)}) collective-permute-start(bf16[64,2304]{1,0:T(8,128)(2,1)S(1)} %collective-permute-done.26), channel_id=1, source_target_pairs={{0,8},{8,16},{16,24},{24,28},{28,20},{20,12},{12,4},{4,0},{1,9},{9... | collective-permute-start | bytes 884744 | tf_op jit(solution)/shard_map/ppermute | solution.py:23
  53.2 17.6 %collective-permute-start.29 = (bf16[64,2304]{1,0:T(8,128)(2,1)S(1)}, bf16[64,2304]{1,0:T(8,128)(2,1)S(1)}, u32[]{:S(2)}, u32[]{:S(2)}) collective-permute-start(bf16[64,2304]{1,0:T(8,128)(2,1)S(1)} %collective-permute-done.27), channel_id=1, source_target_pairs={{0,4},{8,0},{16,8},{24,16},{28,24},{20,28},{12,20},{4,12},{1,5},{9... | collective-permute-start | bytes 884744 | tf_op jit(solution)/shard_map/ppermute | solution.py:23
  74.5 57.9 %collective-permute-start.41 = (bf16[288,2304]{1,0:T(8,128)(2,1)S(1)}, bf16[288,2304]{1,0:T(8,128)(2,1)S(1)}, u32[]{:S(2)}, u32[]{:S(2)}) collective-permute-start(bf16[288,2304]{1,0:T(8,128)(2,1)S(1)} %copy-done.23), channel_id=1, source_target_pairs={{0,2},{1,3},{2,0},{3,1},{4,6},{5,7},{6,4},{7,5},{8,10},{9,11},{10,... | collective-permute-start | bytes 3981320 | tf_op jit(solution)/shard_map/ppermute | solution.py:75
  76.0 44.6 %collective-permute-start.5 = (bf16[128,2304]{1,0:T(8,128)(2,1)S(1)}, bf16[128,2304]{1,0:T(8,128)(2,1)S(1)}, u32[]{:S(2)}, u32[]{:S(2)}) collective-permute-start(bf16[128,2304]{1,0:T(8,128)(2,1)S(1)} %fusion.42), channel_id=1, source_target_pairs={{0,2},{1,3},{2,0},{3,1},{4,6},{5,7},{6,4},{7,5},{8,10},{9,11},{10,... | collective-permute-start | bytes 1769480 | tf_op jit(solution)/shard_map/ppermute | solution.py:75
  77.3 13.6 %collective-permute-start.11 = (bf16[128,2304]{1,0:T(8,128)(2,1)}, bf16[128,2304]{1,0:T(8,128)(2,1)S(1)}, u32[]{:S(2)}, u32[]{:S(2)}) collective-permute-start(bf16[128,2304]{1,0:T(8,128)(2,1)} %collective-permute-done.9), channel_id=1, source_target_pairs={{0,4},{8,0},{16,8},{24,16},{28,24},{20,28},{12,20},{4,12},{1,5},{9... | collective-permute-start | bytes 1769480 | tf_op jit(solution)/shard_map/ppermute | solution.py:23
  103.9 13.4 %collective-permute-start.13 = (bf16[128,2304]{1,0:T(8,128)(2,1)S(1)}, bf16[128,2304]{1,0:T(8,128)(2,1)S(1)}, u32[]{:S(2)}, u32[]{:S(2)}) collective-permute-start(bf16[128,2304]{1,0:T(8,128)(2,1)S(1)} %collective-permute-done.11), channel_id=1, source_target_pairs={{0,4},{8,0},{16,8},{24,16},{28,24},{20,28},{12,20},{4,12},{1,5},{9... | collective-permute-start | bytes 1769480 | tf_op jit(solution)/shard_map/ppermute | solution.py:23
  131.5 21.2 %collective-permute-start.16 = (bf16[4,2,128,256]{3,2,0,1:T(8,128)(2,1)S(1)}, bf16[4,2,128,256]{3,2,0,1:T(8,128)(2,1)}, u32[]{:S(2)}, u32[]{:S(2)}) collective-permute-start(bf16[4,2,128,256]{3,2,0,1:T(8,128)(2,1)S(1)} %get-tuple-element.181), channel_id=1, source_target_pairs={{0,8},{8,16},{16,24},{24,28},{28,20},{20,12},{12,4},{4,0},{1,9},{9... | collective-permute-start | bytes 1572872 | tf_op jit(solution)/shard_map/ppermute | solution.py:23
  132.4 22.1 %collective-permute-start.17 = (bf16[4,2,128,256]{3,2,0,1:T(8,128)(2,1)S(1)}, bf16[4,2,128,256]{3,2,0,1:T(8,128)(2,1)}, u32[]{:S(2)}, u32[]{:S(2)}) collective-permute-start(bf16[4,2,128,256]{3,2,0,1:T(8,128)(2,1)S(1)} %get-tuple-element.181), channel_id=1, source_target_pairs={{0,4},{8,0},{16,8},{24,16},{28,24},{20,28},{12,20},{4,12},{1,5},{9... | collective-permute-start | bytes 1572872 | tf_op jit(solution)/shard_map/ppermute | solution.py:23
  134.8 17.0 %collective-permute-start.14 = (bf16[64,2304]{1,0:T(8,128)(2,1)S(1)}, bf16[64,2304]{1,0:T(8,128)(2,1)S(1)}, u32[]{:S(2)}, u32[]{:S(2)}) collective-permute-start(bf16[64,2304]{1,0:T(8,128)(2,1)S(1)} %get-tuple-element.165), channel_id=1, source_target_pairs={{0,8},{8,16},{16,24},{24,28},{28,20},{20,12},{12,4},{4,0},{1,9},{9... | collective-permute-start | bytes 884744 | tf_op jit(solution)/shard_map/ppermute | solution.py:23
  151.8 30.7 %collective-permute-start.38 = (bf16[288,2304]{1,0:T(8,128)(2,1)}, bf16[288,2304]{1,0:T(8,128)(2,1)}, u32[]{:S(2)}, u32[]{:S(2)}) collective-permute-start(bf16[288,2304]{1,0:T(8,128)(2,1)} %bitcast.21), channel_id=1, source_target_pairs={{0,2},{1,3},{2,0},{3,1},{4,6},{5,7},{6,4},{7,5},{8,10},{9,11},{10,... | collective-permute-start | bytes 3981320 | tf_op jit(solution)/shard_map/ppermute | solution.py:75
  152.7 13.2 %collective-permute-start.18 = (bf16[4,2,128,256]{3,2,0,1:T(8,128)(2,1)}, bf16[4,2,128,256]{3,2,0,1:T(8,128)(2,1)}, u32[]{:S(2)}, u32[]{:S(2)}) collective-permute-start(bf16[4,2,128,256]{3,2,0,1:T(8,128)(2,1)} %collective-permute-done.16), channel_id=1, source_target_pairs={{0,8},{8,16},{16,24},{24,28},{28,20},{20,12},{12,4},{4,0},{1,9},{9... | collective-permute-start | bytes 1572872 | tf_op jit(solution)/shard_map/ppermute | solution.py:23
  154.4 13.2 %collective-permute-start.19 = (bf16[4,2,128,256]{3,2,0,1:T(8,128)(2,1)}, bf16[4,2,128,256]{3,2,0,1:T(8,128)(2,1)}, u32[]{:S(2)}, u32[]{:S(2)}) collective-permute-start(bf16[4,2,128,256]{3,2,0,1:T(8,128)(2,1)} %collective-permute-done.17), channel_id=1, source_target_pairs={{0,4},{8,0},{16,8},{24,16},{28,24},{20,28},{12,20},{4,12},{1,5},{9... | collective-permute-start | bytes 1572872 | tf_op jit(solution)/shard_map/ppermute | solution.py:23
  181.5 19.2 %collective-permute-start.39 = (bf16[288,2304]{1,0:T(8,128)(2,1)}, bf16[288,2304]{1,0:T(8,128)(2,1)S(1)}, u32[]{:S(2)}, u32[]{:S(2)}) collective-permute-start(bf16[288,2304]{1,0:T(8,128)(2,1)} %bitcast.21), channel_id=1, source_target_pairs={{0,1},{1,0},{2,3},{3,2},{4,5},{5,4},{6,7},{7,6},{8,9},{9,8},{10,11... | collective-permute-start | bytes 3981320 | tf_op jit(solution)/shard_map/ppermute | solution.py:75
  182.5 20.9 %collective-permute-start.43 = (bf16[288,2304]{1,0:T(8,128)(2,1)S(1)}, bf16[288,2304]{1,0:T(8,128)(2,1)S(1)}, u32[]{:S(2)}, u32[]{:S(2)}) collective-permute-start(bf16[288,2304]{1,0:T(8,128)(2,1)S(1)} %copy-done.25), channel_id=1, source_target_pairs={{0,1},{1,0},{2,3},{3,2},{4,5},{5,4},{6,7},{7,6},{8,9},{9,8},{10,11... | collective-permute-start | bytes 3981320 | tf_op jit(solution)/shard_map/ppermute | solution.py:75
  186.5 14.3 %collective-permute-start.40 = (bf16[288,2304]{1,0:T(8,128)(2,1)}, bf16[288,2304]{1,0:T(8,128)(2,1)S(1)}, u32[]{:S(2)}, u32[]{:S(2)}) collective-permute-start(bf16[288,2304]{1,0:T(8,128)(2,1)} %collective-permute-done.38), channel_id=1, source_target_pairs={{0,1},{1,0},{2,3},{3,2},{4,5},{5,4},{6,7},{7,6},{8,9},{9,8},{10,11... | collective-permute-start | bytes 3981320 | tf_op jit(solution)/shard_map/ppermute | solution.py:75
  200.4 15.3 %collective-permute-start.34 = (bf16[128,2304]{1,0:T(8,128)(2,1)S(1)}, bf16[128,2304]{1,0:T(8,128)(2,1)S(1)}, u32[]{:S(2)}, u32[]{:S(2)}) collective-permute-start(bf16[128,2304]{1,0:T(8,128)(2,1)S(1)} %fusion.54), channel_id=1, source_target_pairs={{0,2},{1,3},{2,0},{3,1},{4,6},{5,7},{6,4},{7,5},{8,10},{9,11},{10,... | collective-permute-start | bytes 1769480 | tf_op jit(solution)/shard_map/ppermute | solution.py:75
  217.1 14.4 %collective-permute-start.47 = (bf16[128,2304]{1,0:T(8,128)(2,1)S(1)}, bf16[128,2304]{1,0:T(8,128)(2,1)S(1)}, u32[]{:S(2)}, u32[]{:S(2)}) collective-permute-start(bf16[128,2304]{1,0:T(8,128)(2,1)S(1)} %get-tuple-element.69), channel_id=1, source_target_pairs={{0,8},{8,16},{16,24},{24,28},{28,20},{20,12},{12,4},{4,0},{1,9},{9... | collective-permute-start | bytes 1769480 | tf_op jit(solution)/shard_map/ppermute | solution.py:23
  218.8 16.2 %collective-permute-start.44 = (bf16[128,2304]{1,0:T(8,128)(2,1)S(1)}, bf16[128,2304]{1,0:T(8,128)(2,1)S(1)}, u32[]{:S(2)}, u32[]{:S(2)}) collective-permute-start(bf16[128,2304]{1,0:T(8,128)(2,1)S(1)} %get-tuple-element.69), channel_id=1, source_target_pairs={{0,4},{8,0},{16,8},{24,16},{28,24},{20,28},{12,20},{4,12},{1,5},{9... | collective-permute-start | bytes 1769480 | tf_op jit(solution)/shard_map/ppermute | solution.py:23
  231.6 13.5 %collective-permute-start.48 = (bf16[128,2304]{1,0:T(8,128)(2,1)S(1)}, bf16[128,2304]{1,0:T(8,128)(2,1)S(1)}, u32[]{:S(2)}, u32[]{:S(2)}) collective-permute-start(bf16[128,2304]{1,0:T(8,128)(2,1)S(1)} %collective-permute-done.47), channel_id=1, source_target_pairs={{0,8},{8,16},{16,24},{24,28},{28,20},{20,12},{12,4},{4,0},{1,9},{9... | collective-permute-start | bytes 1769480 | tf_op jit(solution)/shard_map/ppermute | solution.py:23
  235.0 13.7 %collective-permute-start.45 = (bf16[128,2304]{1,0:T(8,128)(2,1)S(1)}, bf16[128,2304]{1,0:T(8,128)(2,1)S(1)}, u32[]{:S(2)}, u32[]{:S(2)}) collective-permute-start(bf16[128,2304]{1,0:T(8,128)(2,1)S(1)} %collective-permute-done.44), channel_id=1, source_target_pairs={{0,4},{8,0},{16,8},{24,16},{28,24},{20,28},{12,20},{4,12},{1,5},{9... | collective-permute-start | bytes 1769480 | tf_op jit(solution)/shard_map/ppermute | solution.py:23
  245.0 13.4 %collective-permute-start.49 = (bf16[128,2304]{1,0:T(8,128)(2,1)S(1)}, bf16[128,2304]{1,0:T(8,128)(2,1)S(1)}, u32[]{:S(2)}, u32[]{:S(2)}) collective-permute-start(bf16[128,2304]{1,0:T(8,128)(2,1)S(1)} %collective-permute-done.48), channel_id=1, source_target_pairs={{0,8},{8,16},{16,24},{24,28},{28,20},{20,12},{12,4},{4,0},{1,9},{9... | collective-permute-start | bytes 1769480 | tf_op jit(solution)/shard_map/ppermute | solution.py:23
  361.6 13.3 %collective-permute-start.61 = (bf16[128,2304]{1,0:T(8,128)(2,1)S(1)}, bf16[128,2304]{1,0:T(8,128)(2,1)S(1)}, u32[]{:S(2)}, u32[]{:S(2)}) collective-permute-start(bf16[128,2304]{1,0:T(8,128)(2,1)S(1)} %collective-permute-done.60), channel_id=1, source_target_pairs={{0,4},{8,0},{16,8},{24,16},{28,24},{20,28},{12,20},{4,12},{1,5},{9... | collective-permute-start | bytes 1769480 | tf_op jit(solution)/shard_map/ppermute | solution.py:23
  383.9 13.3 %collective-permute-start.62 = (bf16[128,2304]{1,0:T(8,128)(2,1)S(1)}, bf16[128,2304]{1,0:T(8,128)(2,1)S(1)}, u32[]{:S(2)}, u32[]{:S(2)}) collective-permute-start(bf16[128,2304]{1,0:T(8,128)(2,1)S(1)} %collective-permute-done.61), channel_id=1, source_target_pairs={{0,4},{8,0},{16,8},{24,16},{28,24},{20,28},{12,20},{4,12},{1,5},{9... | collective-permute-start | bytes 1769480 | tf_op jit(solution)/shard_map/ppermute | solution.py:23
  422.3 37.8 %collective-permute-start.68 = (bf16[64,2304]{1,0:T(8,128)(2,1)}, bf16[64,2304]{1,0:T(8,128)(2,1)}, u32[]{:S(2)}, u32[]{:S(2)}) collective-permute-start(bf16[64,2304]{1,0:T(8,128)(2,1)} %get-tuple-element.161), channel_id=1, source_target_pairs={{0,8},{8,16},{16,24},{24,28},{28,20},{20,12},{12,4},{4,0},{1,9},{9... | collective-permute-start | bytes 884744 | tf_op jit(solution)/shard_map/ppermute | solution.py:23
  423.2 40.0 %collective-permute-start.72 = (bf16[64,2304]{1,0:T(8,128)(2,1)}, bf16[64,2304]{1,0:T(8,128)(2,1)}, u32[]{:S(2)}, u32[]{:S(2)}) collective-permute-start(bf16[64,2304]{1,0:T(8,128)(2,1)} %get-tuple-element.162), channel_id=1, source_target_pairs={{0,4},{8,0},{16,8},{24,16},{28,24},{20,28},{12,20},{4,12},{1,5},{9... | collective-permute-start | bytes 884744 | tf_op jit(solution)/shard_map/ppermute | solution.py:23
  434.6 46.5 %collective-permute-start.113 = (bf16[288,2304]{1,0:T(8,128)(2,1)}, bf16[288,2304]{1,0:T(8,128)(2,1)}, u32[]{:S(2)}, u32[]{:S(2)}) collective-permute-start(bf16[288,2304]{1,0:T(8,128)(2,1)} %get-tuple-element.98), channel_id=1, source_target_pairs={{0,1},{1,0},{2,3},{3,2},{4,5},{5,4},{6,7},{7,6},{8,9},{9,8},{10,11... | collective-permute-start | bytes 3981320 | tf_op jit(solution)/shard_map/ppermute | solution.py:75
  434.6 86.4 %collective-permute-start.112 = (bf16[288,2304]{1,0:T(8,128)(2,1)}, bf16[288,2304]{1,0:T(8,128)(2,1)}, u32[]{:S(2)}, u32[]{:S(2)}) collective-permute-start(bf16[288,2304]{1,0:T(8,128)(2,1)} %get-tuple-element.97), channel_id=1, source_target_pairs={{0,1},{1,0},{2,3},{3,2},{4,5},{5,4},{6,7},{7,6},{8,9},{9,8},{10,11... | collective-permute-start | bytes 3981320 | tf_op jit(solution)/shard_map/ppermute | solution.py:75
  445.8 38.0 %collective-permute-start.110 = (bf16[288,2304]{1,0:T(8,128)(2,1)}, bf16[288,2304]{1,0:T(8,128)(2,1)}, u32[]{:S(2)}, u32[]{:S(2)}) collective-permute-start(bf16[288,2304]{1,0:T(8,128)(2,1)} %get-tuple-element.100), channel_id=1, source_target_pairs={{0,1},{1,0},{2,3},{3,2},{4,5},{5,4},{6,7},{7,6},{8,9},{9,8},{10,11... | collective-permute-start | bytes 3981320 | tf_op jit(solution)/shard_map/ppermute | solution.py:75
  462.3 15.2 %collective-permute-start.69 = (bf16[128,2304]{1,0:T(8,128)(2,1)S(1)}, bf16[128,2304]{1,0:T(8,128)(2,1)S(1)}, u32[]{:S(2)}, u32[]{:S(2)}) collective-permute-start(bf16[128,2304]{1,0:T(8,128)(2,1)S(1)} %fusion.12), channel_id=1, source_target_pairs={{0,8},{8,16},{16,24},{24,28},{28,20},{20,12},{12,4},{4,0},{1,9},{9... | collective-permute-start | bytes 1769480 | tf_op jit(solution)/shard_map/ppermute | solution.py:23
  465.1 15.0 %collective-permute-start.73 = (bf16[128,2304]{1,0:T(8,128)(2,1)S(1)}, bf16[128,2304]{1,0:T(8,128)(2,1)S(1)}, u32[]{:S(2)}, u32[]{:S(2)}) collective-permute-start(bf16[128,2304]{1,0:T(8,128)(2,1)S(1)} %fusion.9), channel_id=1, source_target_pairs={{0,4},{8,0},{16,8},{24,16},{28,24},{20,28},{12,20},{4,12},{1,5},{9... | collective-permute-start | bytes 1769480 | tf_op jit(solution)/shard_map/ppermute | solution.py:23
  477.5 74.4 %collective-permute-start.109 = (bf16[288,2304]{1,0:T(8,128)(2,1)S(1)}, bf16[288,2304]{1,0:T(8,128)(2,1)S(1)}, u32[]{:S(2)}, u32[]{:S(2)}) collective-permute-start(bf16[288,2304]{1,0:T(8,128)(2,1)S(1)} %copy-done.26), channel_id=1, source_target_pairs={{0,1},{1,0},{2,3},{3,2},{4,5},{5,4},{6,7},{7,6},{8,9},{9,8},{10,11... | collective-permute-start | bytes 3981320 | tf_op jit(solution)/shard_map/ppermute | solution.py:75
  480.1 21.8 %collective-permute-start.107 = (bf16[288,2304]{1,0:T(8,128)(2,1)S(1)}, bf16[288,2304]{1,0:T(8,128)(2,1)S(1)}, u32[]{:S(2)}, u32[]{:S(2)}) collective-permute-start(bf16[288,2304]{1,0:T(8,128)(2,1)S(1)} %get-tuple-element.102), channel_id=1, source_target_pairs={{0,1},{1,0},{2,3},{3,2},{4,5},{5,4},{6,7},{7,6},{8,9},{9,8},{10,11... | collective-permute-start | bytes 3981320 | tf_op jit(solution)/shard_map/ppermute | solution.py:75
  481.1 15.8 %collective-permute-start.70 = (bf16[128,2304]{1,0:T(8,128)(2,1)S(1)}, bf16[128,2304]{1,0:T(8,128)(2,1)S(1)}, u32[]{:S(2)}, u32[]{:S(2)}) collective-permute-start(bf16[128,2304]{1,0:T(8,128)(2,1)S(1)} %fusion.13), channel_id=1, source_target_pairs={{0,8},{8,16},{16,24},{24,28},{28,20},{20,12},{12,4},{4,0},{1,9},{9... | collective-permute-start | bytes 1769480 | tf_op jit(solution)/shard_map/ppermute | solution.py:23
  483.8 15.5 %collective-permute-start.74 = (bf16[128,2304]{1,0:T(8,128)(2,1)S(1)}, bf16[128,2304]{1,0:T(8,128)(2,1)S(1)}, u32[]{:S(2)}, u32[]{:S(2)}) collective-permute-start(bf16[128,2304]{1,0:T(8,128)(2,1)S(1)} %fusion.10), channel_id=1, source_target_pairs={{0,4},{8,0},{16,8},{24,16},{28,24},{20,28},{12,20},{4,12},{1,5},{9... | collective-permute-start | bytes 1769480 | tf_op jit(solution)/shard_map/ppermute | solution.py:23
  496.9 120.1 %collective-permute-start.106 = (bf16[288,2304]{1,0:T(8,128)(2,1)S(1)}, bf16[288,2304]{1,0:T(8,128)(2,1)S(1)}, u32[]{:S(2)}, u32[]{:S(2)}) collective-permute-start(bf16[288,2304]{1,0:T(8,128)(2,1)S(1)} %get-tuple-element.101), channel_id=1, source_target_pairs={{0,1},{1,0},{2,3},{3,2},{4,5},{5,4},{6,7},{7,6},{8,9},{9,8},{10,11... | collective-permute-start | bytes 3981320 | tf_op jit(solution)/shard_map/ppermute | solution.py:75
  499.4 14.6 %collective-permute-start.71 = (bf16[128,2304]{1,0:T(8,128)(2,1)S(1)}, bf16[128,2304]{1,0:T(8,128)(2,1)S(1)}, u32[]{:S(2)}, u32[]{:S(2)}) collective-permute-start(bf16[128,2304]{1,0:T(8,128)(2,1)S(1)} %fusion.14), channel_id=1, source_target_pairs={{0,8},{8,16},{16,24},{24,28},{28,20},{20,12},{12,4},{4,0},{1,9},{9... | collective-permute-start | bytes 1769480 | tf_op jit(solution)/shard_map/ppermute | solution.py:23
  501.9 14.4 %collective-permute-start.75 = (bf16[128,2304]{1,0:T(8,128)(2,1)S(1)}, bf16[128,2304]{1,0:T(8,128)(2,1)S(1)}, u32[]{:S(2)}, u32[]{:S(2)}) collective-permute-start(bf16[128,2304]{1,0:T(8,128)(2,1)S(1)} %fusion.11), channel_id=1, source_target_pairs={{0,4},{8,0},{16,8},{24,16},{28,24},{20,28},{12,20},{4,12},{1,5},{9... | collective-permute-start | bytes 1769480 | tf_op jit(solution)/shard_map/ppermute | solution.py:23
  514.0 32.1 %collective-permute-start.114 = (bf16[288,2304]{1,0:T(8,128)(2,1)S(1)}, bf16[288,2304]{1,0:T(8,128)(2,1)S(1)}, u32[]{:S(2)}, u32[]{:S(2)}) collective-permute-start(bf16[288,2304]{1,0:T(8,128)(2,1)S(1)} %fusion.23), channel_id=1, source_target_pairs={{0,2},{1,3},{2,0},{3,1},{4,6},{5,7},{6,4},{7,5},{8,10},{9,11},{10,... | collective-permute-start | bytes 3981320 | tf_op jit(solution)/shard_map/ppermute | solution.py:75
  516.3 96.8 %collective-permute-start.111 = (bf16[288,2304]{1,0:T(8,128)(2,1)S(1)}, bf16[288,2304]{1,0:T(8,128)(2,1)S(1)}, u32[]{:S(2)}, u32[]{:S(2)}) collective-permute-start(bf16[288,2304]{1,0:T(8,128)(2,1)S(1)} %fusion.25), channel_id=1, source_target_pairs={{0,2},{1,3},{2,0},{3,1},{4,6},{5,7},{6,4},{7,5},{8,10},{9,11},{10,... | collective-permute-start | bytes 3981320 | tf_op jit(solution)/shard_map/ppermute | solution.py:75
  520.9 96.1 %collective-permute-start.108 = (bf16[288,2304]{1,0:T(8,128)(2,1)S(1)}, bf16[288,2304]{1,0:T(8,128)(2,1)S(1)}, u32[]{:S(2)}, u32[]{:S(2)}) collective-permute-start(bf16[288,2304]{1,0:T(8,128)(2,1)S(1)} %fusion.28), channel_id=1, source_target_pairs={{0,2},{1,3},{2,0},{3,1},{4,6},{5,7},{6,4},{7,5},{8,10},{9,11},{10,... | collective-permute-start | bytes 3981320 | tf_op jit(solution)/shard_map/ppermute | solution.py:75
  546.1 67.0 %collective-permute-start.76 = (bf16[128,2304]{1,0:T(8,128)(2,1)S(1)}, bf16[128,2304]{1,0:T(8,128)(2,1)S(1)}, u32[]{:S(2)}, u32[]{:S(2)}) collective-permute-start(bf16[128,2304]{1,0:T(8,128)(2,1)S(1)} %fusion.46), channel_id=1, source_target_pairs={{0,2},{1,3},{2,0},{3,1},{4,6},{5,7},{6,4},{7,5},{8,10},{9,11},{10,... | collective-permute-start | bytes 1769480 | tf_op jit(solution)/shard_map/ppermute | solution.py:75
  551.9 67.0 %collective-permute-start.77 = (bf16[128,2304]{1,0:T(8,128)(2,1)S(1)}, bf16[128,2304]{1,0:T(8,128)(2,1)S(1)}, u32[]{:S(2)}, u32[]{:S(2)}) collective-permute-start(bf16[128,2304]{1,0:T(8,128)(2,1)S(1)} %fusion.46), channel_id=1, source_target_pairs={{0,1},{1,0},{2,3},{3,2},{4,5},{5,4},{6,7},{7,6},{8,9},{9,8},{10,11... | collective-permute-start | bytes 1769480 | tf_op jit(solution)/shard_map/ppermute | solution.py:75
  663.9 14.5 %collective-permute-start.80 = (bf16[4,2,128,256]{3,2,0,1:T(8,128)(2,1)S(1)}, bf16[4,2,128,256]{3,2,0,1:T(8,128)(2,1)S(1)}, u32[]{:S(2)}, u32[]{:S(2)}) collective-permute-start(bf16[4,2,128,256]{3,2,0,1:T(8,128)(2,1)S(1)} %get-tuple-element.95), channel_id=1, source_target_pairs={{0,8},{8,16},{16,24},{24,28},{28,20},{20,12},{12,4},{4,0},{1,9},{9... | collective-permute-start | bytes 1572872 | tf_op jit(solution)/shard_map/ppermute | solution.py:23
  665.3 15.5 %collective-permute-start.84 = (bf16[4,2,128,256]{3,2,0,1:T(8,128)(2,1)S(1)}, bf16[4,2,128,256]{3,2,0,1:T(8,128)(2,1)S(1)}, u32[]{:S(2)}, u32[]{:S(2)}) collective-permute-start(bf16[4,2,128,256]{3,2,0,1:T(8,128)(2,1)S(1)} %get-tuple-element.96), channel_id=1, source_target_pairs={{0,4},{8,0},{16,8},{24,16},{28,24},{20,28},{12,20},{4,12},{1,5},{9... | collective-permute-start | bytes 1572872 | tf_op jit(solution)/shard_map/ppermute | solution.py:23
  669.6 17.5 %collective-permute-start.104 = (bf16[64,2304]{1,0:T(8,128)(2,1)S(1)}, bf16[64,2304]{1,0:T(8,128)(2,1)S(1)}, u32[]{:S(2)}, u32[]{:S(2)}) collective-permute-start(bf16[64,2304]{1,0:T(8,128)(2,1)S(1)} %add_convert_fusion.2), channel_id=1, source_target_pairs={{0,4},{8,0},{16,8},{24,16},{28,24},{20,28},{12,20},{4,12},{1,5},{9... | collective-permute-start | bytes 884744 | tf_op jit(solution)/shard_map/ppermute | solution.py:23
  673.3 28.0 %collective-permute-start.101 = (bf16[64,2304]{1,0:T(8,128)(2,1)S(1)}, bf16[64,2304]{1,0:T(8,128)(2,1)S(1)}, u32[]{:S(2)}, u32[]{:S(2)}) collective-permute-start(bf16[64,2304]{1,0:T(8,128)(2,1)S(1)} %get-tuple-element.103), channel_id=1, source_target_pairs={{0,8},{8,16},{16,24},{24,28},{28,20},{20,12},{12,4},{4,0},{1,9},{9... | collective-permute-start | bytes 884744 | tf_op jit(solution)/shard_map/ppermute | solution.py:23
  681.2 14.8 %collective-permute-start.81 = (bf16[4,2,128,256]{3,2,0,1:T(8,128)(2,1)S(1)}, bf16[4,2,128,256]{3,2,0,1:T(8,128)(2,1)S(1)}, u32[]{:S(2)}, u32[]{:S(2)}) collective-permute-start(bf16[4,2,128,256]{3,2,0,1:T(8,128)(2,1)S(1)} %get-tuple-element.93), channel_id=1, source_target_pairs={{0,8},{8,16},{16,24},{24,28},{28,20},{20,12},{12,4},{4,0},{1,9},{9... | collective-permute-start | bytes 1572872 | tf_op jit(solution)/shard_map/ppermute | solution.py:23
  683.4 15.0 %collective-permute-start.85 = (bf16[4,2,128,256]{3,2,0,1:T(8,128)(2,1)S(1)}, bf16[4,2,128,256]{3,2,0,1:T(8,128)(2,1)S(1)}, u32[]{:S(2)}, u32[]{:S(2)}) collective-permute-start(bf16[4,2,128,256]{3,2,0,1:T(8,128)(2,1)S(1)} %get-tuple-element.94), channel_id=1, source_target_pairs={{0,4},{8,0},{16,8},{24,16},{28,24},{20,28},{12,20},{4,12},{1,5},{9... | collective-permute-start | bytes 1572872 | tf_op jit(solution)/shard_map/ppermute | solution.py:23
  687.2 17.5 %collective-permute-start.105 = (bf16[64,2304]{1,0:T(8,128)(2,1)S(1)}, bf16[64,2304]{1,0:T(8,128)(2,1)S(1)}, u32[]{:S(2)}, u32[]{:S(2)}) collective-permute-start(bf16[64,2304]{1,0:T(8,128)(2,1)S(1)} %add_convert_fusion.1), channel_id=1, source_target_pairs={{0,4},{8,0},{16,8},{24,16},{28,24},{20,28},{12,20},{4,12},{1,5},{9... | collective-permute-start | bytes 884744 | tf_op jit(solution)/shard_map/ppermute | solution.py:23
  690.5 36.5 %collective-permute-start.90 = (bf16[64,2304]{1,0:T(8,128)(2,1)}, bf16[64,2304]{1,0:T(8,128)(2,1)S(1)}, u32[]{:S(2)}, u32[]{:S(2)}) collective-permute-start(bf16[64,2304]{1,0:T(8,128)(2,1)} %dynamic-slice_convert_fusion.1), channel_id=1, source_target_pairs={{0,8},{8,16},{16,24},{24,28},{28,20},{20,12},{12,4},{4,0},{1,9},{9... | collective-permute-start | bytes 884744 | tf_op jit(solution)/shard_map/ppermute | solution.py:23
  725.2 14.2 %collective-permute-start.89 = (bf16[128,2304]{1,0:T(8,128)(2,1)S(1)}, bf16[128,2304]{1,0:T(8,128)(2,1)S(1)}, u32[]{:S(2)}, u32[]{:S(2)}) collective-permute-start(bf16[128,2304]{1,0:T(8,128)(2,1)S(1)} %fusion.52), channel_id=1, source_target_pairs={{0,2},{1,3},{2,0},{3,1},{4,6},{5,7},{6,4},{7,5},{8,10},{9,11},{10,... | collective-permute-start | bytes 1769480 | tf_op jit(solution)/shard_map/ppermute | solution.py:75
  727.0 13.9 %collective-permute-start.91 = (bf16[128,2304]{1,0:T(8,128)(2,1)S(1)}, bf16[128,2304]{1,0:T(8,128)(2,1)S(1)}, u32[]{:S(2)}, u32[]{:S(2)}) collective-permute-start(bf16[128,2304]{1,0:T(8,128)(2,1)S(1)} %fusion.58), channel_id=1, source_target_pairs={{0,8},{8,16},{16,24},{24,28},{28,20},{20,12},{12,4},{4,0},{1,9},{9... | collective-permute-start | bytes 1769480 | tf_op jit(solution)/shard_map/ppermute | solution.py:23
  731.4 13.6 %collective-permute-start.95 = (bf16[128,2304]{1,0:T(8,128)(2,1)S(1)}, bf16[128,2304]{1,0:T(8,128)(2,1)S(1)}, u32[]{:S(2)}, u32[]{:S(2)}) collective-permute-start(bf16[128,2304]{1,0:T(8,128)(2,1)S(1)} %fusion.61), channel_id=1, source_target_pairs={{0,4},{8,0},{16,8},{24,16},{28,24},{20,28},{12,20},{4,12},{1,5},{9... | collective-permute-start | bytes 1769480 | tf_op jit(solution)/shard_map/ppermute | solution.py:23
  741.1 15.4 %collective-permute-start.92 = (bf16[128,2304]{1,0:T(8,128)(2,1)S(1)}, bf16[128,2304]{1,0:T(8,128)(2,1)S(1)}, u32[]{:S(2)}, u32[]{:S(2)}) collective-permute-start(bf16[128,2304]{1,0:T(8,128)(2,1)S(1)} %fusion.57), channel_id=1, source_target_pairs={{0,8},{8,16},{16,24},{24,28},{28,20},{20,12},{12,4},{4,0},{1,9},{9... | collective-permute-start | bytes 1769480 | tf_op jit(solution)/shard_map/ppermute | solution.py:23
  745.1 25.4 %collective-permute-start.96 = (bf16[128,2304]{1,0:T(8,128)(2,1)S(1)}, bf16[128,2304]{1,0:T(8,128)(2,1)S(1)}, u32[]{:S(2)}, u32[]{:S(2)}) collective-permute-start(bf16[128,2304]{1,0:T(8,128)(2,1)S(1)} %fusion.60), channel_id=1, source_target_pairs={{0,4},{8,0},{16,8},{24,16},{28,24},{20,28},{12,20},{4,12},{1,5},{9... | collective-permute-start | bytes 1769480 | tf_op jit(solution)/shard_map/ppermute | solution.py:23
  756.7 19.2 %collective-permute-start.93 = (bf16[128,2304]{1,0:T(8,128)(2,1)S(1)}, bf16[128,2304]{1,0:T(8,128)(2,1)S(1)}, u32[]{:S(2)}, u32[]{:S(2)}) collective-permute-start(bf16[128,2304]{1,0:T(8,128)(2,1)S(1)} %fusion.56), channel_id=1, source_target_pairs={{0,8},{8,16},{16,24},{24,28},{28,20},{20,12},{12,4},{4,0},{1,9},{9... | collective-permute-start | bytes 1769480 | tf_op jit(solution)/shard_map/ppermute | solution.py:23
  770.6 14.0 %collective-permute-start.97 = (bf16[128,2304]{1,0:T(8,128)(2,1)S(1)}, bf16[128,2304]{1,0:T(8,128)(2,1)S(1)}, u32[]{:S(2)}, u32[]{:S(2)}) collective-permute-start(bf16[128,2304]{1,0:T(8,128)(2,1)S(1)} %fusion.59), channel_id=1, source_target_pairs={{0,4},{8,0},{16,8},{24,16},{28,24},{20,28},{12,20},{4,12},{1,5},{9... | collective-permute-start | bytes 1769480 | tf_op jit(solution)/shard_map/ppermute | solution.py:23
  (147 other events, 1820.2 us)

commit v2 on v1

v2 whole, which is shorter than its diff:
```python
import functools
import math

import jax
import jax.numpy as jnp
from jax import lax
from jax.experimental import pallas as pl
from jax.experimental.pallas import tpu as pltpu
from jax.sharding import PartitionSpec as P

HEAD_DIM = 256
EPS = 1e-06
CAP = 50.0
NEGATIVE = -1e30
BF16 = jnp.bfloat16
F32 = jnp.float32


def ring_order(size):
    return list(range(0, size, 2)) + list(range(size - 1, 0, -2))


def ring_hop(block, step):
    order = ring_order(lax.axis_size("ctx"))
    size = len(order)
    return lax.ppermute(block, "ctx", [(order[i], order[(i + step) % size]) for i in range(size)])


def ring_member(offset):
    size = lax.axis_size("ctx")
    own = lax.axis_index("ctx")
    place = jnp.where(own % 2 == 0, own // 2, size - 1 - own // 2)
    place = (place + offset) % size
    return jnp.where(place < size // 2, 2 * place, 2 * (size - 1 - place) + 1)


def ring_groups():
    half = lax.axis_size("ctx") // 2
    return [[0]] + [[-k, k] for k in range(1, half)] + [[half]]


def tie(*values):
    return lax.optimization_barrier(values)


def ring_gather(own, use, side=None, state=(), first=()):
    half = lax.axis_size("ctx") // 2
    middle = own.shape[0] // 2
    own, state, result = tie(own, state, first)
    blocks, results = [own], []
    behind = ahead = own
    for i in range(half):
        last = i == half - 1
        if last:
            moved = [ring_hop(behind[:middle], 1), ring_hop(ahead[middle:], -1)]
        else:
            moved = [ring_hop(behind, 1), ring_hop(ahead, -1)]
        result = use(i, blocks, result)
        if side:
            state = side(i, state)
        moved, result, state = tie(moved, result, state)
        results.append(result)
        if not last:
            blocks = behind, ahead = moved
    results.append(use(half, moved, result))
    return (results, state) if side else results


def add_terms(terms, moved):
    to_behind, to_ahead = terms
    behind, ahead = (block.astype(F32) for block in moved)
    if behind.shape != to_ahead.shape:
        gap = jnp.zeros_like(behind)
        behind = jnp.concatenate([behind, gap], axis=0)
        ahead = jnp.concatenate([gap, ahead], axis=0)
    return [
        (to_ahead.astype(F32) + behind).astype(BF16),
        (to_behind.astype(F32) + ahead).astype(BF16),
    ]


def ring_scatter(term, operands, side=None, state=(), join=add_terms):
    half = lax.axis_size("ctx") // 2
    far = term(half, operands[half])
    if len(far) == 1:
        middle = far[0].shape[0] // 2
        far = [far[0][:middle], far[0][middle:]]
    sums = [part.astype(BF16) for part in far]
    for i in range(half - 1, -1, -1):
        sums, operand, state = tie(sums, operands[i], state)
        moved = [ring_hop(sums[0], 1), ring_hop(sums[1], -1)]
        terms = term(i, operand)
        if side:
            state = side(i, state)
        moved, terms, state = tie(moved, terms, state)
        if i > 0:
            sums = join(terms, moved)
    return (terms[0], *moved), state


def far_hop(block):
    size = lax.axis_size("fsdp")
    return lax.ppermute(block, "fsdp", [(i, i ^ (size // 2)) for i in range(size)])


def near_hop(block):
    size = lax.axis_size("fsdp")
    return lax.ppermute(block, "fsdp", [(i, i ^ 1) for i in range(size)])


def add_from(block, axis, masks):
    size = lax.axis_size(axis)
    routes = [[(i, i ^ mask) for i in range(size)] for mask in masks if mask < size]
    return sum((lax.ppermute(block, axis, route) for route in routes), block)


def low_masks():
    return range(1, 4)


def high_masks():
    return range(4, lax.axis_size("ctx"), 4)


def rms_norm(values, gain):
    return values * lax.rsqrt(jnp.mean(values * values, axis=-1, keepdims=True) + EPS) * gain


def norm_back(values, gain, cotangent):
    scale = lax.rsqrt(jnp.mean(values * values, axis=-1, keepdims=True) + EPS)
    normal = values * scale
    turned = cotangent * gain
    along = jnp.mean(turned * normal, axis=-1, keepdims=True)
    return scale * (turned - normal * along), jnp.sum(cotangent * normal, axis=0)


def rotate(values, cosine, sine):
    middle = values.shape[-1] // 2
    first = values[..., :middle]
    second = values[..., middle:]
    return jnp.concatenate(
        [first * cosine - second * sine, second * cosine + first * sine], axis=-1
    )


def dot(a, b, dims):
    return lax.dot_general(a, b, (dims, ((), ())), preferred_element_type=F32)


def nn(a, b):
    return dot(a, b, ((1,), (0,)))


def nt(a, b):
    return dot(a, b, ((1,), (1,)))


def tn(a, b):
    return dot(a, b, ((0,), (0,)))


def gelu_parts(gate):
    slope = math.sqrt(2.0 / math.pi)
    square = gate * gate
    tanh = jnp.tanh(slope * gate * (1.0 + 0.044715 * square))
    value = 0.5 * gate * (1.0 + tanh)
    inner = slope * (1.0 + 3.0 * 0.044715 * square)
    return value, 0.5 * (1.0 + tanh) + 0.5 * gate * (1.0 - tanh * tanh) * inner


def normed(values):
    scale = lax.rsqrt(jnp.mean(values * values, axis=-1, keepdims=True) + EPS)
    return values * scale, scale


def pulled(values, gain, cotangent):
    normal, scale = normed(values)
    through = cotangent * gain
    along = jnp.mean(through * normal, axis=-1, keepdims=True)
    return scale * (through - normal * along), jnp.sum(cotangent * normal, axis=0, keepdims=True)


def middle_kernel(rows_ref, kept_ref, moved_ref, gain_two_ref, gain_three_ref, *outs):
    attn_out_ref, resid_ref, normed_two_ref = outs
    attn_out = kept_ref[...] + moved_ref[...].astype(F32)
    resid = rows_ref[...].astype(F32) + normed(attn_out)[0] * gain_two_ref[...]
    attn_out_ref[...] = attn_out
    resid_ref[...] = resid
    normed_two_ref[...] = (normed(resid)[0] * gain_three_ref[...]).astype(BF16)


def end_kernel(term_ref, behind_ref, ahead_ref, resid_ref, grad_ref, gain_ref, *outs):
    block_out_ref, d_mlp_ref, grad_gain_ref = outs
    mlp_out = term_ref[...] + (behind_ref[...].astype(F32) + ahead_ref[...].astype(F32))
    block_out_ref[...] = (resid_ref[...] + normed(mlp_out)[0] * gain_ref[...]).astype(BF16)
    d_mlp, grad_gain_ref[...] = pulled(mlp_out, gain_ref[...], grad_ref[...].astype(F32))
    d_mlp_ref[...] = d_mlp.astype(BF16)


def back_kernel(
    term_ref,
    behind_ref,
    ahead_ref,
    resid_ref,
    attn_out_ref,
    grad_ref,
    gain_two_ref,
    gain_three_ref,
    d_resid_ref,
    d_attn_ref,
    grad_two_ref,
    grad_three_ref,
):
    d_normed = term_ref[...] + (behind_ref[...].astype(F32) + ahead_ref[...].astype(F32))
    d_rows, grad_three_ref[...] = pulled(resid_ref[...], gain_three_ref[...], d_normed)
    d_resid = grad_ref[...].astype(F32) + d_rows
    d_resid_ref[...] = d_resid
    d_attn, grad_two_ref[...] = pulled(attn_out_ref[...], gain_two_ref[...], d_resid)
    d_attn_ref[...] = d_attn.astype(BF16)


def by_rows_call(kernel, args, outs):
    return pl.pallas_call(
        kernel,
        out_shape=[jax.ShapeDtypeStruct(*out) for out in outs],
        compiler_params=pltpu.CompilerParams(vmem_limit_bytes=24 << 20),
        cost_estimate=FREE,
    )(*args)


def input_kernel(seqs, refs_in, refs_w, rows_ref, scale_ref, kept_ref, sent_ref, gain_ref):
    total = sum(nn(d[...], w[...]) for d, w in zip(refs_in, refs_w))
    half = total.shape[0] // 2
    kept_ref[...] = total[:half]
    sent_ref[...] = total[half:].astype(BF16)
    normal = rows_ref[...].astype(F32) * scale_ref[...]
    gain_ref[...] = jnp.sum(total * normal, axis=0, keepdims=True)


def input_terms(ds, weights, rows, scale):
    count, width = rows.shape
    half = count // 2
    tile = tile_of(width, 768)

    def kernel(*refs):
        input_kernel(0, refs[:3], refs[3:6], *refs[6:])

    by_cols = lambda i: (0, i)
    return pl.pallas_call(
        kernel,
        grid=(width // tile,),
        out_shape=[
            jax.ShapeDtypeStruct((half, width), F32),
            jax.ShapeDtypeStruct((half, width), BF16),
            jax.ShapeDtypeStruct((1, width), F32),
        ],
        in_specs=[pl.BlockSpec(d.shape, lambda i: (0, 0)) for d in ds]
        + [pl.BlockSpec((w.shape[0], tile), by_cols) for w in weights]
        + [pl.BlockSpec((count, tile), by_cols), pl.BlockSpec((count, 1), lambda i: (0, 0))],
        out_specs=[
            pl.BlockSpec((half, tile), by_cols),
            pl.BlockSpec((half, tile), by_cols),
            pl.BlockSpec((1, tile), by_cols),
        ],
        compiler_params=ROOMY,
        cost_estimate=FREE,
    )(*ds, *weights, rows, scale)


def stacked(flat):
    heads = flat.shape[1] // HEAD_DIM
    return jnp.concatenate(
        [flat[:, h * HEAD_DIM : (h + 1) * HEAD_DIM] for h in range(heads)], axis=0
    )


def side_by_side(tall, rows):
    return jnp.concatenate(
        [tall[i : i + rows] for i in range(0, tall.shape[0], rows)], axis=1
    )


FREE = pl.CostEstimate(flops=0, bytes_accessed=0, transcendentals=0)
ROOMY = pltpu.CompilerParams(vmem_limit_bytes=56 << 20)


def blank(shapes):
    return pl.pallas_call(
        lambda *refs: None,
        out_shape=[jax.ShapeDtypeStruct(shape, BF16) for shape in shapes],
        out_specs=[pl.BlockSpec(memory_space=pl.ANY)] * len(shapes),
    )()


def place_kernel(cols, n_blocks, members_ref, *refs):
    blocks, outs = refs[:n_blocks], refs[n_blocks + len(cols) :]

    for n, block in enumerate(blocks):

        @pl.when(pl.program_id(0) == n)
        def _(block=block):
            start = 0
            for out, count in zip(outs, cols):
                out[...] = block[start : start + count]
                start += count


def place_rows(fulls, blocks, members, cols):
    width = blocks[0].shape[1]
    if any(count % 16 for count in cols):
        for block, member in zip(blocks, members):
            start = 0
            for m, count in enumerate(cols):
                part = block[start : start + count]
                fulls[m] = lax.dynamic_update_slice_in_dim(fulls[m], part, member * count, axis=0)
                start += count
        return fulls
    n_blocks = len(blocks)
    return pl.pallas_call(
        functools.partial(place_kernel, cols, n_blocks),
        grid_spec=pltpu.PrefetchScalarGridSpec(
            num_scalar_prefetch=1,
            grid=(n_blocks,),
            in_specs=[pl.BlockSpec(block.shape, lambda i, m: (0, 0)) for block in blocks]
            + [pl.BlockSpec(memory_space=pl.ANY)] * len(fulls),
            out_specs=[pl.BlockSpec((count, width), lambda i, m: (m[i], 0)) for count in cols],
        ),
        out_shape=[jax.ShapeDtypeStruct(full.shape, full.dtype) for full in fulls],
        input_output_aliases={1 + n_blocks + m: m for m in range(len(fulls))},
        cost_estimate=FREE,
    )(jnp.stack(members), *blocks, *fulls)


def put_kernel(n_blocks, *refs):
    for n in range(n_blocks):

        @pl.when(pl.program_id(0) == n)
        def _(n=n):
            refs[-1][...] = refs[n][...]


def put_blocks(full, blocks, at, along):
    shape = blocks[0].shape
    where = (lambda i: (i, at, 0)) if along == 0 else (lambda i: (0, at + i, 0))
    return pl.pallas_call(
        functools.partial(put_kernel, len(blocks)),
        grid=(len(blocks),),
        out_shape=jax.ShapeDtypeStruct(full.shape, full.dtype),
        in_specs=[pl.BlockSpec(shape, lambda i: (0, 0, 0))] * len(blocks)
        + [pl.BlockSpec(memory_space=pl.ANY)],
        out_specs=pl.BlockSpec(shape, where),
        input_output_aliases={len(blocks): 0},
        cost_estimate=FREE,
    )(*blocks, full)


def tile_of(count, tile):
    return tile if count % tile == 0 else count


def stack_rows(refs):
    return jnp.concatenate([ref[...] for ref in refs], axis=0) if len(refs) > 1 else refs[0][...]


def weight_grad_kernel(groups, blocks, *refs):
    units, rows, out_ref, all_rows = refs[:groups], refs[groups : groups + blocks], refs[-2], refs[-1]

    @pl.when(pl.program_id(0) == 0)
    def _():
        at = 0
        for row in rows:
            all_rows[at : at + row.shape[0]] = row[...]
            at += row.shape[0]

    out_ref[...] = tn(stack_rows(units), all_rows[...]).astype(BF16)


def weight_grad(units, rows, part=None):
    count, width = units[0].shape[1], rows[0].shape[1]
    total = sum(row.shape[0] for row in rows)
    tile = tile_of(count, 384)
    first, tiles, before = part or (0, count // tile, None)
    first, tiles = min(first, count // tile - 1), min(tiles, count // tile)
    held = [] if before is None else [before]
    return pl.pallas_call(
        functools.partial(weight_grad_kernel, len(units), len(rows)),
        grid=(tiles,),
        out_shape=jax.ShapeDtypeStruct((count, width), BF16),
        in_specs=[pl.BlockSpec((unit.shape[0], tile), lambda i: (0, first + i)) for unit in units]
        + [pl.BlockSpec(row.shape, lambda i: (0, 0)) for row in rows]
        + [pl.BlockSpec(memory_space=pl.ANY)] * len(held),
        out_specs=pl.BlockSpec((tile, width), lambda i: (first + i, 0)),
        scratch_shapes=[pltpu.VMEM((total, width), BF16)],
        input_output_aliases={len(units) + len(rows): 0} if held else {},
        compiler_params=ROOMY,
        cost_estimate=FREE,
    )(*units, *rows, *held)


def expand_kernel(blocks, *refs):
    rows = stack_rows(refs[:blocks])
    gate_ref, up_ref, value_ref, slope_ref, hidden_ref = refs[blocks:]
    gate, up = nt(rows, gate_ref[0]), nt(rows, up_ref[0])
    value, slope = gelu_parts(gate)
    value_ref[...] = value
    slope_ref[...] = up * slope
    hidden_ref[...] = (value * up).astype(BF16)


def contract_kernel(blocks, *refs):
    rows = stack_rows(refs[:blocks])
    down_ref, value_ref, slope_ref, d_gate_ref, d_up_ref = refs[blocks:]
    d_hidden = nt(rows, down_ref[...])
    d_gate_ref[...] = (d_hidden * slope_ref[...]).astype(BF16)
    d_up_ref[...] = (d_hidden * value_ref[...]).astype(BF16)


def unit_call(kernel, rows, weights, units, outs):
    count, width = weights[0][0].shape[-2:]
    total = sum(row.shape[0] for row in rows)
    tile = tile_of(count, 384)
    weight_specs = [
        pl.BlockSpec((1,) * len(at) + (tile, width), lambda i, at=at: (*at, i, 0))
        for _, at in weights
    ]
    flat = pl.BlockSpec((total, tile), lambda i: (0, i))
    return pl.pallas_call(
        functools.partial(kernel, len(rows)),
        grid=(count // tile,),
        out_shape=[jax.ShapeDtypeStruct((total, count), out) for out in outs],
        in_specs=[pl.BlockSpec(row.shape, lambda i: (0, 0)) for row in rows]
        + weight_specs
        + [flat] * len(units),
        out_specs=[flat] * len(outs),
        compiler_params=pltpu.CompilerParams(vmem_limit_bytes=24 << 20),
        cost_estimate=FREE,
    )(*rows, *(weight for weight, _ in weights), *units)


def out_kernel(*refs):
    ins, weights, out_ref = refs[: len(refs) // 2], refs[len(refs) // 2 : -1], refs[-1]
    total = sum(nn(a[...], w[...].reshape(w.shape[-2:])) for a, w in zip(ins, weights))
    out_ref[...] = total.astype(out_ref.dtype)


def out_call(ins, weights, rows, at, out):
    count, width = weights[0][0].shape[-2:]
    tile = tile_of(width, 768)
    return pl.pallas_call(
        out_kernel,
        grid=(width // tile,),
        out_shape=jax.ShapeDtypeStruct((rows, width), out),
        in_specs=[pl.BlockSpec((rows, count), lambda i: (at, 0))] * len(ins)
        + [
            pl.BlockSpec((1,) * len(lead) + (count, tile), lambda i, lead=lead: (*lead, 0, i))
            for _, lead in weights
        ],
        out_specs=pl.BlockSpec((rows, tile), lambda i: (0, i)),
        compiler_params=pltpu.CompilerParams(vmem_limit_bytes=24 << 20),
        cost_estimate=FREE,
    )(*ins, *(weight for weight, _ in weights))


def gather_kernel(counts, *refs):
    ins, outs = refs[len(counts) : -len(counts)], refs[-len(counts) :]
    for out, cols in zip(outs, counts):
        start = 0
        for count in cols:
            out[start : start + count] = ins[0][...].astype(out.dtype)
            start += count
            ins = ins[1:]


def member_rows(parts, dtype):
    width = parts[0][0][0].shape[1]
    counts = [cols for _, cols, _ in parts]
    if any(count % 16 for cols in counts for count in cols):
        return [
            jnp.concatenate(
                [
                    lax.dynamic_slice_in_dim(full, member * c, c, axis=0)
                    for full, c in zip(arrays, cols)
                ],
                axis=0,
            ).astype(dtype)
            for arrays, cols, member in parts
        ]
    return pl.pallas_call(
        functools.partial(gather_kernel, counts),
        grid_spec=pltpu.PrefetchScalarGridSpec(
            num_scalar_prefetch=len(parts),
            grid=(1,),
            in_specs=[
                pl.BlockSpec((count, width), lambda i, *m, side=side: (m[side][0], 0))
                for side, cols in enumerate(counts)
                for count in cols
            ],
            out_specs=[pl.BlockSpec((sum(cols), width), lambda i, *m: (0, 0)) for cols in counts],
        ),
        out_shape=[jax.ShapeDtypeStruct((sum(cols), width), dtype) for cols in counts],
        compiler_params=ROOMY,
        cost_estimate=FREE,
    )(
        *(member.reshape(1) for _, _, member in parts),
        *(array for arrays, _, _ in parts for array in arrays),
    )


def keys_back_kernel(term_ref, behind_ref, ahead_ref, cosine_ref, sine_ref, rows_ref, *outs):
    d_keys_ref, d_values_ref, grad_keys_ref, grad_values_ref = outs
    total = term_ref[...].astype(F32) + (
        behind_ref[...].astype(F32) + ahead_ref[...].astype(F32)
    )
    d_keys = rotate(total[0], cosine_ref[...], -sine_ref[...]).astype(BF16)
    d_keys = d_keys.reshape(-1, HEAD_DIM)
    d_values = total[1].astype(BF16).reshape(-1, HEAD_DIM)
    d_keys_ref[...] = d_keys
    d_values_ref[...] = d_values
    grad_keys_ref[...] = tn(d_keys, rows_ref[...]).astype(BF16)
    grad_values_ref[...] = tn(d_values, rows_ref[...]).astype(BF16)


def keys_back(parts, cosine, sine, rows):
    count, width = rows.shape
    tile = tile_of(width, 768)
    whole = pl.BlockSpec(parts[0].shape, lambda i: (0, 0, 0, 0))
    flat = pl.BlockSpec((count, HEAD_DIM), lambda i: (0, 0))
    angle = pl.BlockSpec(cosine.shape, lambda i: (0, 0))
    tall = pl.BlockSpec((HEAD_DIM, tile), lambda i: (0, i))
    return pl.pallas_call(
        keys_back_kernel,
        grid=(width // tile,),
        out_shape=[jax.ShapeDtypeStruct((count, HEAD_DIM), BF16)] * 2
        + [jax.ShapeDtypeStruct((HEAD_DIM, width), BF16)] * 2,
        in_specs=[whole] * 3 + [angle] * 2 + [pl.BlockSpec((count, tile), lambda i: (0, i))],
        out_specs=[flat] * 2 + [tall] * 2,
        compiler_params=ROOMY,
        cost_estimate=FREE,
    )(*parts, cosine, sine, rows)


def turned(raw, cosine, sine):
    return jnp.concatenate(
        [
            rotate(raw[:, at : at + HEAD_DIM], cosine, sine)
            for at in range(0, raw.shape[1], HEAD_DIM)
        ],
        axis=1,
    )


def queries_kernel(rows_ref, weight_ref, cosine_ref, sine_ref, out_ref):
    raw = nt(rows_ref[...], weight_ref[...])
    out_ref[...] = (turned(raw, cosine_ref[...], sine_ref[...]) * HEAD_DIM ** (-0.5)).astype(BF16)


def keys_kernel(rows_ref, key_ref, value_ref, cosine_ref, sine_ref, out_ref):
    rows = rows_ref[...]
    out_ref[0, 0] = rotate(nt(rows, key_ref[...]), cosine_ref[...], sine_ref[...]).astype(BF16)
    out_ref[1, 0] = nt(rows, value_ref[...]).astype(BF16)


def project(kernel, rows, weights, cosine, sine, out, out_spec):
    tokens, width = cosine.shape[0], rows.shape[1]

    def whole(array):
        return pl.BlockSpec(array.shape, lambda i: (0, 0))

    return pl.pallas_call(
        kernel,
        grid=(rows.shape[0] // tokens,),
        out_shape=jax.ShapeDtypeStruct(out, BF16),
        in_specs=[pl.BlockSpec((tokens, width), lambda i: (i, 0))]
        + [whole(array) for array in (*weights, cosine, sine)],
        out_specs=out_spec,
        compiler_params=pltpu.CompilerParams(vmem_limit_bytes=16 << 20),
        cost_estimate=FREE,
    )(rows, *weights, cosine, sine)


def attend_kernel(keys_ref, values_ref, queries_ref, query_pos_ref, key_pos_ref, mixed_ref):
    queries = stacked(queries_ref[...])
    tanh = jnp.tanh(nt(queries, keys_ref[0]) * (1.0 / CAP))
    weights = jnp.where(key_pos_ref[...] <= query_pos_ref[...], jnp.exp(CAP * tanh), 0.0)
    total = jnp.sum(weights, axis=1, keepdims=True)
    mixed = nn(weights.astype(BF16), values_ref[0]) / total
    mixed_ref[...] = side_by_side(mixed.astype(BF16), queries_ref.shape[0])


def attend_back_kernel(
    keys_ref,
    values_ref,
    queries_ref,
    d_attn_ref,
    d_attn_next_ref,
    output_ref,
    query_pos_ref,
    key_pos_ref,
    cosine_ref,
    sine_ref,
    *refs,
):
    blocks = key_pos_ref.shape[0] // queries_ref.shape[0]
    d_queries_ref, *d_both_refs = refs[-blocks - 2 :]
    rows = queries_ref.shape[0]
    queries = stacked(queries_ref[...])
    d_attn = jnp.where(pl.program_id(0) == 0, d_attn_ref[...], d_attn_next_ref[...])
    d_mixed = stacked(nt(d_attn, output_ref[...]).astype(BF16))
    keys = keys_ref[0]
    tanh = jnp.tanh(nt(keys, queries) * (1.0 / CAP))
    weights = jnp.where(key_pos_ref[...] <= query_pos_ref[...], jnp.exp(CAP * tanh), 0.0)
    probs = weights * (1.0 / jnp.sum(weights, axis=0, keepdims=True))
    d_values = nn(probs.astype(BF16), d_mixed).astype(BF16)
    for n, out in enumerate(d_both_refs[:-2]):
        out[1, 0] = d_values[n * rows : (n + 1) * rows]
    d_both_refs[-1][0, 0] = d_values[(blocks - 1) * rows :]
    d_probs = nt(values_ref[0], d_mixed)
    delta = jnp.sum(probs * d_probs, axis=0, keepdims=True)
    d_scores = (probs * (d_probs - delta) * (1.0 - tanh * tanh)).astype(BF16)
    d_keys = nn(d_scores, queries).astype(BF16)
    for n, out in enumerate(d_both_refs[:-2]):
        out[0, 0] = d_keys[n * rows : (n + 1) * rows]
    d_both_refs[-2][0, 0] = d_keys[(blocks - 1) * rows :]
    d_queries = tn(d_scores, keys) * HEAD_DIM ** (-0.5)
    d_queries = rotate(d_queries, cosine_ref[...], -sine_ref[...])
    d_queries_ref[...] = side_by_side(d_queries.astype(BF16), rows)


def attention_call(kernel, both, seqs, at, outs, args, specs, out_specs, earlier=()):
    count = both.shape[1]
    total = both.shape[0] // 2
    held = len(args) + 2
    return pl.pallas_call(
        kernel,
        grid=(seqs,),
        out_shape=[jax.ShapeDtypeStruct(*out) for out in outs],
        in_specs=[
            pl.BlockSpec((1, count, HEAD_DIM), lambda i: (at(i), 0, 0)),
            pl.BlockSpec((1, count, HEAD_DIM), lambda i: (at(i) + total, 0, 0)),
        ]
        + specs
        + [pl.BlockSpec(memory_space=pl.ANY)] * len(earlier),
        out_specs=out_specs,
        input_output_aliases={held + n: n for n in range(len(earlier))},
        compiler_params=ROOMY,
        cost_estimate=FREE,
    )(both, both, *args, *earlier)


def body(
    block_in,
    stretch_order,
    weight_query,
    weight_key,
    weight_value,
    weight_output,
    weight_gate,
    weight_up,
    weight_down,
    gain_preattn,
    gain_postattn,
    gain_premlp,
    gain_postmlp,
    grad_out,
):
    n_ctx, n_fsdp = lax.axis_size("ctx"), lax.axis_size("fsdp")
    own_ctx, own_fsdp = lax.axis_index("ctx"), lax.axis_index("fsdp")
    rows_in = block_in[0].astype(F32)
    tokens, width = rows_in.shape
    half = tokens // 2
    half_ring = n_ctx // 2
    groups = ring_groups()
    members = [[ring_member(k) for k in group] for group in groups]

    steps = jnp.arange(HEAD_DIM // 2, dtype=F32)
    inverse = jnp.exp(steps * (-2.0 * math.log(10000.0) / HEAD_DIM))

    def positions(member):
        starts = lax.dynamic_slice_in_dim(stretch_order, member, 1, axis=0)[0]
        return (starts[:, None] * half + jnp.arange(half, dtype=jnp.int32)[None, :]).reshape(-1)

    query_pos = positions(own_ctx)
    key_pos = [jnp.concatenate([positions(m) for m in group]) for group in members]
    angle = query_pos.astype(F32)[:, None] * inverse[None, :]
    cosine, sine = jnp.cos(angle), jnp.sin(angle)

    gains = jnp.stack([gain_preattn, gain_postattn, gain_premlp, gain_postmlp])
    share = gains.shape[1]
    own_place = (own_ctx * n_fsdp + own_fsdp) * share
    gains = lax.dynamic_update_slice_in_dim(jnp.zeros((4, width), F32), gains, own_place, axis=1)

    cols = [weight_query.shape[1], weight_key.shape[1], weight_value.shape[1]]
    cols.append(weight_output.shape[0])
    cuts = [sum(cols[:i]) for i in range(len(cols) + 1)]
    own = jnp.concatenate([weight_query.T, weight_key.T, weight_value.T, weight_output], axis=0)

    def place_blocks(i, blocks, placed):
        if i == half_ring:
            member = [ring_member(i)]
            return [
                part
                for n, block in enumerate(blocks)
                for part in place_rows(placed[2 * n : 2 * n + 2], [block], member, cols[2 * n : 2 * n + 2])
            ]
        ends = [i] if i == 0 else [-i, i]
        return list(place_rows(list(placed), list(blocks), [ring_member(k) for k in ends], cols))

    flying = {}

    def prepare(i, state):
        if i == 0:
            gate_own, up_own = state
            rows = [block_in[0], far_hop(block_in[0]), near_hop(block_in[0])]
            own = jnp.stack([gate_own.T, up_own.T])
            return rows, add_from(gains, "fsdp", low_masks()), own
        if i == 1:
            rows, sums, own = state
            flying["gate_up"] = lax.all_gather(own, "fsdp", axis=1, tiled=True)
            rows = [*rows, near_hop(rows[1])]
            return rows, add_from(sums, "ctx", low_masks())
        if i == 2:
            rows, sums = state
            return jnp.concatenate(rows, axis=0), add_from(sums, "ctx", high_masks())
        if i == half_ring - 1:
            rows, sums = state
            long = rows.astype(F32)
            scales = lax.rsqrt(jnp.mean(long * long, axis=-1, keepdims=True) + EPS)
            return rows, scales, (long * scales * sums[0]).astype(BF16), sums
        return state

    results, (all_rows, scales, normed_one, gains) = ring_gather(
        own,
        place_blocks,
        prepare,
        (weight_gate, weight_up),
        blank([(c * n_ctx, width) for c in cols]),
    )
    query_full, key_full, value_full, output_full = results[-1]
    gain_one, gain_two, gain_three, gain_four = gains[0], gains[1], gains[2], gains[3]

    seqs = n_fsdp
    group = query_full.shape[0] // HEAD_DIM

    by_rows = pl.BlockSpec((tokens, group * HEAD_DIM), lambda i: (i, 0))
    both_own = project(
        keys_kernel,
        normed_one,
        [key_full, value_full],
        cosine,
        sine,
        (2, seqs, tokens, HEAD_DIM),
        pl.BlockSpec((2, 1, tokens, HEAD_DIM), lambda i: (0, i, 0, 0)),
    ).reshape(2 * seqs, tokens, HEAD_DIM)

    def take_keys(i, blocks, both):
        return put_blocks(both, list(blocks), max(2 * i - 1, 0), 0 if i == half_ring else 1)

    def keys_side(i, state):
        if i == 0:
            return project(
                queries_kernel,
                normed_one,
                [query_full],
                cosine,
                sine,
                (seqs * tokens, group * HEAD_DIM),
                by_rows,
            )
        if i == 1:
            return state, flying.pop("gate_up"), weight_down
        if i == 2:
            queries, gate_up, own = state
            flying["down"] = lax.all_gather(own, "fsdp", axis=0, tiled=True)
            return queries, gate_up
        return state

    count = tokens * n_ctx
    results, (queries, gate_up) = ring_gather(
        both_own,
        take_keys,
        keys_side,
        (),
        blank([(2 * seqs, count, HEAD_DIM)])[0],
    )
    both = results[-1]
    rows_pos = jnp.tile(query_pos, group)
    key_pos = jnp.concatenate(key_pos)
    def fixed(*shape):
        return pl.BlockSpec(shape, lambda i: (0, 0))

    (mixed,) = attention_call(
        attend_kernel,
        both,
        seqs,
        lambda i: i,
        [(queries.shape, BF16)],
        [queries, rows_pos[:, None], key_pos[None, :]],
        [by_rows, fixed(group * tokens, 1), fixed(1, count)],
        [by_rows],
    )

    def by_seq(flat):
        return [flat[i * tokens : (i + 1) * tokens] for i in range(seqs)]

    def fold(terms):
        moved = near_hop(jnp.stack([term.astype(BF16) for term in terms[2:]]))
        return terms[0] + moved[0].astype(F32), (terms[1] + moved[1].astype(F32)).astype(BF16)

    kept, sent = fold(by_seq(nn(mixed, output_full)))
    row = (tokens, width)
    gain_rows = [gain[None, :] for gain in (gain_two, gain_three, gain_four)]
    attn_out, resid, normed_two_own = by_rows_call(
        middle_kernel,
        [block_in[0], kept, far_hop(sent), *gain_rows[:2]],
        [(row, F32), (row, F32), (row, BF16)],
    )

    gate_weight, up_weight = (gate_up, (0,)), (gate_up, (1,))

    def expand(i, blocks, last):
        weights = [gate_weight, up_weight]
        return unit_call(expand_kernel, blocks, weights, [], [F32, F32, BF16]), list(blocks)

    def finish_down(i, state):
        return flying.pop("down") if i == 0 else state

    results, down_full = ring_gather(normed_two_own, expand, finish_down)
    values_act, slopes_act, hidden = zip(*(parts for parts, _ in results))
    normed_two = [block for _, blocks in results for block in blocks]

    def apart(flat):
        return [flat[n : n + tokens] for n in range(0, flat.shape[0], tokens)]

    def down_term(i, hidden_part):
        out = BF16 if i else F32
        return apart(out_call([hidden_part], [(down_full, ())], hidden_part.shape[0], 0, out))

    mlp_parts, _ = ring_scatter(down_term, hidden)

    block_out, d_mlp_own, grad_four = by_rows_call(
        end_kernel,
        [*mlp_parts, resid, grad_out[0], gain_rows[2]],
        [(row, BF16), (row, BF16), ((1, width), F32)],
    )

    def contract(i, blocks, last):
        return unit_call(
            contract_kernel,
            blocks,
            [(down_full, ())],
            [values_act[i], slopes_act[i]],
            [BF16, BF16],
        ), list(blocks)

    results = ring_gather(d_mlp_own, contract)
    d_gate, d_up = zip(*(grads for grads, _ in results))
    d_mlp = [block for _, blocks in results for block in blocks]

    def to_owner(full):
        return lax.psum_scatter(full, "fsdp", scatter_dimension=0, tiled=True)

    def grad_up_work(i, state):
        if i == half_ring - 2:
            return state, weight_grad(*state, (0, 2, None))
        if i == half_ring - 3:
            return weight_grad(*state[0], (2, 1, state[1]))
        return state

    def rows_term(i, grads):
        out = BF16 if i else F32
        return apart(out_call(grads, [gate_weight, up_weight], grads[0].shape[0], 0, out))

    d_normed_parts, grad_up_full = ring_scatter(
        rows_term,
        list(zip(d_gate, d_up)),
        grad_up_work,
        (d_up, normed_two),
    )
    d_resid, d_attn_own, grad_two, grad_three = by_rows_call(
        back_kernel,
        [*d_normed_parts, resid, attn_out, grad_out[0], *gain_rows[:2]],
        [(row, F32), (row, BF16), ((1, width), F32), ((1, width), F32)],
    )
    cosines, sines = jnp.tile(cosine, (group, 1)), jnp.tile(sine, (group, 1))
    angles = fixed(group * tokens, HEAD_DIM // 2)
    pair = (2, seqs, tokens, HEAD_DIM)

    def attend_back(chip, d_attn, earlier):
        def at(i):
            return 2 * i + chip

        def half_of(first):
            return pl.BlockSpec((first, 1, tokens, HEAD_DIM), lambda i: (0, at(i), 0, 0))

        by_seq_rows = pl.BlockSpec((tokens, group * HEAD_DIM), lambda i: (at(i), 0))
        return attention_call(
            attend_back_kernel,
            both,
            2,
            at,
            [(queries.shape, BF16)] + [(pair, BF16)] * (n_ctx - 1) + [((1, *pair[1:]), BF16)] * 2,
            [queries, *d_attn, output_full, rows_pos[None, :], key_pos[:, None], cosines, sines],
            [by_seq_rows, fixed(tokens, width), fixed(tokens, width)]
            + [fixed(*output_full.shape), fixed(1, group * tokens), fixed(count, 1)]
            + [angles, angles],
            [by_seq_rows] + [half_of(2)] * (n_ctx - 1) + [half_of(1)] * 2,
            earlier,
        )

    d_attn_far, d_attn_near = far_hop(d_attn_own), near_hop(d_attn_own)
    earlier = attend_back(0, [d_attn_own, d_attn_near], ())
    d_attn_far, earlier, grad_up_full = tie(d_attn_far, earlier, grad_up_full)
    flying["up"] = to_owner(grad_up_full)
    d_attn_last = near_hop(d_attn_far)
    d_query_raw, *d_both = attend_back(1, [d_attn_far, d_attn_last], earlier)
    d_attn = jnp.concatenate([d_attn_own, d_attn_far, d_attn_near, d_attn_last], axis=0)

    def both_of(distance):
        at = max(2 * distance - 1, 0)
        return d_both[at : at + (1 if distance == 0 else 2)]

    def query_work(i, state):
        if i == half_ring - 2:
            return weight_grad(*state[0]), *state[1:]
        if i == half_ring - 3:
            flying["gate"] = to_owner(state[0])
            return weight_grad(*state[1])
        if i == 0:
            flying["down"] = to_owner(state)
            return (
                flying.pop("up"),
                tn(d_query_raw, normed_one).astype(BF16),
                tn(mixed, d_attn).astype(BF16),
            )
        return state

    d_both, state = ring_scatter(
        lambda i, blocks: blocks,
        [both_of(distance) for distance in range(half_ring + 1)],
        query_work,
        ((d_gate, normed_two), (hidden, d_mlp)),
    )
    grad_up, grad_query_full, grad_output_full = state
    d_key_raw, d_value_raw, grad_key_full, grad_value_full = keys_back(
        d_both, cosine, sine, normed_one
    )
    grad_fulls = [grad_query_full, grad_key_full, grad_value_full, grad_output_full]

    def weight_terms(i, fulls):
        if i == half_ring:
            member = ring_member(i)
            return member_rows([(fulls[:2], cols[:2], member), (fulls[2:], cols[2:], member)], BF16)
        ends = [0] if i == 0 else [-i, i]
        return member_rows([(fulls, cols, ring_member(k)) for k in ends], BF16)

    def input_side(i, state):
        if i == half_ring - 1:
            ds, up = state
            kept, sent, grad_one = input_terms(
                ds, [query_full, key_full, value_full], all_rows, scales
            )
            return kept, sent, jnp.concatenate([grad_one, grad_two, grad_three, grad_four], axis=0), up
        if i == half_ring - 2:
            kept, sent, sums, up = state
            sums = add_from(sums, "fsdp", low_masks())
            return kept, near_hop(sent), sums, up.T.astype(F32), flying.pop("gate")
        if i == half_ring - 3:
            kept, near, sums, up, gate = state
            total = kept + near.astype(F32)
            arrived = far_hop(total[tokens:].astype(BF16))
            sums = add_from(sums, "ctx", low_masks())
            return total[:tokens] + arrived.astype(F32), sums, up, gate
        if i == 0:
            d_normed_one, sums, up, gate = state
            d_rows_attn, _ = norm_back(rows_in, gain_one, d_normed_one)
            sums = add_from(sums, "ctx", high_masks())
            return d_resid + d_rows_attn, sums, up, gate.T.astype(F32)
        return state

    grad_all, state = ring_scatter(
        weight_terms,
        [grad_fulls] * (half_ring + 1),
        input_side,
        ((d_query_raw, d_key_raw, d_value_raw), grad_up),
    )
    grad_all = grad_all[0].astype(F32) + (grad_all[1].astype(F32) + grad_all[2].astype(F32))
    grad_in, grad_gains, grad_up, grad_gate = state
    grad_down, grad_all = tie(flying.pop("down"), grad_all)
    grad_down = grad_down.astype(F32)
    grad_query, grad_key, grad_value, grad_output = (
        grad_all[a:b] for a, b in zip(cuts, cuts[1:])
    )
    grad_query, grad_key, grad_value = grad_query.T, grad_key.T, grad_value.T
    grad_gains = lax.dynamic_slice_in_dim(grad_gains, own_place, share, axis=1)
    return (
        block_out[None],
        grad_in[None],
        grad_query,
        grad_key,
        grad_value,
        grad_output,
        grad_gate,
        grad_up,
        grad_down,
        grad_gains[0],
        grad_gains[1],
        grad_gains[2],
        grad_gains[3],
    )


def solution(mesh):
    rows = P("fsdp", "ctx", None)
    columns = P(None, ("fsdp", "ctx"))
    units = P(("fsdp", "ctx"), None)
    gain = P(("ctx", "fsdp"))
    weights = (columns, columns, columns, units, columns, columns, units)
    return jax.shard_map(
        body,
        mesh=mesh,
        in_specs=(rows, P()) + weights + (gain,) * 4 + (rows,),
        out_specs=(rows, rows) + weights + (gain,) * 4,
        check_vma=False,
    )
```

time: 798 us -> 639 us (0.80)
  Pallas kernels: 0 us -> 189 us
  matrix products: 182 us -> 9.81 us
  waiting for transfers between devices: 380 us -> 238 us
  starting transfers between devices: 123 us -> 89 us
  between operations: 3.59 us -> 15.9 us
  local copies, waits for them, and re-layouts: 54.9 us -> 45.2 us
    pallas_call x0 -> x52, Pallas kernels: none -> 189 us  [the longest x4 35.8 us: weight_grad(): pl.pallas_call(functools.partial(weight_grad_kernel, len(units), len(rows...]
    dot_general x63 -> x3, matrix products: 170 us -> 9.81 us  [dot(): return lax.dot_general(a, b, (dims, ((), ())), preferred_element_type=F32)]
    ppermute x80 -> x64, waiting for transfers between devices: 257 us -> 156 us  [ring_hop(): lax.ppermute(block, 'ctx', [(order[i], order[(i + step) % size]) for i in...]
    ppermute x40 -> x24, waiting for transfers between devices: 124 us -> 81.7 us  [the longest x4 50.1 us: far_hop(): lax.ppermute(block, 'fsdp', [(i, i ^ size // 2) for i in range(size)])]
    ppermute x80 -> x64, starting transfers between devices: 95.3 us -> 67 us  [ring_hop(): lax.ppermute(block, 'ctx', [(order[i], order[(i + step) % size]) for i in...]
    convert_element_type x21 -> x29, other arithmetic: 7.01 us -> 26.1 us  [the longest x12 9.32 us: add_terms(): (to_behind.astype(F32) + ahead).astype(BF16)]
    dynamic_update_slice x23 -> x0, local copies, waits for them, and re-layouts: 17.7 us -> none  [put_blocks(): whole = lax.dynamic_update_slice_in_dim(whole, block, at * size, axis=0)]
    unnamed x214 -> x263, local copies, waits for them, and re-layouts: 16.4 us -> 29.2 us
  transfers between devices with their start and end apart: 120 -> 93, of which waited for: 64 -> 56; matrix products, arithmetic and copies ran while one was open for 27% -> 10% of each run, Pallas kernels for 0% -> 27%
where the time goes in v2:
time: 639 us; the launch traced here: 630 us
  waiting for transfers between devices  238 us (37%)
  Pallas kernels  189 us (30%)
  starting transfers between devices  89 us (14%)
  local copies, waits for them, and re-layouts  45.2 us (7%)
  other arithmetic  44 us (7%)
  between operations  15.9 us (2%)
  matrix products  9.81 us (2%)
    ppermute x64, waiting for transfers between devices, ring_hop(): lax.ppermute(block, 'ctx', [(order[i], order[(i + step) % size]) for i in...  156 us
    ppermute x64, starting transfers between devices, ring_hop(): lax.ppermute(block, 'ctx', [(order[i], order[(i + step) % size]) for i in...  67 us
    ppermute x4, waiting for transfers between devices, far_hop(): lax.ppermute(block, 'fsdp', [(i, i ^ size // 2) for i in range(size)])  50.1 us
    pallas_call x4, Pallas kernels, weight_grad(): pl.pallas_call(functools.partial(weight_grad_kernel, len(units), len(rows...  35.8 us
    pallas_call x10, Pallas kernels, unit_call(): pl.pallas_call(functools.partial(kernel, len(rows)), grid=(count // tile,...  34.2 us
    pallas_call x10, Pallas kernels, out_call(): pl.pallas_call(out_kernel, grid=(width // tile,), out_shape=jax.ShapeDtyp...  29.5 us
    unnamed x263, local copies, waits for them, and re-layouts  29.2 us
    ppermute x14, waiting for transfers between devices, add_from(): return sum((lax.ppermute(block, axis, route) for route in routes), block)  25.9 us
  transfers between devices with their start and end apart: 93, of which 56 were waited for; matrix products, arithmetic and copies ran while one was open for 10% of the time, Pallas kernels for 27%

profile of v2, /device:TPU:0, one launch (start us, length us, event | category | flops | bytes accessed | tf_op | source)
XLA Modules:
  0.0 630.2 jit_solution(13590926816901836859)
XLA Ops:
  8.8 2.6 collective-permute-start.5
  14.8 3.1 pad_maximum_fusion
  22.2 13.0 %collective-permute-done.2 = bf16[128,2304]{1,0:T(8,128)(2,1)S(1)} collective-permute-done((bf16[128,2304]{1,0:T(8,128)(2,1)S(1)}, bf16[128,2304]{1,0:T(8,128)(2,1)S(1)}, u32[]{:S(2)}, u32[]{:S(2)}) %collective-permute-start.2) | collective-permute-done | bytes 589856 | tf_op jit(solution)/shard_map/ppermute | solution.py:103
  43.4 3.8 shard_map.239
  47.1 11.5 %collective-permute-done.10 = f32[4,2304]{1,0:T(4,128)S(1)} collective-permute-done((f32[4,2304]{1,0:T(4,128)S(1)}, f32[4,2304]{1,0:T(4,128)S(1)}, u32[]{:S(2)}, u32[]{:S(2)}) %collective-permute-start.10) | collective-permute-done | bytes 36896 | tf_op jit(solution)/shard_map/ppermute | solution.py:114
  64.5 2.8 collective-permute-start.15
  67.3 2.6 pad_maximum_fusion.1.refs_6_
  69.9 3.6 shard_map.240
  73.5 13.2 %collective-permute-done.15 = f32[4,2304]{1,0:T(4,128)} collective-permute-done((f32[4,2304]{1,0:T(4,128)}, f32[4,2304]{1,0:T(4,128)}, u32[]{:S(2)}, u32[]{:S(2)}) %collective-permute-start.15) | collective-permute-done | bytes 36896 | tf_op jit(solution)/shard_map/ppermute | solution.py:114
  93.1 3.4 shard_map.241
  100.3 2.9 collective-permute-done.17.refs_0_
  110.6 4.2 shard_map.244
  116.8 3.6 shard_map.247.queries_ref
  123.2 3.3 collective-permute-done.18.refs_0_
  131.8 6.3 collective-permute-done.20.refs_0_
  144.1 6.4 %collective-permute-done.22.refs_0_ = bf16[8,128,256]{2,1,0:T(8,128)(2,1)S(1)} collective-permute-done((bf16[8,128,256]{2,1,0:T(8,128)(2,1)}, bf16[8,128,256]{2,1,0:T(8,128)(2,1)S(1)}, u32[]{:S(2)}, u32[]{:S(2)}) %collective-permute-start.22) | collective-permute-done | bytes 524320 | tf_op jit(solution)/shard_map/ppermute | solution.py:26
  161.8 5.4 shard_map.252
  167.2 2.6 fusion.47
  170.1 2.8 collective-permute-done.26
  175.8 13.8 %collective-permute-done.27.moved_ref = bf16[128,2304]{1,0:T(8,128)(2,1)S(1)} collective-permute-done((bf16[128,2304]{1,0:T(8,128)(2,1)S(1)}, bf16[128,2304]{1,0:T(8,128)(2,1)S(1)}, u32[]{:S(2)}, u32[]{:S(2)}) %collective-permute-start.27) | collective-permute-done | bytes 589856 | tf_op jit(solution)/shard_map/ppermute | solution.py:103
  193.4 3.5 shard_map.254
  199.2 7.2 %collective-permute-done.28.refs_0_.refs_6_ = bf16[128,2304]{1,0:T(8,128)(2,1)S(1)} collective-permute-done((bf16[128,2304]{1,0:T(8,128)(2,1)S(1)}, bf16[128,2304]{1,0:T(8,128)(2,1)S(1)}, u32[]{:S(2)}, u32[]{:S(2)}) %collective-permute-start.28) | collective-permute-done | bytes 589856 | tf_op jit(solution)/shard_map/ppermute | solution.py:26
  209.8 4.0 copy-done
  213.8 5.6 shard_map.255
  225.1 4.5 shard_map.256
  229.6 6.1 collective-permute-done.32.refs_0_.refs_10_
  239.1 4.5 shard_map.257
  245.6 3.5 shard_map.258
  255.6 4.9 collective-permute-done.36
  266.7 8.7 %collective-permute-done.38 = bf16[128,2304]{1,0:T(8,128)(2,1)S(1)} collective-permute-done((bf16[128,2304]{1,0:T(8,128)(2,1)S(1)}, bf16[128,2304]{1,0:T(8,128)(2,1)S(1)}, u32[]{:S(2)}, u32[]{:S(2)}) %collective-permute-start.38) | collective-permute-done | bytes 589856 | tf_op jit(solution)/shard_map/ppermute | solution.py:26
  281.6 13.1 %collective-permute-done.40 = bf16[128,2304]{1,0:T(8,128)(2,1)S(1)} collective-permute-done((bf16[128,2304]{1,0:T(8,128)(2,1)S(1)}, bf16[128,2304]{1,0:T(8,128)(2,1)S(1)}, u32[]{:S(2)}, u32[]{:S(2)}) %collective-permute-start.40) | collective-permute-done | bytes 589856 | tf_op jit(solution)/shard_map/ppermute | solution.py:26
  300.1 11.2 %collective-permute-done.42.behind_ref = bf16[128,2304]{1,0:T(8,128)(2,1)S(1)} collective-permute-done((bf16[128,2304]{1,0:T(8,128)(2,1)S(1)}, bf16[128,2304]{1,0:T(8,128)(2,1)S(1)}, u32[]{:S(2)}, u32[]{:S(2)}) %collective-permute-start.42) | collective-permute-done | bytes 589856 | tf_op jit(solution)/shard_map/ppermute | solution.py:26
  319.0 8.9 %collective-permute-done.44.refs_0_.refs_6_ = bf16[128,2304]{1,0:T(8,128)(2,1)S(1)} collective-permute-done((bf16[128,2304]{1,0:T(8,128)(2,1)S(1)}, bf16[128,2304]{1,0:T(8,128)(2,1)S(1)}, u32[]{:S(2)}, u32[]{:S(2)}) %collective-permute-start.44) | collective-permute-done | bytes 589856 | tf_op jit(solution)/shard_map/ppermute | solution.py:26
  330.0 2.7 shard_map.266
  333.5 7.3 %collective-permute-done.46.refs_0_.refs_8_ = bf16[128,2304]{1,0:T(8,128)(2,1)S(1)} collective-permute-done((bf16[128,2304]{1,0:T(8,128)(2,1)S(1)}, bf16[128,2304]{1,0:T(8,128)(2,1)S(1)}, u32[]{:S(2)}, u32[]{:S(2)}) %collective-permute-start.46) | collective-permute-done | bytes 589856 | tf_op jit(solution)/shard_map/ppermute | solution.py:26
  344.3 2.7 shard_map.267
  347.1 5.1 collective-permute-done.48.refs_0_.refs_10_
  356.1 2.7 shard_map.268
  360.7 2.6 collective-permute-done.51.refs_1_.refs_13_
  365.5 2.8 shard_map.270
  370.6 4.3 shard_map.271
  379.7 4.3 shard_map.272
  384.0 8.6 %shard_map.273.refs_14_ = bf16[1152,2304]{1,0:T(8,128)(2,1)} custom-call(bf16[128,1152]{1,0:T(8,128)(2,1)} %copy-done.28, bf16[256,1152]{1,0:T(8,128)(2,1)} %copy-done.16, bf16[256,1152]{1,0:T(8,128)(2,1)} %copy-done.18, bf16[256,1152]{1,0:T(8,128)(2,1)} %copy-done.19, bf16[128,1152]{1,0:T(8,128)(2,1)} %copy-done.30, bf16[128,2304]{1,0:T(8,128)(2,1)} %copy-done.11, ...), custom_call_target="tpu_custom_call" | custom-call | tf_op jit(solution)/shard_map/pallas_call | solution.py:385
  395.9 4.0 copy-done.1
  399.9 4.3 shard_map.274
  405.3 5.9 shard_map.275
  417.2 4.0 copy-done.2
  421.2 2.8 shard_map.276.term_ref
  432.6 8.7 %shard_map.278 = (bf16[512,512]{1,0:T(8,128)(2,1)}, bf16[2,4,128,256]{3,2,1,0:T(8,128)(2,1)}, bf16[2,4,128,256]{3,2,1,0:T(8,128)(2,1)}, bf16[2,4,128,256]{3,2,1,...) custom-call(bf16[8,1024,256]{2,1,0:T(8,128)(2,1)} %shard_map.251.key, ...), custom_call_target="tpu_custom_call" | custom-call | tf_op jit(solution)/shard_map/pallas_call | solution.py:633
  441.3 3.7 collective-permute-done.60.d_attn_ref
  448.3 9.3 %shard_map.279 = (bf16[512,512]{1,0:T(8,128)(2,1)}, bf16[2,4,128,256]{3,2,1,0:T(8,128)(2,1)}, bf16[2,4,128,256]{3,2,1,0:T(8,128)(2,1)}, bf16[2,4,128,256]{3,2,1,...) custom-call(bf16[8,1024,256]{2,1,0:T(8,128)(2,1)} %shard_map.251.key, ...), custom_call_target="tpu_custom_call", output_to_operand_aliasing={{0}: (10, {}), {1}: (11, {}), {2}: (12, {}), {3}: (13, {}),... | custom-call | tf_op jit(solution)/shard_map/pallas_call | solution.py:633
  459.7 6.4 %collective-permute-done.63 = bf16[1,4,128,256]{3,2,1,0:T(8,128)(2,1)S(1)} collective-permute-done((bf16[1,4,128,256]{3,2,1,0:T(8,128)(2,1)}, bf16[1,4,128,256]{3,2,1,0:T(8,128)(2,1)S(1)}, u32[]{:S(2)}, u32[]{:S(2)}) %collective-permute-start.63) | collective-permute-done | bytes 262176 | tf_op jit(solution)/shard_map/ppermute | solution.py:26
  472.6 10.7 %shard_map.280 = bf16[1152,2304]{1,0:T(8,128)(2,1)} custom-call(bf16[128,1152]{1,0:T(8,128)(2,1)} %copy-done.57, bf16[256,1152]{1,0:T(8,128)(2,1)} %copy-done.41, bf16[256,1152]{1,0:T(8,128)(2,1)} %copy-done.42, bf16[256,1152]{1,0:T(8,128)(2,1)} %copy-done.43, bf16[128,1152]{1,0:T(8,128)(2,1)} %copy-done.59, bf16[128,2304]{1,0:T(8,128)(2,1)} %copy-done.11, ...), custom_call_target="tpu_custom_call" | custom-call | tf_op jit(solution)/shard_map/pallas_call | solution.py:385
  490.1 10.6 %shard_map.281 = bf16[1152,2304]{1,0:T(8,128)(2,1)} custom-call(bf16[128,1152]{1,0:T(8,128)(2,1)} %copy-done.48, bf16[256,1152]{1,0:T(8,128)(2,1)} %copy-done.33, bf16[256,1152]{1,0:T(8,128)(2,1)} %copy-done.34, bf16[256,1152]{1,0:T(8,128)(2,1)} %copy-done.35, bf16[128,1152]{1,0:T(8,128)(2,1)} %copy-done.50, bf16[128,2304]{1,0:T(8,128)(2,1)} %copy-done.36, ...), custom_call_target="tpu_custom_call" | custom-call | tf_op jit(solution)/shard_map/pallas_call | solution.py:385
  505.6 2.9 convolution_convert_fusion.1.refs_2_.refs_6_.refs_1_
  508.5 4.3 convolution_convert_fusion.refs_5_.refs_9_.refs_4_
  515.6 5.6 shard_map.282
  526.7 2.9 shard_map.284
  529.6 7.4 %shard_map.285 = (f32[256,2304]{1,0:T(8,128)}, bf16[256,2304]{1,0:T(8,128)(2,1)}, f32[1,2304]{1,0:T(1,128)}) custom-call(bf16[512,512]{1,0:T(8,128)(2,1)} %get-tuple-element.1101.refs_0_, bf16[512,256]{1,0:T(8,128)(2,1)} %get-tuple-element.1102.refs_1_, bf16[512,256]{1,0:T(8,128)(2,1)} %get-tuple-element.1103.refs_2_, ...), custom_call_target="tpu_custom_call" | custom-call | tf_op jit(solution)/shard_map/pallas_call | solution.py:249
  544.2 2.7 shard_map.286
  547.0 15.2 %collective-permute-done.73 = bf16[192,2304]{1,0:T(8,128)(2,1)S(1)} collective-permute-done((bf16[192,2304]{1,0:T(8,128)(2,1)S(1)}, bf16[192,2304]{1,0:T(8,128)(2,1)S(1)}, u32[]{:S(2)}, u32[]{:S(2)}) %collective-permute-start.73) | collective-permute-done | bytes 884768 | tf_op jit(solution)/shard_map/ppermute | solution.py:26
  572.5 3.1 shard_map.287
  576.6 19.6 %collective-permute-done.81 = bf16[128,2304]{1,0:T(8,128)(2,1)S(1)} collective-permute-done((bf16[128,2304]{1,0:T(8,128)(2,1)S(1)}, bf16[128,2304]{1,0:T(8,128)(2,1)S(1)}, u32[]{:S(2)}, u32[]{:S(2)}) %collective-permute-start.81) | collective-permute-done | bytes 589856 | tf_op jit(solution)/shard_map/ppermute | solution.py:103
  606.4 9.5 %collective-permute-done.85 = bf16[192,2304]{1,0:T(8,128)(2,1)S(1)} collective-permute-done((bf16[192,2304]{1,0:T(8,128)(2,1)S(1)}, bf16[192,2304]{1,0:T(8,128)(2,1)S(1)}, u32[]{:S(2)}, u32[]{:S(2)}) %collective-permute-start.85) | collective-permute-done | bytes 884768 | tf_op jit(solution)/shard_map/ppermute | solution.py:26
  (555 shorter events, 231.0 us)
Async XLA Ops:
  7.2 131.6 %all-gather.3.cloned.1.call-start = ((), (), s32[]{:S(2)}) async-start(), calls=%async_computation.3 | async-start | bytes 13271040 | tf_op jit(solution)/shard_map/all_gather | solution.py:718
  8.2 11.8 %collective-permute-start.4 = (f32[4,2304]{1,0:T(4,128)S(1)}, f32[4,2304]{1,0:T(4,128)S(1)}, u32[]{:S(2)}, u32[]{:S(2)}) collective-permute-start(f32[4,2304]{1,0:T(4,128)S(1)} %dynamic_update_slice.5), channel_id=1, source_target_pairs={{0,1},{1,0},{2,3},{3,2},{4,5},{5,4},{6,7},{7,6},{8,9},{9,8},{10,11... | collective-permute-start | bytes 110600 | tf_op jit(solution)/shard_map/ppermute | solution.py:114
  8.8 13.2 %collective-permute-start.5 = (f32[4,2304]{1,0:T(4,128)S(1)}, f32[4,2304]{1,0:T(4,128)S(1)}, u32[]{:S(2)}, u32[]{:S(2)}) collective-permute-start(f32[4,2304]{1,0:T(4,128)S(1)} %dynamic_update_slice.5), channel_id=1, source_target_pairs={{0,2},{1,3},{2,0},{3,1},{4,6},{5,7},{6,4},{7,5},{8,10},{9,11},{10,... | collective-permute-start | bytes 110600 | tf_op jit(solution)/shard_map/ppermute | solution.py:114
  11.4 10.8 %collective-permute-start.6 = (f32[4,2304]{1,0:T(4,128)S(1)}, f32[4,2304]{1,0:T(4,128)S(1)}, u32[]{:S(2)}, u32[]{:S(2)}) collective-permute-start(f32[4,2304]{1,0:T(4,128)S(1)} %dynamic_update_slice.5), channel_id=1, source_target_pairs={{0,3},{1,2},{2,1},{3,0},{4,7},{5,6},{6,5},{7,4},{8,11},{9,10},{10,... | collective-permute-start | bytes 110600 | tf_op jit(solution)/shard_map/ppermute | solution.py:114
  12.7 22.5 %collective-permute-start = (bf16[192,2304]{1,0:T(8,128)(2,1)S(1)}, bf16[192,2304]{1,0:T(8,128)(2,1)}, u32[]{:S(2)}, u32[]{:S(2)}) collective-permute-start(bf16[192,2304]{1,0:T(8,128)(2,1)S(1)} %pad_maximum_fusion.3.refs_0_), channel_id=1, source_target_pairs={{0,8},{8,16},{16,24},{24,28},{28,20},{20,12},{12,4},{4,0},{1,9},{9... | collective-permute-start | bytes 2654216 | tf_op jit(solution)/shard_map/ppermute | solution.py:26
  14.6 21.7 %collective-permute-start.1 = (bf16[192,2304]{1,0:T(8,128)(2,1)S(1)}, bf16[192,2304]{1,0:T(8,128)(2,1)}, u32[]{:S(2)}, u32[]{:S(2)}) collective-permute-start(bf16[192,2304]{1,0:T(8,128)(2,1)S(1)} %pad_maximum_fusion.3.refs_0_), channel_id=1, source_target_pairs={{0,4},{8,0},{16,8},{24,16},{28,24},{20,28},{12,20},{4,12},{1,5},{9... | collective-permute-start | bytes 2654216 | tf_op jit(solution)/shard_map/ppermute | solution.py:26
  20.1 15.2 %collective-permute-start.2 = (bf16[128,2304]{1,0:T(8,128)(2,1)S(1)}, bf16[128,2304]{1,0:T(8,128)(2,1)S(1)}, u32[]{:S(2)}, u32[]{:S(2)}) collective-permute-start(bf16[128,2304]{1,0:T(8,128)(2,1)S(1)} %bitcast.79), channel_id=1, source_target_pairs={{0,2},{1,3},{2,0},{3,1},{4,6},{5,7},{6,4},{7,5},{8,10},{9,11},{10,... | collective-permute-start | bytes 1769480 | tf_op jit(solution)/shard_map/ppermute | solution.py:103
  22.1 13.2 %collective-permute-start.3 = (bf16[128,2304]{1,0:T(8,128)(2,1)S(1)}, bf16[128,2304]{1,0:T(8,128)(2,1)S(1)}, u32[]{:S(2)}, u32[]{:S(2)}) collective-permute-start(bf16[128,2304]{1,0:T(8,128)(2,1)S(1)} %bitcast.80), channel_id=1, source_target_pairs={{0,1},{1,0},{2,3},{3,2},{4,5},{5,4},{6,7},{7,6},{8,9},{9,8},{10,11... | collective-permute-start | bytes 1769480 | tf_op jit(solution)/shard_map/ppermute | solution.py:108
  36.3 171.4 %all-gather.5.cloned.1.call-start = ((), (), s32[]{:S(2)}) async-start(), calls=%async_computation.4 | async-start | bytes 6635520 | tf_op jit(solution)/shard_map/all_gather | solution.py:773
  36.4 24.2 %collective-permute-start.7 = (bf16[192,2304]{1,0:T(8,128)(2,1)}, bf16[192,2304]{1,0:T(8,128)(2,1)}, u32[]{:S(2)}, u32[]{:S(2)}) collective-permute-start(bf16[192,2304]{1,0:T(8,128)(2,1)} %collective-permute-done.refs_0_), channel_id=1, source_target_pairs={{0,8},{8,16},{16,24},{24,28},{28,20},{20,12},{12,4},{4,0},{1,9},{9... | collective-permute-start | bytes 2654216 | tf_op jit(solution)/shard_map/ppermute | solution.py:26
  37.9 22.7 %collective-permute-start.8 = (bf16[192,2304]{1,0:T(8,128)(2,1)}, bf16[192,2304]{1,0:T(8,128)(2,1)}, u32[]{:S(2)}, u32[]{:S(2)}) collective-permute-start(bf16[192,2304]{1,0:T(8,128)(2,1)} %collective-permute-done.1.refs_1_), channel_id=1, source_target_pairs={{0,4},{8,0},{16,8},{24,16},{28,24},{20,28},{12,20},{4,12},{1,5},{9... | collective-permute-start | bytes 2654216 | tf_op jit(solution)/shard_map/ppermute | solution.py:26
  38.5 20.2 %collective-permute-start.10 = (f32[4,2304]{1,0:T(4,128)S(1)}, f32[4,2304]{1,0:T(4,128)S(1)}, u32[]{:S(2)}, u32[]{:S(2)}) collective-permute-start(f32[4,2304]{1,0:T(4,128)S(1)} %add_add_fusion.4), channel_id=1, source_target_pairs={{0,4},{4,0},{8,12},{12,8},{16,20},{20,16},{24,28},{28,24},{1,5},{5... | collective-permute-start | bytes 110600 | tf_op jit(solution)/shard_map/ppermute | solution.py:114
  39.1 20.8 %collective-permute-start.11 = (f32[4,2304]{1,0:T(4,128)S(1)}, f32[4,2304]{1,0:T(4,128)S(1)}, u32[]{:S(2)}, u32[]{:S(2)}) collective-permute-start(f32[4,2304]{1,0:T(4,128)S(1)} %add_add_fusion.4), channel_id=1, source_target_pairs={{0,8},{4,12},{8,0},{12,4},{16,24},{20,28},{24,16},{28,20},{1,9},{5... | collective-permute-start | bytes 110600 | tf_op jit(solution)/shard_map/ppermute | solution.py:114
  40.7 19.1 %collective-permute-start.12 = (f32[4,2304]{1,0:T(4,128)S(1)}, f32[4,2304]{1,0:T(4,128)S(1)}, u32[]{:S(2)}, u32[]{:S(2)}) collective-permute-start(f32[4,2304]{1,0:T(4,128)S(1)} %add_add_fusion.4), channel_id=1, source_target_pairs={{0,12},{4,8},{8,4},{12,0},{16,28},{20,24},{24,20},{28,16},{1,13},{... | collective-permute-start | bytes 110600 | tf_op jit(solution)/shard_map/ppermute | solution.py:114
  60.6 26.8 %collective-permute-start.13 = (bf16[192,2304]{1,0:T(8,128)(2,1)}, bf16[192,2304]{1,0:T(8,128)(2,1)}, u32[]{:S(2)}, u32[]{:S(2)}) collective-permute-start(bf16[192,2304]{1,0:T(8,128)(2,1)} %collective-permute-done.7.refs_0_), channel_id=1, source_target_pairs={{0,8},{8,16},{16,24},{24,28},{28,20},{20,12},{12,4},{4,0},{1,9},{9... | collective-permute-start | bytes 2654216 | tf_op jit(solution)/shard_map/ppermute | solution.py:26
  61.5 26.0 %collective-permute-start.14 = (bf16[192,2304]{1,0:T(8,128)(2,1)}, bf16[192,2304]{1,0:T(8,128)(2,1)}, u32[]{:S(2)}, u32[]{:S(2)}) collective-permute-start(bf16[192,2304]{1,0:T(8,128)(2,1)} %collective-permute-done.8.refs_1_), channel_id=1, source_target_pairs={{0,4},{8,0},{16,8},{24,16},{28,24},{20,28},{12,20},{4,12},{1,5},{9... | collective-permute-start | bytes 2654216 | tf_op jit(solution)/shard_map/ppermute | solution.py:26
  64.5 22.2 %collective-permute-start.15 = (f32[4,2304]{1,0:T(4,128)}, f32[4,2304]{1,0:T(4,128)}, u32[]{:S(2)}, u32[]{:S(2)}) collective-permute-start(f32[4,2304]{1,0:T(4,128)} %add_add_fusion.3), channel_id=1, source_target_pairs={{0,16},{4,20},{8,24},{12,28},{16,0},{20,4},{24,8},{28,12},{1,17},{... | collective-permute-start | bytes 110600 | tf_op jit(solution)/shard_map/ppermute | solution.py:114
  89.3 11.0 %collective-permute-start.16 = (bf16[96,2304]{1,0:T(8,128)(2,1)}, bf16[96,2304]{1,0:T(8,128)(2,1)}, u32[]{:S(2)}, u32[]{:S(2)}) collective-permute-start(bf16[96,2304]{1,0:T(8,128)(2,1)} %slice.138), channel_id=1, source_target_pairs={{0,8},{8,16},{16,24},{24,28},{28,20},{20,12},{12,4},{4,0},{1,9},{9... | collective-permute-start | bytes 1327112 | tf_op jit(solution)/shard_map/ppermute | solution.py:26
  92.5 10.7 %collective-permute-start.17 = (bf16[96,2304]{1,0:T(8,128)(2,1)}, bf16[96,2304]{1,0:T(8,128)(2,1)S(1)}, u32[]{:S(2)}, u32[]{:S(2)}) collective-permute-start(bf16[96,2304]{1,0:T(8,128)(2,1)} %slice.139), channel_id=1, source_target_pairs={{0,4},{8,0},{16,8},{24,16},{28,24},{20,28},{12,20},{4,12},{1,5},{9... | collective-permute-start | bytes 1327112 | tf_op jit(solution)/shard_map/ppermute | solution.py:26
  114.8 11.6 %collective-permute-start.18 = (bf16[8,128,256]{2,1,0:T(8,128)(2,1)}, bf16[8,128,256]{2,1,0:T(8,128)(2,1)S(1)}, u32[]{:S(2)}, u32[]{:S(2)}) collective-permute-start(bf16[8,128,256]{2,1,0:T(8,128)(2,1)} %bitcast.21.refs_0_), channel_id=1, source_target_pairs={{0,8},{8,16},{16,24},{24,28},{28,20},{20,12},{12,4},{4,0},{1,9},{9... | collective-permute-start | bytes 1572872 | tf_op jit(solution)/shard_map/ppermute | solution.py:26
  115.2 11.6 %collective-permute-start.19 = (bf16[8,128,256]{2,1,0:T(8,128)(2,1)}, bf16[8,128,256]{2,1,0:T(8,128)(2,1)S(1)}, u32[]{:S(2)}, u32[]{:S(2)}) collective-permute-start(bf16[8,128,256]{2,1,0:T(8,128)(2,1)} %bitcast.21.refs_0_), channel_id=1, source_target_pairs={{0,4},{8,0},{16,8},{24,16},{28,24},{20,28},{12,20},{4,12},{1,5},{9... | collective-permute-start | bytes 1572872 | tf_op jit(solution)/shard_map/ppermute | solution.py:26
  128.1 10.7 %collective-permute-start.21 = (bf16[8,128,256]{2,1,0:T(8,128)(2,1)}, bf16[8,128,256]{2,1,0:T(8,128)(2,1)S(1)}, u32[]{:S(2)}, u32[]{:S(2)}) collective-permute-start(bf16[8,128,256]{2,1,0:T(8,128)(2,1)} %copy-done.97), channel_id=1, source_target_pairs={{0,4},{8,0},{16,8},{24,16},{28,24},{20,28},{12,20},{4,12},{1,5},{9... | collective-permute-start | bytes 1572872 | tf_op jit(solution)/shard_map/ppermute | solution.py:26
  138.8 376.7 %reduce-scatter.4.cloned.1.call-start = ((), (), s32[]{:S(2)}) async-start(), calls=%async_computation.5 | async-start | bytes 6635520 | tf_op jit(solution)/shard_map/reduce_scatter | solution.py:860
  139.7 10.8 %collective-permute-start.22 = (bf16[8,128,256]{2,1,0:T(8,128)(2,1)}, bf16[8,128,256]{2,1,0:T(8,128)(2,1)S(1)}, u32[]{:S(2)}, u32[]{:S(2)}) collective-permute-start(bf16[8,128,256]{2,1,0:T(8,128)(2,1)} %collective-permute-done.20.refs_0_), channel_id=1, source_target_pairs={{0,8},{8,16},{16,24},{24,28},{28,20},{20,12},{12,4},{4,0},{1,9},{9... | collective-permute-start | bytes 1572872 | tf_op jit(solution)/shard_map/ppermute | solution.py:26
  173.2 16.4 %collective-permute-start.27 = (bf16[128,2304]{1,0:T(8,128)(2,1)S(1)}, bf16[128,2304]{1,0:T(8,128)(2,1)S(1)}, u32[]{:S(2)}, u32[]{:S(2)}) collective-permute-start(bf16[128,2304]{1,0:T(8,128)(2,1)S(1)} %get-tuple-element.1194), channel_id=1, source_target_pairs={{0,2},{1,3},{2,0},{3,1},{4,6},{5,7},{6,4},{7,5},{8,10},{9,11},{10,... | collective-permute-start | bytes 1769480 | tf_op jit(solution)/shard_map/ppermute | solution.py:103
  191.4 15.1 %collective-permute-start.28 = (bf16[128,2304]{1,0:T(8,128)(2,1)S(1)}, bf16[128,2304]{1,0:T(8,128)(2,1)S(1)}, u32[]{:S(2)}, u32[]{:S(2)}) collective-permute-start(bf16[128,2304]{1,0:T(8,128)(2,1)S(1)} %get-tuple-element.1008.refs_0_.refs_5_), channel_id=1, source_target_pairs={{0,8},{8,16},{16,24},{24,28},{28,20},{20,12},{12,4},{4,0},{1,9},{9... | collective-permute-start | bytes 1769480 | tf_op jit(solution)/shard_map/ppermute | solution.py:26
  192.8 14.9 %collective-permute-start.29 = (bf16[128,2304]{1,0:T(8,128)(2,1)S(1)}, bf16[128,2304]{1,0:T(8,128)(2,1)}, u32[]{:S(2)}, u32[]{:S(2)}) collective-permute-start(bf16[128,2304]{1,0:T(8,128)(2,1)S(1)} %get-tuple-element.1008.refs_0_.refs_5_), channel_id=1, source_target_pairs={{0,4},{8,0},{16,8},{24,16},{28,24},{20,28},{12,20},{4,12},{1,5},{9... | collective-permute-start | bytes 1769480 | tf_op jit(solution)/shard_map/ppermute | solution.py:26
  207.7 13.9 %collective-permute-start.30 = (bf16[128,2304]{1,0:T(8,128)(2,1)S(1)}, bf16[128,2304]{1,0:T(8,128)(2,1)S(1)}, u32[]{:S(2)}, u32[]{:S(2)}) collective-permute-start(bf16[128,2304]{1,0:T(8,128)(2,1)S(1)} %collective-permute-done.28.refs_0_.refs_6_), channel_id=1, source_target_pairs={{0,8},{8,16},{16,24},{24,28},{28,20},{20,12},{12,4},{4,0},{1,9},{9... | collective-permute-start | bytes 1769480 | tf_op jit(solution)/shard_map/ppermute | solution.py:26
  209.2 13.8 %collective-permute-start.31 = (bf16[128,2304]{1,0:T(8,128)(2,1)}, bf16[128,2304]{1,0:T(8,128)(2,1)S(1)}, u32[]{:S(2)}, u32[]{:S(2)}) collective-permute-start(bf16[128,2304]{1,0:T(8,128)(2,1)} %collective-permute-done.29.refs_1_.refs_7_), channel_id=1, source_target_pairs={{0,4},{8,0},{16,8},{24,16},{28,24},{20,28},{12,20},{4,12},{1,5},{9... | collective-permute-start | bytes 1769480 | tf_op jit(solution)/shard_map/ppermute | solution.py:26
  223.0 12.7 %collective-permute-start.32 = (bf16[128,2304]{1,0:T(8,128)(2,1)S(1)}, bf16[128,2304]{1,0:T(8,128)(2,1)S(1)}, u32[]{:S(2)}, u32[]{:S(2)}) collective-permute-start(bf16[128,2304]{1,0:T(8,128)(2,1)S(1)} %collective-permute-done.30.refs_0_.refs_8_), channel_id=1, source_target_pairs={{0,8},{8,16},{16,24},{24,28},{28,20},{20,12},{12,4},{4,0},{1,9},{9... | collective-permute-start | bytes 1769480 | tf_op jit(solution)/shard_map/ppermute | solution.py:26
  224.5 12.4 %collective-permute-start.33 = (bf16[128,2304]{1,0:T(8,128)(2,1)S(1)}, bf16[128,2304]{1,0:T(8,128)(2,1)S(1)}, u32[]{:S(2)}, u32[]{:S(2)}) collective-permute-start(bf16[128,2304]{1,0:T(8,128)(2,1)S(1)} %collective-permute-done.31.refs_1_.refs_9_), channel_id=1, source_target_pairs={{0,4},{8,0},{16,8},{24,16},{28,24},{20,28},{12,20},{4,12},{1,5},{9... | collective-permute-start | bytes 1769480 | tf_op jit(solution)/shard_map/ppermute | solution.py:26
  264.2 11.3 %collective-permute-start.38 = (bf16[128,2304]{1,0:T(8,128)(2,1)S(1)}, bf16[128,2304]{1,0:T(8,128)(2,1)S(1)}, u32[]{:S(2)}, u32[]{:S(2)}) collective-permute-start(bf16[128,2304]{1,0:T(8,128)(2,1)S(1)} %add_convert_fusion.17), channel_id=1, source_target_pairs={{0,8},{8,16},{16,24},{24,28},{28,20},{20,12},{12,4},{4,0},{1,9},{9... | collective-permute-start | bytes 1769480 | tf_op jit(solution)/shard_map/ppermute | solution.py:26
  264.4 12.1 %collective-permute-start.39 = (bf16[128,2304]{1,0:T(8,128)(2,1)S(1)}, bf16[128,2304]{1,0:T(8,128)(2,1)S(1)}, u32[]{:S(2)}, u32[]{:S(2)}) collective-permute-start(bf16[128,2304]{1,0:T(8,128)(2,1)S(1)} %add_convert_fusion.16), channel_id=1, source_target_pairs={{0,4},{8,0},{16,8},{24,16},{28,24},{20,28},{12,20},{4,12},{1,5},{9... | collective-permute-start | bytes 1769480 | tf_op jit(solution)/shard_map/ppermute | solution.py:26
  279.3 15.4 %collective-permute-start.40 = (bf16[128,2304]{1,0:T(8,128)(2,1)S(1)}, bf16[128,2304]{1,0:T(8,128)(2,1)S(1)}, u32[]{:S(2)}, u32[]{:S(2)}) collective-permute-start(bf16[128,2304]{1,0:T(8,128)(2,1)S(1)} %add_convert_fusion.15), channel_id=1, source_target_pairs={{0,8},{8,16},{16,24},{24,28},{28,20},{20,12},{12,4},{4,0},{1,9},{9... | collective-permute-start | bytes 1769480 | tf_op jit(solution)/shard_map/ppermute | solution.py:26
  280.3 15.7 %collective-permute-start.41 = (bf16[128,2304]{1,0:T(8,128)(2,1)S(1)}, bf16[128,2304]{1,0:T(8,128)(2,1)S(1)}, u32[]{:S(2)}, u32[]{:S(2)}) collective-permute-start(bf16[128,2304]{1,0:T(8,128)(2,1)S(1)} %add_convert_fusion.14), channel_id=1, source_target_pairs={{0,4},{8,0},{16,8},{24,16},{28,24},{20,28},{12,20},{4,12},{1,5},{9... | collective-permute-start | bytes 1769480 | tf_op jit(solution)/shard_map/ppermute | solution.py:26
  296.3 15.0 %collective-permute-start.42 = (bf16[128,2304]{1,0:T(8,128)(2,1)S(1)}, bf16[128,2304]{1,0:T(8,128)(2,1)S(1)}, u32[]{:S(2)}, u32[]{:S(2)}) collective-permute-start(bf16[128,2304]{1,0:T(8,128)(2,1)S(1)} %add_convert_fusion.13), channel_id=1, source_target_pairs={{0,8},{8,16},{16,24},{24,28},{28,20},{20,12},{12,4},{4,0},{1,9},{9... | collective-permute-start | bytes 1769480 | tf_op jit(solution)/shard_map/ppermute | solution.py:26
  296.6 15.3 %collective-permute-start.43 = (bf16[128,2304]{1,0:T(8,128)(2,1)S(1)}, bf16[128,2304]{1,0:T(8,128)(2,1)S(1)}, u32[]{:S(2)}, u32[]{:S(2)}) collective-permute-start(bf16[128,2304]{1,0:T(8,128)(2,1)S(1)} %add_convert_fusion.12), channel_id=1, source_target_pairs={{0,4},{8,0},{16,8},{24,16},{28,24},{20,28},{12,20},{4,12},{1,5},{9... | collective-permute-start | bytes 1769480 | tf_op jit(solution)/shard_map/ppermute | solution.py:26
  314.1 13.8 %collective-permute-start.44 = (bf16[128,2304]{1,0:T(8,128)(2,1)S(1)}, bf16[128,2304]{1,0:T(8,128)(2,1)S(1)}, u32[]{:S(2)}, u32[]{:S(2)}) collective-permute-start(bf16[128,2304]{1,0:T(8,128)(2,1)S(1)} %get-tuple-element.1061.refs_0_.refs_5_), channel_id=1, source_target_pairs={{0,8},{8,16},{16,24},{24,28},{28,20},{20,12},{12,4},{4,0},{1,9},{9... | collective-permute-start | bytes 1769480 | tf_op jit(solution)/shard_map/ppermute | solution.py:26
  314.1 13.8 %collective-permute-start.45 = (bf16[128,2304]{1,0:T(8,128)(2,1)S(1)}, bf16[128,2304]{1,0:T(8,128)(2,1)S(1)}, u32[]{:S(2)}, u32[]{:S(2)}) collective-permute-start(bf16[128,2304]{1,0:T(8,128)(2,1)S(1)} %get-tuple-element.1061.refs_0_.refs_5_), channel_id=1, source_target_pairs={{0,4},{8,0},{16,8},{24,16},{28,24},{20,28},{12,20},{4,12},{1,5},{9... | collective-permute-start | bytes 1769480 | tf_op jit(solution)/shard_map/ppermute | solution.py:26
  327.9 12.9 %collective-permute-start.46 = (bf16[128,2304]{1,0:T(8,128)(2,1)S(1)}, bf16[128,2304]{1,0:T(8,128)(2,1)S(1)}, u32[]{:S(2)}, u32[]{:S(2)}) collective-permute-start(bf16[128,2304]{1,0:T(8,128)(2,1)S(1)} %collective-permute-done.44.refs_0_.refs_6_), channel_id=1, source_target_pairs={{0,8},{8,16},{16,24},{24,28},{28,20},{20,12},{12,4},{4,0},{1,9},{9... | collective-permute-start | bytes 1769480 | tf_op jit(solution)/shard_map/ppermute | solution.py:26
  329.4 12.9 %collective-permute-start.47 = (bf16[128,2304]{1,0:T(8,128)(2,1)S(1)}, bf16[128,2304]{1,0:T(8,128)(2,1)S(1)}, u32[]{:S(2)}, u32[]{:S(2)}) collective-permute-start(bf16[128,2304]{1,0:T(8,128)(2,1)S(1)} %collective-permute-done.45.refs_1_.refs_7_), channel_id=1, source_target_pairs={{0,4},{8,0},{16,8},{24,16},{28,24},{20,28},{12,20},{4,12},{1,5},{9... | collective-permute-start | bytes 1769480 | tf_op jit(solution)/shard_map/ppermute | solution.py:26
  377.4 15.3 %collective-permute-start.54 = (bf16[128,2304]{1,0:T(8,128)(2,1)S(1)}, bf16[128,2304]{1,0:T(8,128)(2,1)S(1)}, u32[]{:S(2)}, u32[]{:S(2)}) collective-permute-start(bf16[128,2304]{1,0:T(8,128)(2,1)S(1)} %add_convert_fusion.11), channel_id=1, source_target_pairs={{0,8},{8,16},{16,24},{24,28},{28,20},{20,12},{12,4},{4,0},{1,9},{9... | collective-permute-start | bytes 1769480 | tf_op jit(solution)/shard_map/ppermute | solution.py:26
  377.8 14.9 %collective-permute-start.55 = (bf16[128,2304]{1,0:T(8,128)(2,1)S(1)}, bf16[128,2304]{1,0:T(8,128)(2,1)S(1)}, u32[]{:S(2)}, u32[]{:S(2)}) collective-permute-start(bf16[128,2304]{1,0:T(8,128)(2,1)S(1)} %add_convert_fusion.10), channel_id=1, source_target_pairs={{0,4},{8,0},{16,8},{24,16},{28,24},{20,28},{12,20},{4,12},{1,5},{9... | collective-permute-start | bytes 1769480 | tf_op jit(solution)/shard_map/ppermute | solution.py:26
  393.8 18.6 %collective-permute-start.56 = (bf16[128,2304]{1,0:T(8,128)(2,1)}, bf16[128,2304]{1,0:T(8,128)(2,1)}, u32[]{:S(2)}, u32[]{:S(2)}) collective-permute-start(bf16[128,2304]{1,0:T(8,128)(2,1)} %add_convert_fusion.9), channel_id=1, source_target_pairs={{0,8},{8,16},{16,24},{24,28},{28,20},{20,12},{12,4},{4,0},{1,9},{9... | collective-permute-start | bytes 1769480 | tf_op jit(solution)/shard_map/ppermute | solution.py:26
  394.2 18.3 %collective-permute-start.57 = (bf16[128,2304]{1,0:T(8,128)(2,1)S(1)}, bf16[128,2304]{1,0:T(8,128)(2,1)}, u32[]{:S(2)}, u32[]{:S(2)}) collective-permute-start(bf16[128,2304]{1,0:T(8,128)(2,1)S(1)} %add_convert_fusion.8), channel_id=1, source_target_pairs={{0,4},{8,0},{16,8},{24,16},{28,24},{20,28},{12,20},{4,12},{1,5},{9... | collective-permute-start | bytes 1769480 | tf_op jit(solution)/shard_map/ppermute | solution.py:26
  428.9 16.1 %collective-permute-start.60 = (bf16[128,2304]{1,0:T(8,128)(2,1)}, bf16[128,2304]{1,0:T(8,128)(2,1)}, u32[]{:S(2)}, u32[]{:S(2)}) collective-permute-start(bf16[128,2304]{1,0:T(8,128)(2,1)} %get-tuple-element.899.d_attn_ref), channel_id=1, source_target_pairs={{0,2},{1,3},{2,0},{3,1},{4,6},{5,7},{6,4},{7,5},{8,10},{9,11},{10,... | collective-permute-start | bytes 1769480 | tf_op jit(solution)/shard_map/ppermute | solution.py:103
  445.0 118.2 %reduce-scatter.6.cloned.1.call-start = ((), (), s32[]{:S(2)}) async-start(), calls=%async_computation.6 | async-start | bytes 6635520 | tf_op jit(solution)/shard_map/reduce_scatter | solution.py:860
  470.6 13.2 %collective-permute-start.65 = (bf16[2,4,128,256]{3,2,1,0:T(8,128)(2,1)}, bf16[2,4,128,256]{3,2,1,0:T(8,128)(2,1)}, u32[]{:S(2)}, u32[]{:S(2)}) collective-permute-start(bf16[2,4,128,256]{3,2,1,0:T(8,128)(2,1)} %add_convert_fusion.23), channel_id=1, source_target_pairs={{0,8},{8,16},{16,24},{24,28},{28,20},{20,12},{12,4},{4,0},{1,9},{9... | collective-permute-start | bytes 1572872 | tf_op jit(solution)/shard_map/ppermute | solution.py:26
  470.9 13.1 %collective-permute-start.66 = (bf16[2,4,128,256]{3,2,1,0:T(8,128)(2,1)}, bf16[2,4,128,256]{3,2,1,0:T(8,128)(2,1)}, u32[]{:S(2)}, u32[]{:S(2)}) collective-permute-start(bf16[2,4,128,256]{3,2,1,0:T(8,128)(2,1)} %add_convert_fusion.22), channel_id=1, source_target_pairs={{0,4},{8,0},{16,8},{24,16},{28,24},{20,28},{12,20},{4,12},{1,5},{9... | collective-permute-start | bytes 1572872 | tf_op jit(solution)/shard_map/ppermute | solution.py:26
  488.0 131.0 %reduce-scatter.8.cloned.1.call-start = ((), (), s32[]{:S(2)}) async-start(), calls=%async_computation.7 | async-start | bytes 6635520 | tf_op jit(solution)/shard_map/reduce_scatter | solution.py:860
  488.1 12.7 %collective-permute-start.67 = (bf16[2,4,128,256]{3,2,1,0:T(8,128)(2,1)}, bf16[2,4,128,256]{3,2,1,0:T(8,128)(2,1)}, u32[]{:S(2)}, u32[]{:S(2)}) collective-permute-start(bf16[2,4,128,256]{3,2,1,0:T(8,128)(2,1)} %add_convert_fusion.21), channel_id=1, source_target_pairs={{0,8},{8,16},{16,24},{24,28},{28,20},{20,12},{12,4},{4,0},{1,9},{9... | collective-permute-start | bytes 1572872 | tf_op jit(solution)/shard_map/ppermute | solution.py:26
  488.7 12.3 %collective-permute-start.68 = (bf16[2,4,128,256]{3,2,1,0:T(8,128)(2,1)}, bf16[2,4,128,256]{3,2,1,0:T(8,128)(2,1)}, u32[]{:S(2)}, u32[]{:S(2)}) collective-permute-start(bf16[2,4,128,256]{3,2,1,0:T(8,128)(2,1)} %add_convert_fusion.20), channel_id=1, source_target_pairs={{0,4},{8,0},{16,8},{24,16},{28,24},{20,28},{12,20},{4,12},{1,5},{9... | collective-permute-start | bytes 1572872 | tf_op jit(solution)/shard_map/ppermute | solution.py:26
  503.5 11.2 %collective-permute-start.69 = (bf16[2,4,128,256]{3,2,1,0:T(8,128)(2,1)S(1)}, bf16[2,4,128,256]{3,2,1,0:T(8,128)(2,1)S(1)}, u32[]{:S(2)}, u32[]{:S(2)}) collective-permute-start(bf16[2,4,128,256]{3,2,1,0:T(8,128)(2,1)S(1)} %add_convert_fusion.19), channel_id=1, source_target_pairs={{0,8},{8,16},{16,24},{24,28},{28,20},{20,12},{12,4},{4,0},{1,9},{9... | collective-permute-start | bytes 1572872 | tf_op jit(solution)/shard_map/ppermute | solution.py:26
  504.6 11.0 %collective-permute-start.70 = (bf16[2,4,128,256]{3,2,1,0:T(8,128)(2,1)S(1)}, bf16[2,4,128,256]{3,2,1,0:T(8,128)(2,1)}, u32[]{:S(2)}, u32[]{:S(2)}) collective-permute-start(bf16[2,4,128,256]{3,2,1,0:T(8,128)(2,1)S(1)} %add_convert_fusion.18), channel_id=1, source_target_pairs={{0,4},{8,0},{16,8},{24,16},{28,24},{20,28},{12,20},{4,12},{1,5},{9... | collective-permute-start | bytes 1572872 | tf_op jit(solution)/shard_map/ppermute | solution.py:26
  523.3 14.4 %collective-permute-start.71 = (bf16[96,2304]{1,0:T(8,128)(2,1)}, bf16[96,2304]{1,0:T(8,128)(2,1)S(1)}, u32[]{:S(2)}, u32[]{:S(2)}) collective-permute-start(bf16[96,2304]{1,0:T(8,128)(2,1)} %get-tuple-element.1093), channel_id=1, source_target_pairs={{0,8},{8,16},{16,24},{24,28},{28,20},{20,12},{12,4},{4,0},{1,9},{9... | collective-permute-start | bytes 1327112 | tf_op jit(solution)/shard_map/ppermute | solution.py:26
  524.0 13.8 %collective-permute-start.72 = (bf16[96,2304]{1,0:T(8,128)(2,1)}, bf16[96,2304]{1,0:T(8,128)(2,1)S(1)}, u32[]{:S(2)}, u32[]{:S(2)}) collective-permute-start(bf16[96,2304]{1,0:T(8,128)(2,1)} %get-tuple-element.1094), channel_id=1, source_target_pairs={{0,4},{8,0},{16,8},{24,16},{28,24},{20,28},{12,20},{4,12},{1,5},{9... | collective-permute-start | bytes 1327112 | tf_op jit(solution)/shard_map/ppermute | solution.py:26
  540.2 23.0 %collective-permute-start.75 = (bf16[256,2304]{1,0:T(8,128)(2,1)}, bf16[256,2304]{1,0:T(8,128)(2,1)S(1)}, u32[]{:S(2)}, u32[]{:S(2)}) collective-permute-start(bf16[256,2304]{1,0:T(8,128)(2,1)} %get-tuple-element.1130), channel_id=1, source_target_pairs={{0,1},{1,0},{2,3},{3,2},{4,5},{5,4},{6,7},{7,6},{8,9},{9,8},{10,11... | collective-permute-start | bytes 3538952 | tf_op jit(solution)/shard_map/ppermute | solution.py:108
  540.5 21.7 %collective-permute-start.73 = (bf16[192,2304]{1,0:T(8,128)(2,1)S(1)}, bf16[192,2304]{1,0:T(8,128)(2,1)S(1)}, u32[]{:S(2)}, u32[]{:S(2)}) collective-permute-start(bf16[192,2304]{1,0:T(8,128)(2,1)S(1)} %add_convert_fusion.5), channel_id=1, source_target_pairs={{0,8},{8,16},{16,24},{24,28},{28,20},{20,12},{12,4},{4,0},{1,9},{9... | collective-permute-start | bytes 2654216 | tf_op jit(solution)/shard_map/ppermute | solution.py:26
  541.1 22.1 %collective-permute-start.74 = (bf16[192,2304]{1,0:T(8,128)(2,1)S(1)}, bf16[192,2304]{1,0:T(8,128)(2,1)}, u32[]{:S(2)}, u32[]{:S(2)}) collective-permute-start(bf16[192,2304]{1,0:T(8,128)(2,1)S(1)} %add_convert_fusion.4), channel_id=1, source_target_pairs={{0,4},{8,0},{16,8},{24,16},{28,24},{20,28},{12,20},{4,12},{1,5},{9... | collective-permute-start | bytes 2654216 | tf_op jit(solution)/shard_map/ppermute | solution.py:26
  570.2 25.9 %collective-permute-start.81 = (bf16[128,2304]{1,0:T(8,128)(2,1)S(1)}, bf16[128,2304]{1,0:T(8,128)(2,1)S(1)}, u32[]{:S(2)}, u32[]{:S(2)}) collective-permute-start(bf16[128,2304]{1,0:T(8,128)(2,1)S(1)} %slice.230), channel_id=1, source_target_pairs={{0,2},{1,3},{2,0},{3,1},{4,6},{5,7},{6,4},{7,5},{8,10},{9,11},{10,... | collective-permute-start | bytes 1769480 | tf_op jit(solution)/shard_map/ppermute | solution.py:103
  571.3 25.0 %collective-permute-start.79 = (bf16[192,2304]{1,0:T(8,128)(2,1)}, bf16[192,2304]{1,0:T(8,128)(2,1)S(1)}, u32[]{:S(2)}, u32[]{:S(2)}) collective-permute-start(bf16[192,2304]{1,0:T(8,128)(2,1)} %add_convert_fusion.3), channel_id=1, source_target_pairs={{0,8},{8,16},{16,24},{24,28},{28,20},{20,12},{12,4},{4,0},{1,9},{9... | collective-permute-start | bytes 2654216 | tf_op jit(solution)/shard_map/ppermute | solution.py:26
  575.6 20.7 %collective-permute-start.80 = (bf16[192,2304]{1,0:T(8,128)(2,1)S(1)}, bf16[192,2304]{1,0:T(8,128)(2,1)S(1)}, u32[]{:S(2)}, u32[]{:S(2)}) collective-permute-start(bf16[192,2304]{1,0:T(8,128)(2,1)S(1)} %add_convert_fusion.2), channel_id=1, source_target_pairs={{0,4},{8,0},{16,8},{24,16},{28,24},{20,28},{12,20},{4,12},{1,5},{9... | collective-permute-start | bytes 2654216 | tf_op jit(solution)/shard_map/ppermute | solution.py:26
  598.7 17.2 %collective-permute-start.85 = (bf16[192,2304]{1,0:T(8,128)(2,1)S(1)}, bf16[192,2304]{1,0:T(8,128)(2,1)S(1)}, u32[]{:S(2)}, u32[]{:S(2)}) collective-permute-start(bf16[192,2304]{1,0:T(8,128)(2,1)S(1)} %add_convert_fusion.1), channel_id=1, source_target_pairs={{0,8},{8,16},{16,24},{24,28},{28,20},{20,12},{12,4},{4,0},{1,9},{9... | collective-permute-start | bytes 2654216 | tf_op jit(solution)/shard_map/ppermute | solution.py:26
  600.1 17.4 %collective-permute-start.86 = (bf16[192,2304]{1,0:T(8,128)(2,1)S(1)}, bf16[192,2304]{1,0:T(8,128)(2,1)S(1)}, u32[]{:S(2)}, u32[]{:S(2)}) collective-permute-start(bf16[192,2304]{1,0:T(8,128)(2,1)S(1)} %add_convert_fusion), channel_id=1, source_target_pairs={{0,4},{8,0},{16,8},{24,16},{28,24},{20,28},{12,20},{4,12},{1,5},{9... | collective-permute-start | bytes 2654216 | tf_op jit(solution)/shard_map/ppermute | solution.py:26
  (157 other events, 1643.3 us)
Sparse Core Ops, SparseCore 0:
  36.5 71.2 all-gather.2
  139.0 40.4 all-gather.4
  445.1 49.2 reduce-scatter.3
  497.0 53.3 reduce-scatter.5
  552.8 61.3 reduce-scatter.7

commit v3 on v2

--- a/solution.py
+++ b/solution.py
@@ -43,18 +43,21 @@
     return lax.optimization_barrier(values)
 
 
+def ring_moves(i, behind, ahead):
+    if i < lax.axis_size("ctx") // 2 - 1:
+        return [ring_hop(behind, 1), ring_hop(ahead, -1)]
+    middle = behind.shape[0] // 2
+    return [ring_hop(behind[:middle], 1), ring_hop(ahead[middle:], -1)]
+
+
 def ring_gather(own, use, side=None, state=(), first=()):
     half = lax.axis_size("ctx") // 2
-    middle = own.shape[0] // 2
     own, state, result = tie(own, state, first)
     blocks, results = [own], []
     behind = ahead = own
     for i in range(half):
         last = i == half - 1
-        if last:
-            moved = [ring_hop(behind[:middle], 1), ring_hop(ahead[middle:], -1)]
-        else:
-            moved = [ring_hop(behind, 1), ring_hop(ahead, -1)]
+        moved = ring_moves(i, behind, ahead)
         result = use(i, blocks, result)
         if side:
             state = side(i, state)
@@ -77,6 +80,33 @@
         (to_ahead.astype(F32) + behind).astype(BF16),
         (to_behind.astype(F32) + ahead).astype(BF16),
     ]
+
+
+def add_kernel(halves, to_behind_ref, to_ahead_ref, behind_ref, ahead_ref, ahead_out, behind_out):
+    behind, ahead = behind_ref[...].astype(F32), ahead_ref[...].astype(F32)
+    if halves:
+        first = pl.program_id(0) == 0
+        behind, ahead = jnp.where(first, behind, 0.0), jnp.where(first, 0.0, ahead)
+    ahead_out[...] = (to_ahead_ref[...].astype(F32) + behind).astype(BF16)
+    behind_out[...] = (to_behind_ref[...].astype(F32) + ahead).astype(BF16)
+
+
+def add_terms_here(terms, moved):
+    whole, part = terms[0].shape, moved[0].shape
+    block = (whole[0] // 2, *whole[1:])
+    rest = (0,) * (len(whole) - 1)
+    halves = whole != part
+    here = pl.BlockSpec(block, lambda i: (i, *rest))
+    there = pl.BlockSpec(block, lambda i: (0, *rest)) if halves else here
+    return pl.pallas_call(
+        functools.partial(add_kernel, halves),
+        grid=(2,),
+        out_shape=[jax.ShapeDtypeStruct(whole, BF16)] * 2,
+        in_specs=[here, here, there, there],
+        out_specs=[here, here],
+        compiler_params=ROOMY,
+        cost_estimate=FREE,
+    )(*terms, *moved)
 
 
 def ring_scatter(term, operands, side=None, state=(), join=add_terms):
@@ -437,25 +467,28 @@
     )(*rows, *(weight for weight, _ in weights), *units)
 
 
-def out_kernel(*refs):
-    ins, weights, out_ref = refs[: len(refs) // 2], refs[len(refs) // 2 : -1], refs[-1]
+def out_kernel(pairs, *refs):
+    ins, weights, outs = refs[:pairs], refs[pairs : 2 * pairs], refs[2 * pairs :]
     total = sum(nn(a[...], w[...].reshape(w.shape[-2:])) for a, w in zip(ins, weights))
-    out_ref[...] = total.astype(out_ref.dtype)
-
-
-def out_call(ins, weights, rows, at, out):
+    rows = outs[0].shape[0]
+    for n, out in enumerate(outs):
+        out[...] = total[n * rows : (n + 1) * rows].astype(out.dtype)
+
+
+def out_call(ins, weights, rows, out):
     count, width = weights[0][0].shape[-2:]
+    blocks = ins[0].shape[0] // rows
     tile = tile_of(width, 768)
     return pl.pallas_call(
-        out_kernel,
+        functools.partial(out_kernel, len(ins)),
         grid=(width // tile,),
-        out_shape=jax.ShapeDtypeStruct((rows, width), out),
-        in_specs=[pl.BlockSpec((rows, count), lambda i: (at, 0))] * len(ins)
+        out_shape=[jax.ShapeDtypeStruct((rows, width), out)] * blocks,
+        in_specs=[pl.BlockSpec(a.shape, lambda i: (0, 0)) for a in ins]
         + [
             pl.BlockSpec((1,) * len(lead) + (count, tile), lambda i, lead=lead: (*lead, 0, i))
             for _, lead in weights
         ],
-        out_specs=pl.BlockSpec((rows, tile), lambda i: (0, i)),
+        out_specs=[pl.BlockSpec((rows, tile), lambda i: (0, i))] * blocks,
         compiler_params=pltpu.CompilerParams(vmem_limit_bytes=24 << 20),
         cost_estimate=FREE,
     )(*ins, *(weight for weight, _ in weights))
@@ -692,18 +725,17 @@
     cols = [weight_query.shape[1], weight_key.shape[1], weight_value.shape[1]]
     cols.append(weight_output.shape[0])
     cuts = [sum(cols[:i]) for i in range(len(cols) + 1)]
-    own = jnp.concatenate([weight_query.T, weight_key.T, weight_value.T, weight_output], axis=0)
-
-    def place_blocks(i, blocks, placed):
-        if i == half_ring:
-            member = [ring_member(i)]
-            return [
-                part
-                for n, block in enumerate(blocks)
-                for part in place_rows(placed[2 * n : 2 * n + 2], [block], member, cols[2 * n : 2 * n + 2])
-            ]
-        ends = [i] if i == 0 else [-i, i]
-        return list(place_rows(list(placed), list(blocks), [ring_member(k) for k in ends], cols))
+
+    def place_group(i, blocks, fulls, cols):
+        ends = [0] if i == 0 else [-i, i]
+        return list(place_rows(list(fulls), list(blocks), [ring_member(k) for k in ends], cols))
+
+    def place_far(blocks, fulls, cols):
+        member = [ring_member(half_ring)]
+        return [
+            place_rows([full], [block], member, [c])[0]
+            for full, block, c in zip(fulls, blocks, cols)
+        ]
 
     flying = {}
 
@@ -712,7 +744,8 @@
             gate_own, up_own = state
             rows = [block_in[0], far_hop(block_in[0]), near_hop(block_in[0])]
             own = jnp.stack([gate_own.T, up_own.T])
-            return rows, add_from(gains, "fsdp", low_masks()), own
+            rows[2], part = tie(rows[2], gains)
+            return rows, add_from(part, "fsdp", low_masks()), own
         if i == 1:
             rows, sums, own = state
             flying["gate_up"] = lax.all_gather(own, "fsdp", axis=1, tiled=True)
@@ -728,20 +761,33 @@
             return rows, scales, (long * scales * sums[0]).astype(BF16), sums
         return state
 
-    results, (all_rows, scales, normed_one, gains) = ring_gather(
-        own,
-        place_blocks,
-        prepare,
-        (weight_gate, weight_up),
-        blank([(c * n_ctx, width) for c in cols]),
-    )
-    query_full, key_full, value_full, output_full = results[-1]
+    kv_cols, qo_cols = cols[1:3], [cols[0], cols[3]]
+    kv_own = jnp.concatenate([weight_key.T, weight_value.T], axis=0)
+    qo_own = jnp.concatenate([weight_query.T, weight_output], axis=0)
+    kv_own, qo_own, state = tie(kv_own, qo_own, (weight_gate, weight_up))
+    kv, qo, kv_group, qo_group = [kv_own] * 2, [qo_own] * 2, [kv_own], [qo_own]
+    kv_full = blank([(c * n_ctx, width) for c in kv_cols])
+    qo_full = blank([(c * n_ctx, width) for c in qo_cols])
+    late = half_ring - 2
+    for i in range(half_ring):
+        kv_moved = ring_moves(i, *kv)
+        qo_moved = ring_moves(i, *qo) if i < late else qo
+        kv_full = place_group(i, kv_group, kv_full, kv_cols)
+        if i <= late:
+            qo_full = place_group(i, qo_group, qo_full, qo_cols)
+        state = prepare(i, state)
+        kv_moved, qo_moved, kv_full, qo_full, state = tie(kv_moved, qo_moved, kv_full, qo_full, state)
+        kv = kv_group = kv_moved
+        qo = qo_group = qo_moved
+    all_rows, scales, normed_one, gains = state
     gain_one, gain_two, gain_three, gain_four = gains[0], gains[1], gains[2], gains[3]
 
     seqs = n_fsdp
-    group = query_full.shape[0] // HEAD_DIM
+    group = weight_query.shape[1] * n_ctx // HEAD_DIM
 
     by_rows = pl.BlockSpec((tokens, group * HEAD_DIM), lambda i: (i, 0))
+    qo_moved = ring_moves(late, *qo)
+    key_full, value_full = place_far(kv, kv_full, kv_cols)
     both_own = project(
         keys_kernel,
         normed_one,
@@ -751,13 +797,19 @@
         (2, seqs, tokens, HEAD_DIM),
         pl.BlockSpec((2, 1, tokens, HEAD_DIM), lambda i: (0, i, 0, 0)),
     ).reshape(2 * seqs, tokens, HEAD_DIM)
+    qo, both_own = tie(qo_moved, both_own)
 
     def take_keys(i, blocks, both):
         return put_blocks(both, list(blocks), max(2 * i - 1, 0), 0 if i == half_ring else 1)
 
     def keys_side(i, state):
         if i == 0:
-            return project(
+            qo, qo_full = state
+            moved = ring_moves(half_ring - 1, *qo)
+            return moved, place_group(half_ring - 1, qo, qo_full, qo_cols)
+        if i == 1:
+            query_full, output_full = place_far(*state, qo_cols)
+            queries = project(
                 queries_kernel,
                 normed_one,
                 [query_full],
@@ -766,20 +818,19 @@
                 (seqs * tokens, group * HEAD_DIM),
                 by_rows,
             )
-        if i == 1:
-            return state, flying.pop("gate_up"), weight_down
+            return queries, query_full, output_full, flying.pop("gate_up"), weight_down
         if i == 2:
-            queries, gate_up, own = state
+            *kept, own = state
             flying["down"] = lax.all_gather(own, "fsdp", axis=0, tiled=True)
-            return queries, gate_up
+            return kept
         return state
 
     count = tokens * n_ctx
-    results, (queries, gate_up) = ring_gather(
+    results, (queries, query_full, output_full, gate_up) = ring_gather(
         both_own,
         take_keys,
         keys_side,
-        (),
+        (qo, qo_full),
         blank([(2 * seqs, count, HEAD_DIM)])[0],
     )
     both = results[-1]
@@ -828,12 +879,9 @@
     values_act, slopes_act, hidden = zip(*(parts for parts, _ in results))
     normed_two = [block for _, blocks in results for block in blocks]
 
-    def apart(flat):
-        return [flat[n : n + tokens] for n in range(0, flat.shape[0], tokens)]
-
     def down_term(i, hidden_part):
         out = BF16 if i else F32
-        return apart(out_call([hidden_part], [(down_full, ())], hidden_part.shape[0], 0, out))
+        return out_call([hidden_part], [(down_full, ())], tokens, out)
 
     mlp_parts, _ = ring_scatter(down_term, hidden)
 
@@ -862,15 +910,13 @@
     def grad_up_work(i, state):
         if i == half_ring - 2:
             return state, weight_grad(*state, (0, 2, None))
-        if i == half_ring - 3:
-            return weight_grad(*state[0], (2, 1, state[1]))
         return state
 
     def rows_term(i, grads):
         out = BF16 if i else F32
-        return apart(out_call(grads, [gate_weight, up_weight], grads[0].shape[0], 0, out))
-
-    d_normed_parts, grad_up_full = ring_scatter(
+        return out_call(list(grads), [gate_weight, up_weight], tokens, out)
+
+    d_normed_parts, (sides, grad_up_part) = ring_scatter(
         rows_term,
         list(zip(d_gate, d_up)),
         grad_up_work,
@@ -909,6 +955,8 @@
 
     d_attn_far, d_attn_near = far_hop(d_attn_own), near_hop(d_attn_own)
     earlier = attend_back(0, [d_attn_own, d_attn_near], ())
+    grad_up_part, _ = tie(grad_up_part, d_attn_near)
+    grad_up_full = weight_grad(*sides, (2, 1, grad_up_part))
     d_attn_far, earlier, grad_up_full = tie(d_attn_far, earlier, grad_up_full)
     flying["up"] = to_owner(grad_up_full)
     d_attn_last = near_hop(d_attn_far)
@@ -939,6 +987,7 @@
         [both_of(distance) for distance in range(half_ring + 1)],
         query_work,
         ((d_gate, normed_two), (hidden, d_mlp)),
+        add_terms_here,
     )
     grad_up, grad_query_full, grad_output_full = state
     d_key_raw, d_value_raw, grad_key_full, grad_value_full = keys_back(

time: 639 us -> 628 us (0.983)
  waiting for transfers between devices: 238 us -> 215 us
  Pallas kernels: 189 us -> 206 us
  other arithmetic: 44 us -> 33 us
  starting transfers between devices: 89 us -> 98.1 us
    ppermute x14, waiting for transfers between devices: 25.9 us -> 0.04 us  [add_from(): return sum((lax.ppermute(block, axis, route) for route in routes), block)]
    ppermute x64 -> x72, waiting for transfers between devices: 156 us -> 174 us  [ring_hop(): lax.ppermute(block, 'ctx', [(order[i], order[(i + step) % size]) for i in...]
    ppermute x4, waiting for transfers between devices: 50.1 us -> 35.9 us  [far_hop(): lax.ppermute(block, 'fsdp', [(i, i ^ size // 2) for i in range(size)])]
    pallas_call x6 -> x12, Pallas kernels: 16.6 us -> 27.5 us  [place_rows(): pl.pallas_call(functools.partial(place_kernel, cols, n_blocks), grid_spec...]
    ppermute x64 -> x72, starting transfers between devices: 67 us -> 75.7 us  [ring_hop(): lax.ppermute(block, 'ctx', [(order[i], order[(i + step) % size]) for i in...]
    pallas_call x10 -> x13, Pallas kernels: 29.5 us -> 36.6 us  [the longest x10 29.6 us: out_call(): pl.pallas_call(functools.partial(out_kernel, len(ins)), grid=(width // ti...]
    unnamed x263 -> x271, local copies, waits for them, and re-layouts: 29.2 us -> 26 us
  transfers between devices with their start and end apart: 93 -> 101, of which waited for: 56 -> 52; matrix products, arithmetic and copies ran while one was open for 10% -> 8% of each run, Pallas kernels for 27% -> 31%
where the time goes in v3:
time: 628 us; the launch traced here: 619 us
  waiting for transfers between devices  215 us (34%)
  Pallas kernels  206 us (33%)
  starting transfers between devices  98.1 us (16%)
  local copies, waits for them, and re-layouts  41.3 us (7%)
  other arithmetic  33 us (5%)
  between operations  15.9 us (3%)
  matrix products  9.79 us (2%)
    ppermute x72, waiting for transfers between devices, ring_hop(): lax.ppermute(block, 'ctx', [(order[i], order[(i + step) % size]) for i in...  174 us
    ppermute x72, starting transfers between devices, ring_hop(): lax.ppermute(block, 'ctx', [(order[i], order[(i + step) % size]) for i in...  75.7 us
    pallas_call x4, Pallas kernels, weight_grad(): pl.pallas_call(functools.partial(weight_grad_kernel, len(units), len(rows...  35.9 us
    ppermute x4, waiting for transfers between devices, far_hop(): lax.ppermute(block, 'fsdp', [(i, i ^ size // 2) for i in range(size)])  35.9 us
    pallas_call x10, Pallas kernels, unit_call(): pl.pallas_call(functools.partial(kernel, len(rows)), grid=(count // tile,...  34.2 us
    pallas_call x10, Pallas kernels, out_call(): pl.pallas_call(functools.partial(out_kernel, len(ins)), grid=(width // ti...  29.6 us
    pallas_call x12, Pallas kernels, place_rows(): pl.pallas_call(functools.partial(place_kernel, cols, n_blocks), grid_spec...  27.5 us
    unnamed x271, local copies, waits for them, and re-layouts  26 us
  transfers between devices with their start and end apart: 101, of which 52 were waited for; matrix products, arithmetic and copies ran while one was open for 8% of the time, Pallas kernels for 31%

profile of v3, /device:TPU:0, one launch (start us, length us, event | category | flops | bytes accessed | tf_op | source)
XLA Modules:
  0.0 619.4 jit_solution(17335209168536162242)
XLA Ops:
  10.6 2.6 collective-permute-start.2
  15.7 3.1 pad_maximum_fusion
  26.3 7.2 %collective-permute-done.refs_0_ = bf16[64,2304]{1,0:T(8,128)(2,1)S(1)} collective-permute-done((bf16[64,2304]{1,0:T(8,128)(2,1)S(1)}, bf16[64,2304]{1,0:T(8,128)(2,1)S(1)}, u32[]{:S(2)}, u32[]{:S(2)}) %collective-permute-start) | collective-permute-done | bytes 294944 | tf_op jit(solution)/shard_map/ppermute | solution.py:26
  35.0 4.7 collective-permute-done.4
  46.7 3.2 shard_map.242
  49.9 2.7 shard_map.241
  55.2 11.1 %collective-permute-done.10.refs_1_ = bf16[64,2304]{1,0:T(8,128)(2,1)} collective-permute-done((bf16[64,2304]{1,0:T(8,128)(2,1)}, bf16[64,2304]{1,0:T(8,128)(2,1)}, u32[]{:S(2)}, u32[]{:S(2)}) %collective-permute-start.10) | collective-permute-done | bytes 294944 | tf_op jit(solution)/shard_map/ppermute | solution.py:26
  66.4 2.6 collective-permute-start.19
  72.4 2.7 shard_map.243
  75.1 3.0 shard_map.244
  85.3 2.7 shard_map.245
  99.6 4.2 shard_map.248
  113.2 3.0 shard_map.251
  116.2 4.6 collective-permute-done.26.refs_0_
  128.8 3.6 shard_map.254.queries_ref
  142.5 7.8 %collective-permute-done.30.refs_0_ = bf16[8,128,256]{2,1,0:T(8,128)(2,1)S(1)} collective-permute-done((bf16[8,128,256]{2,1,0:T(8,128)(2,1)}, bf16[8,128,256]{2,1,0:T(8,128)(2,1)S(1)}, u32[]{:S(2)}, u32[]{:S(2)}) %collective-permute-start.30) | collective-permute-done | bytes 524320 | tf_op jit(solution)/shard_map/ppermute | solution.py:26
  161.3 5.4 shard_map.259
  166.8 2.6 fusion.40
  169.7 2.8 collective-permute-done.34
  175.6 12.6 %collective-permute-done.35.moved_ref = bf16[128,2304]{1,0:T(8,128)(2,1)S(1)} collective-permute-done((bf16[128,2304]{1,0:T(8,128)(2,1)S(1)}, bf16[128,2304]{1,0:T(8,128)(2,1)S(1)}, u32[]{:S(2)}, u32[]{:S(2)}) %collective-permute-start.35) | collective-permute-done | bytes 589856 | tf_op jit(solution)/shard_map/ppermute | solution.py:133
  192.0 3.5 shard_map.261
  197.9 6.7 %collective-permute-done.36.refs_0_.refs_6_ = bf16[128,2304]{1,0:T(8,128)(2,1)S(1)} collective-permute-done((bf16[128,2304]{1,0:T(8,128)(2,1)S(1)}, bf16[128,2304]{1,0:T(8,128)(2,1)S(1)}, u32[]{:S(2)}, u32[]{:S(2)}) %collective-permute-start.36) | collective-permute-done | bytes 589856 | tf_op jit(solution)/shard_map/ppermute | solution.py:26
  207.2 4.0 copy-done
  211.2 5.6 shard_map.262
  222.7 4.5 shard_map.263
  227.3 6.0 collective-permute-done.40.refs_0_.refs_10_
  236.6 4.5 shard_map.264
  243.1 3.4 shard_map.265
  250.5 2.5 shard_map.267
  253.0 4.8 collective-permute-done.44
  264.3 9.4 %collective-permute-done.46 = bf16[128,2304]{1,0:T(8,128)(2,1)S(1)} collective-permute-done((bf16[128,2304]{1,0:T(8,128)(2,1)S(1)}, bf16[128,2304]{1,0:T(8,128)(2,1)S(1)}, u32[]{:S(2)}, u32[]{:S(2)}) %collective-permute-start.46) | collective-permute-done | bytes 589856 | tf_op jit(solution)/shard_map/ppermute | solution.py:26
  279.5 10.0 %collective-permute-done.48 = bf16[128,2304]{1,0:T(8,128)(2,1)S(1)} collective-permute-done((bf16[128,2304]{1,0:T(8,128)(2,1)S(1)}, bf16[128,2304]{1,0:T(8,128)(2,1)S(1)}, u32[]{:S(2)}, u32[]{:S(2)}) %collective-permute-start.48) | collective-permute-done | bytes 589856 | tf_op jit(solution)/shard_map/ppermute | solution.py:26
  295.6 12.1 %collective-permute-done.50.behind_ref = bf16[128,2304]{1,0:T(8,128)(2,1)S(1)} collective-permute-done((bf16[128,2304]{1,0:T(8,128)(2,1)S(1)}, bf16[128,2304]{1,0:T(8,128)(2,1)S(1)}, u32[]{:S(2)}, u32[]{:S(2)}) %collective-permute-start.50) | collective-permute-done | bytes 589856 | tf_op jit(solution)/shard_map/ppermute | solution.py:26
  313.8 9.8 %collective-permute-done.52.refs_0_.refs_6_ = bf16[128,2304]{1,0:T(8,128)(2,1)S(1)} collective-permute-done((bf16[128,2304]{1,0:T(8,128)(2,1)S(1)}, bf16[128,2304]{1,0:T(8,128)(2,1)S(1)}, u32[]{:S(2)}, u32[]{:S(2)}) %collective-permute-start.52) | collective-permute-done | bytes 589856 | tf_op jit(solution)/shard_map/ppermute | solution.py:26
  325.7 2.7 shard_map.273
  329.3 7.7 %collective-permute-done.54.refs_0_.refs_8_ = bf16[128,2304]{1,0:T(8,128)(2,1)S(1)} collective-permute-done((bf16[128,2304]{1,0:T(8,128)(2,1)S(1)}, bf16[128,2304]{1,0:T(8,128)(2,1)S(1)}, u32[]{:S(2)}, u32[]{:S(2)}) %collective-permute-start.54) | collective-permute-done | bytes 589856 | tf_op jit(solution)/shard_map/ppermute | solution.py:26
  339.1 2.7 shard_map.274
  341.9 5.1 collective-permute-done.56.refs_0_.refs_10_
  350.7 2.7 shard_map.275
  359.4 2.8 shard_map.277
  364.3 4.3 shard_map.278
  374.9 4.3 shard_map.279
  379.3 8.6 %shard_map.280.refs_14_ = bf16[1152,2304]{1,0:T(8,128)(2,1)} custom-call(bf16[128,1152]{1,0:T(8,128)(2,1)} %copy-done.25, bf16[256,1152]{1,0:T(8,128)(2,1)} %copy-done.15, bf16[256,1152]{1,0:T(8,128)(2,1)} %copy-done.17, bf16[256,1152]{1,0:T(8,128)(2,1)} %copy-done.18, bf16[128,1152]{1,0:T(8,128)(2,1)} %copy-done.27, bf16[128,2304]{1,0:T(8,128)(2,1)} %copy-done.10, ...), custom_call_target="tpu_custom_call" | custom-call | tf_op jit(solution)/shard_map/pallas_call | solution.py:415
  392.2 4.0 copy-done.1
  396.2 4.4 shard_map.281
  404.7 2.9 shard_map.282.term_ref
  407.6 5.0 collective-permute-done.66.behind_ref
  420.4 5.9 shard_map.285
  427.6 8.8 %shard_map.284 = (bf16[512,512]{1,0:T(8,128)(2,1)}, bf16[2,4,128,256]{3,2,1,0:T(8,128)(2,1)}, bf16[2,4,128,256]{3,2,1,0:T(8,128)(2,1)}, bf16[2,4,128,256]{3,2,1,...) custom-call(bf16[8,1024,256]{2,1,0:T(8,128)(2,1)} %shard_map.258.key, ...), custom_call_target="tpu_custom_call" | custom-call | tf_op jit(solution)/shard_map/pallas_call | solution.py:666
  439.8 9.1 %shard_map.286 = (bf16[512,512]{1,0:T(8,128)(2,1)}, bf16[2,4,128,256]{3,2,1,0:T(8,128)(2,1)}, bf16[2,4,128,256]{3,2,1,0:T(8,128)(2,1)}, bf16[2,4,128,256]{3,2,1,...) custom-call(bf16[8,1024,256]{2,1,0:T(8,128)(2,1)} %shard_map.258.key, ...), custom_call_target="tpu_custom_call", output_to_operand_aliasing={{0}: (10, {}), {1}: (11, {}), {2}: (12, {}), {3}: (13, {}),... | custom-call | tf_op jit(solution)/shard_map/pallas_call | solution.py:666
  451.0 6.8 %collective-permute-done.71.behind_ref = bf16[1,4,128,256]{3,2,1,0:T(8,128)(2,1)S(1)} collective-permute-done((bf16[1,4,128,256]{3,2,1,0:T(8,128)(2,1)}, bf16[1,4,128,256]{3,2,1,0:T(8,128)(2,1)S(1)}, u32[]{:S(2)}, u32[]{:S(2)}) %collective-permute-start.71) | collective-permute-done | bytes 262176 | tf_op jit(solution)/shard_map/ppermute | solution.py:26
  463.6 10.8 %shard_map.288 = bf16[1152,2304]{1,0:T(8,128)(2,1)} custom-call(bf16[128,1152]{1,0:T(8,128)(2,1)} %copy-done.55, bf16[256,1152]{1,0:T(8,128)(2,1)} %copy-done.37, bf16[256,1152]{1,0:T(8,128)(2,1)} %copy-done.38, bf16[256,1152]{1,0:T(8,128)(2,1)} %copy-done.39, bf16[128,1152]{1,0:T(8,128)(2,1)} %copy-done.57, bf16[128,2304]{1,0:T(8,128)(2,1)} %copy-done.10, ...), custom_call_target="tpu_custom_call" | custom-call | tf_op jit(solution)/shard_map/pallas_call | solution.py:415
  480.4 10.7 %shard_map.290 = bf16[1152,2304]{1,0:T(8,128)(2,1)} custom-call(bf16[128,1152]{1,0:T(8,128)(2,1)} %copy-done.46, bf16[256,1152]{1,0:T(8,128)(2,1)} %copy-done.29, bf16[256,1152]{1,0:T(8,128)(2,1)} %copy-done.30, bf16[256,1152]{1,0:T(8,128)(2,1)} %copy-done.31, bf16[128,1152]{1,0:T(8,128)(2,1)} %copy-done.48, bf16[128,2304]{1,0:T(8,128)(2,1)} %copy-done.32, ...), custom_call_target="tpu_custom_call" | custom-call | tf_op jit(solution)/shard_map/pallas_call | solution.py:415
  496.1 2.9 convolution_convert_fusion.1.refs_2_.refs_6_.refs_1_
  499.0 4.3 convolution_convert_fusion.refs_5_.refs_9_.refs_4_
  503.3 2.5 collective-permute-done.77.behind_ref
  506.4 5.3 shard_map.292
  517.2 2.8 shard_map.294
  520.0 7.4 %shard_map.295 = (f32[256,2304]{1,0:T(8,128)}, bf16[256,2304]{1,0:T(8,128)(2,1)}, f32[1,2304]{1,0:T(1,128)}) custom-call(bf16[512,512]{1,0:T(8,128)(2,1)} %get-tuple-element.1260.refs_0_, bf16[512,256]{1,0:T(8,128)(2,1)} %get-tuple-element.1261.refs_1_, bf16[512,256]{1,0:T(8,128)(2,1)} %get-tuple-element.1262.refs_2_, ...), custom_call_target="tpu_custom_call" | custom-call | tf_op jit(solution)/shard_map/pallas_call | solution.py:279
  534.6 2.7 shard_map.296
  537.4 15.2 %collective-permute-done.81 = bf16[192,2304]{1,0:T(8,128)(2,1)S(1)} collective-permute-done((bf16[192,2304]{1,0:T(8,128)(2,1)S(1)}, bf16[192,2304]{1,0:T(8,128)(2,1)S(1)}, u32[]{:S(2)}, u32[]{:S(2)}) %collective-permute-start.81) | collective-permute-done | bytes 884768 | tf_op jit(solution)/shard_map/ppermute | solution.py:26
  563.1 2.8 shard_map.297
  567.4 18.6 %collective-permute-done.89 = bf16[128,2304]{1,0:T(8,128)(2,1)S(1)} collective-permute-done((bf16[128,2304]{1,0:T(8,128)(2,1)S(1)}, bf16[128,2304]{1,0:T(8,128)(2,1)S(1)}, u32[]{:S(2)}, u32[]{:S(2)}) %collective-permute-start.89) | collective-permute-done | bytes 589856 | tf_op jit(solution)/shard_map/ppermute | solution.py:133
  595.4 9.9 %collective-permute-done.93 = bf16[192,2304]{1,0:T(8,128)(2,1)S(1)} collective-permute-done((bf16[192,2304]{1,0:T(8,128)(2,1)S(1)}, bf16[192,2304]{1,0:T(8,128)(2,1)S(1)}, u32[]{:S(2)}, u32[]{:S(2)}) %collective-permute-start.93) | collective-permute-done | bytes 884768 | tf_op jit(solution)/shard_map/ppermute | solution.py:26
  (578 shorter events, 240.6 us)
Async XLA Ops:
  7.2 130.0 %all-gather.3.cloned.1.call-start = ((), (), s32[]{:S(2)}) async-start(), calls=%async_computation.3 | async-start | bytes 13271040 | tf_op jit(solution)/shard_map/all_gather | solution.py:751
  10.6 24.4 %collective-permute-start.2 = (bf16[128,2304]{1,0:T(8,128)(2,1)S(1)}, bf16[128,2304]{1,0:T(8,128)(2,1)S(1)}, u32[]{:S(2)}, u32[]{:S(2)}) collective-permute-start(bf16[128,2304]{1,0:T(8,128)(2,1)S(1)} %pad_maximum_fusion.3.refs_0_), channel_id=1, source_target_pairs={{0,8},{8,16},{16,24},{24,28},{28,20},{20,12},{12,4},{4,0},{1,9},{9... | collective-permute-start | bytes 1769480 | tf_op jit(solution)/shard_map/ppermute | solution.py:26
  13.3 21.8 %collective-permute-start.3 = (bf16[128,2304]{1,0:T(8,128)(2,1)S(1)}, bf16[128,2304]{1,0:T(8,128)(2,1)}, u32[]{:S(2)}, u32[]{:S(2)}) collective-permute-start(bf16[128,2304]{1,0:T(8,128)(2,1)S(1)} %pad_maximum_fusion.3.refs_0_), channel_id=1, source_target_pairs={{0,4},{8,0},{16,8},{24,16},{28,24},{20,28},{12,20},{4,12},{1,5},{9... | collective-permute-start | bytes 1769480 | tf_op jit(solution)/shard_map/ppermute | solution.py:26
  24.5 15.2 %collective-permute-start.4 = (bf16[128,2304]{1,0:T(8,128)(2,1)S(1)}, bf16[128,2304]{1,0:T(8,128)(2,1)S(1)}, u32[]{:S(2)}, u32[]{:S(2)}) collective-permute-start(bf16[128,2304]{1,0:T(8,128)(2,1)S(1)} %bitcast.80), channel_id=1, source_target_pairs={{0,2},{1,3},{2,0},{3,1},{4,6},{5,7},{6,4},{7,5},{8,10},{9,11},{10,... | collective-permute-start | bytes 1769480 | tf_op jit(solution)/shard_map/ppermute | solution.py:133
  39.8 165.4 %all-gather.5.cloned.1.call-start = ((), (), s32[]{:S(2)}) async-start(), calls=%async_computation.4 | async-start | bytes 6635520 | tf_op jit(solution)/shard_map/all_gather | solution.py:824
  40.6 12.0 %collective-permute-start.14 = (f32[4,2304]{1,0:T(4,128)S(1)}, f32[4,2304]{1,0:T(4,128)S(1)}, u32[]{:S(2)}, u32[]{:S(2)}) collective-permute-start(f32[4,2304]{1,0:T(4,128)S(1)} %add_add_fusion.4), channel_id=1, source_target_pairs={{0,4},{4,0},{8,12},{12,8},{16,20},{20,16},{24,28},{28,24},{1,5},{5... | collective-permute-start | bytes 110600 | tf_op jit(solution)/shard_map/ppermute | solution.py:144
  42.2 11.9 %collective-permute-start.15 = (f32[4,2304]{1,0:T(4,128)S(1)}, f32[4,2304]{1,0:T(4,128)S(1)}, u32[]{:S(2)}, u32[]{:S(2)}) collective-permute-start(f32[4,2304]{1,0:T(4,128)S(1)} %add_add_fusion.4), channel_id=1, source_target_pairs={{0,8},{4,12},{8,0},{12,4},{16,24},{20,28},{24,16},{28,20},{1,9},{5... | collective-permute-start | bytes 110600 | tf_op jit(solution)/shard_map/ppermute | solution.py:144
  44.6 21.7 %collective-permute-start.11 = (bf16[128,2304]{1,0:T(8,128)(2,1)S(1)}, bf16[128,2304]{1,0:T(8,128)(2,1)}, u32[]{:S(2)}, u32[]{:S(2)}) collective-permute-start(bf16[128,2304]{1,0:T(8,128)(2,1)S(1)} %collective-permute-done.2.refs_0_), channel_id=1, source_target_pairs={{0,8},{8,16},{16,24},{24,28},{28,20},{20,12},{12,4},{4,0},{1,9},{9... | collective-permute-start | bytes 1769480 | tf_op jit(solution)/shard_map/ppermute | solution.py:26
  46.3 20.1 %collective-permute-start.12 = (bf16[128,2304]{1,0:T(8,128)(2,1)}, bf16[128,2304]{1,0:T(8,128)(2,1)}, u32[]{:S(2)}, u32[]{:S(2)}) collective-permute-start(bf16[128,2304]{1,0:T(8,128)(2,1)} %collective-permute-done.3.refs_1_), channel_id=1, source_target_pairs={{0,4},{8,0},{16,8},{24,16},{28,24},{20,28},{12,20},{4,12},{1,5},{9... | collective-permute-start | bytes 1769480 | tf_op jit(solution)/shard_map/ppermute | solution.py:26
  52.6 13.8 %collective-permute-start.10 = (bf16[64,2304]{1,0:T(8,128)(2,1)}, bf16[64,2304]{1,0:T(8,128)(2,1)}, u32[]{:S(2)}, u32[]{:S(2)}) collective-permute-start(bf16[64,2304]{1,0:T(8,128)(2,1)} %copy-done.101), channel_id=1, source_target_pairs={{0,4},{8,0},{16,8},{24,16},{28,24},{20,28},{12,20},{4,12},{1,5},{9... | collective-permute-start | bytes 884744 | tf_op jit(solution)/shard_map/ppermute | solution.py:26
  54.1 12.3 %collective-permute-start.9 = (bf16[64,2304]{1,0:T(8,128)(2,1)}, bf16[64,2304]{1,0:T(8,128)(2,1)}, u32[]{:S(2)}, u32[]{:S(2)}) collective-permute-start(bf16[64,2304]{1,0:T(8,128)(2,1)} %copy-done.100), channel_id=1, source_target_pairs={{0,8},{8,16},{16,24},{24,28},{28,20},{20,12},{12,4},{4,0},{1,9},{9... | collective-permute-start | bytes 884744 | tf_op jit(solution)/shard_map/ppermute | solution.py:26
  54.6 11.8 %collective-permute-start.13 = (bf16[128,2304]{1,0:T(8,128)(2,1)S(1)}, bf16[128,2304]{1,0:T(8,128)(2,1)S(1)}, u32[]{:S(2)}, u32[]{:S(2)}) collective-permute-start(bf16[128,2304]{1,0:T(8,128)(2,1)S(1)} %collective-permute-done.4), channel_id=1, source_target_pairs={{0,1},{1,0},{2,3},{3,2},{4,5},{5,4},{6,7},{7,6},{8,9},{9,8},{10,11... | collective-permute-start | bytes 1769480 | tf_op jit(solution)/shard_map/ppermute | solution.py:138
  66.4 11.7 %collective-permute-start.19 = (f32[4,2304]{1,0:T(4,128)}, f32[4,2304]{1,0:T(4,128)}, u32[]{:S(2)}, u32[]{:S(2)}) collective-permute-start(f32[4,2304]{1,0:T(4,128)} %add_add_fusion.3), channel_id=1, source_target_pairs={{0,16},{4,20},{8,24},{12,28},{16,0},{20,4},{24,8},{28,12},{1,17},{... | collective-permute-start | bytes 110600 | tf_op jit(solution)/shard_map/ppermute | solution.py:144
  88.0 15.8 %collective-permute-start.22 = (bf16[128,2304]{1,0:T(8,128)(2,1)}, bf16[128,2304]{1,0:T(8,128)(2,1)}, u32[]{:S(2)}, u32[]{:S(2)}) collective-permute-start(bf16[128,2304]{1,0:T(8,128)(2,1)} %collective-permute-done.11.refs_0_), channel_id=1, source_target_pairs={{0,8},{8,16},{16,24},{24,28},{28,20},{20,12},{12,4},{4,0},{1,9},{9... | collective-permute-start | bytes 1769480 | tf_op jit(solution)/shard_map/ppermute | solution.py:26
  89.6 14.3 %collective-permute-start.23 = (bf16[128,2304]{1,0:T(8,128)(2,1)}, bf16[128,2304]{1,0:T(8,128)(2,1)}, u32[]{:S(2)}, u32[]{:S(2)}) collective-permute-start(bf16[128,2304]{1,0:T(8,128)(2,1)} %collective-permute-done.12.refs_1_), channel_id=1, source_target_pairs={{0,4},{8,0},{16,8},{24,16},{28,24},{20,28},{12,20},{4,12},{1,5},{9... | collective-permute-start | bytes 1769480 | tf_op jit(solution)/shard_map/ppermute | solution.py:26
  103.8 18.7 %collective-permute-start.24 = (bf16[8,128,256]{2,1,0:T(8,128)(2,1)}, bf16[8,128,256]{2,1,0:T(8,128)(2,1)S(1)}, u32[]{:S(2)}, u32[]{:S(2)}) collective-permute-start(bf16[8,128,256]{2,1,0:T(8,128)(2,1)} %bitcast.21.refs_0_), channel_id=1, source_target_pairs={{0,8},{8,16},{16,24},{24,28},{28,20},{20,12},{12,4},{4,0},{1,9},{9... | collective-permute-start | bytes 1572872 | tf_op jit(solution)/shard_map/ppermute | solution.py:26
  105.3 17.2 %collective-permute-start.25 = (bf16[8,128,256]{2,1,0:T(8,128)(2,1)}, bf16[8,128,256]{2,1,0:T(8,128)(2,1)S(1)}, u32[]{:S(2)}, u32[]{:S(2)}) collective-permute-start(bf16[8,128,256]{2,1,0:T(8,128)(2,1)} %bitcast.21.refs_0_), channel_id=1, source_target_pairs={{0,4},{8,0},{16,8},{24,16},{28,24},{20,28},{12,20},{4,12},{1,5},{9... | collective-permute-start | bytes 1572872 | tf_op jit(solution)/shard_map/ppermute | solution.py:26
  107.5 13.2 %collective-permute-start.26 = (bf16[64,2304]{1,0:T(8,128)(2,1)}, bf16[64,2304]{1,0:T(8,128)(2,1)}, u32[]{:S(2)}, u32[]{:S(2)}) collective-permute-start(bf16[64,2304]{1,0:T(8,128)(2,1)} %slice.111), channel_id=1, source_target_pairs={{0,8},{8,16},{16,24},{24,28},{28,20},{20,12},{12,4},{4,0},{1,9},{9... | collective-permute-start | bytes 884744 | tf_op jit(solution)/shard_map/ppermute | solution.py:26
  110.7 11.8 %collective-permute-start.27 = (bf16[64,2304]{1,0:T(8,128)(2,1)}, bf16[64,2304]{1,0:T(8,128)(2,1)}, u32[]{:S(2)}, u32[]{:S(2)}) collective-permute-start(bf16[64,2304]{1,0:T(8,128)(2,1)} %slice.112), channel_id=1, source_target_pairs={{0,4},{8,0},{16,8},{24,16},{28,24},{20,28},{12,20},{4,12},{1,5},{9... | collective-permute-start | bytes 884744 | tf_op jit(solution)/shard_map/ppermute | solution.py:26
  123.4 13.8 %collective-permute-start.28 = (bf16[8,128,256]{2,1,0:T(8,128)(2,1)S(1)}, bf16[8,128,256]{2,1,0:T(8,128)(2,1)}, u32[]{:S(2)}, u32[]{:S(2)}) collective-permute-start(bf16[8,128,256]{2,1,0:T(8,128)(2,1)S(1)} %collective-permute-done.24.refs_0_), channel_id=1, source_target_pairs={{0,8},{8,16},{16,24},{24,28},{28,20},{20,12},{12,4},{4,0},{1,9},{9... | collective-permute-start | bytes 1572872 | tf_op jit(solution)/shard_map/ppermute | solution.py:26
  123.9 13.3 %collective-permute-start.29 = (bf16[8,128,256]{2,1,0:T(8,128)(2,1)}, bf16[8,128,256]{2,1,0:T(8,128)(2,1)S(1)}, u32[]{:S(2)}, u32[]{:S(2)}) collective-permute-start(bf16[8,128,256]{2,1,0:T(8,128)(2,1)} %copy-done.98), channel_id=1, source_target_pairs={{0,4},{8,0},{16,8},{24,16},{28,24},{20,28},{12,20},{4,12},{1,5},{9... | collective-permute-start | bytes 1572872 | tf_op jit(solution)/shard_map/ppermute | solution.py:26
  137.2 369.2 %reduce-scatter.4.cloned.1.call-start = ((), (), s32[]{:S(2)}) async-start(), calls=%async_computation.5 | async-start | bytes 6635520 | tf_op jit(solution)/shard_map/reduce_scatter | solution.py:908
  138.0 12.3 %collective-permute-start.30 = (bf16[8,128,256]{2,1,0:T(8,128)(2,1)}, bf16[8,128,256]{2,1,0:T(8,128)(2,1)S(1)}, u32[]{:S(2)}, u32[]{:S(2)}) collective-permute-start(bf16[8,128,256]{2,1,0:T(8,128)(2,1)} %collective-permute-done.28.refs_0_), channel_id=1, source_target_pairs={{0,8},{8,16},{16,24},{24,28},{28,20},{20,12},{12,4},{4,0},{1,9},{9... | collective-permute-start | bytes 1572872 | tf_op jit(solution)/shard_map/ppermute | solution.py:26
  138.6 12.2 %collective-permute-start.31 = (bf16[8,128,256]{2,1,0:T(8,128)(2,1)}, bf16[8,128,256]{2,1,0:T(8,128)(2,1)S(1)}, u32[]{:S(2)}, u32[]{:S(2)}) collective-permute-start(bf16[8,128,256]{2,1,0:T(8,128)(2,1)} %copy-done.96), channel_id=1, source_target_pairs={{0,4},{8,0},{16,8},{24,16},{28,24},{20,28},{12,20},{4,12},{1,5},{9... | collective-permute-start | bytes 1572872 | tf_op jit(solution)/shard_map/ppermute | solution.py:26
  172.8 15.4 %collective-permute-start.35 = (bf16[128,2304]{1,0:T(8,128)(2,1)S(1)}, bf16[128,2304]{1,0:T(8,128)(2,1)S(1)}, u32[]{:S(2)}, u32[]{:S(2)}) collective-permute-start(bf16[128,2304]{1,0:T(8,128)(2,1)S(1)} %get-tuple-element.1354), channel_id=1, source_target_pairs={{0,2},{1,3},{2,0},{3,1},{4,6},{5,7},{6,4},{7,5},{8,10},{9,11},{10,... | collective-permute-start | bytes 1769480 | tf_op jit(solution)/shard_map/ppermute | solution.py:133
  190.0 14.6 %collective-permute-start.36 = (bf16[128,2304]{1,0:T(8,128)(2,1)S(1)}, bf16[128,2304]{1,0:T(8,128)(2,1)S(1)}, u32[]{:S(2)}, u32[]{:S(2)}) collective-permute-start(bf16[128,2304]{1,0:T(8,128)(2,1)S(1)} %get-tuple-element.1163.refs_0_.refs_5_), channel_id=1, source_target_pairs={{0,8},{8,16},{16,24},{24,28},{28,20},{20,12},{12,4},{4,0},{1,9},{9... | collective-permute-start | bytes 1769480 | tf_op jit(solution)/shard_map/ppermute | solution.py:26
  190.6 14.5 %collective-permute-start.37 = (bf16[128,2304]{1,0:T(8,128)(2,1)S(1)}, bf16[128,2304]{1,0:T(8,128)(2,1)}, u32[]{:S(2)}, u32[]{:S(2)}) collective-permute-start(bf16[128,2304]{1,0:T(8,128)(2,1)S(1)} %get-tuple-element.1163.refs_0_.refs_5_), channel_id=1, source_target_pairs={{0,4},{8,0},{16,8},{24,16},{28,24},{20,28},{12,20},{4,12},{1,5},{9... | collective-permute-start | bytes 1769480 | tf_op jit(solution)/shard_map/ppermute | solution.py:26
  205.2 13.5 %collective-permute-start.38 = (bf16[128,2304]{1,0:T(8,128)(2,1)S(1)}, bf16[128,2304]{1,0:T(8,128)(2,1)S(1)}, u32[]{:S(2)}, u32[]{:S(2)}) collective-permute-start(bf16[128,2304]{1,0:T(8,128)(2,1)S(1)} %collective-permute-done.36.refs_0_.refs_6_), channel_id=1, source_target_pairs={{0,8},{8,16},{16,24},{24,28},{28,20},{20,12},{12,4},{4,0},{1,9},{9... | collective-permute-start | bytes 1769480 | tf_op jit(solution)/shard_map/ppermute | solution.py:26
  206.9 13.7 %collective-permute-start.39 = (bf16[128,2304]{1,0:T(8,128)(2,1)}, bf16[128,2304]{1,0:T(8,128)(2,1)S(1)}, u32[]{:S(2)}, u32[]{:S(2)}) collective-permute-start(bf16[128,2304]{1,0:T(8,128)(2,1)} %collective-permute-done.37.refs_1_.refs_7_), channel_id=1, source_target_pairs={{0,4},{8,0},{16,8},{24,16},{28,24},{20,28},{12,20},{4,12},{1,5},{9... | collective-permute-start | bytes 1769480 | tf_op jit(solution)/shard_map/ppermute | solution.py:26
  220.7 12.6 %collective-permute-start.40 = (bf16[128,2304]{1,0:T(8,128)(2,1)S(1)}, bf16[128,2304]{1,0:T(8,128)(2,1)S(1)}, u32[]{:S(2)}, u32[]{:S(2)}) collective-permute-start(bf16[128,2304]{1,0:T(8,128)(2,1)S(1)} %collective-permute-done.38.refs_0_.refs_8_), channel_id=1, source_target_pairs={{0,8},{8,16},{16,24},{24,28},{28,20},{20,12},{12,4},{4,0},{1,9},{9... | collective-permute-start | bytes 1769480 | tf_op jit(solution)/shard_map/ppermute | solution.py:26
  222.1 12.4 %collective-permute-start.41 = (bf16[128,2304]{1,0:T(8,128)(2,1)S(1)}, bf16[128,2304]{1,0:T(8,128)(2,1)S(1)}, u32[]{:S(2)}, u32[]{:S(2)}) collective-permute-start(bf16[128,2304]{1,0:T(8,128)(2,1)S(1)} %collective-permute-done.39.refs_1_.refs_9_), channel_id=1, source_target_pairs={{0,4},{8,0},{16,8},{24,16},{28,24},{20,28},{12,20},{4,12},{1,5},{9... | collective-permute-start | bytes 1769480 | tf_op jit(solution)/shard_map/ppermute | solution.py:26
  259.7 14.0 %collective-permute-start.46 = (bf16[128,2304]{1,0:T(8,128)(2,1)S(1)}, bf16[128,2304]{1,0:T(8,128)(2,1)S(1)}, u32[]{:S(2)}, u32[]{:S(2)}) collective-permute-start(bf16[128,2304]{1,0:T(8,128)(2,1)S(1)} %add_convert_fusion.17), channel_id=1, source_target_pairs={{0,8},{8,16},{16,24},{24,28},{28,20},{20,12},{12,4},{4,0},{1,9},{9... | collective-permute-start | bytes 1769480 | tf_op jit(solution)/shard_map/ppermute | solution.py:26
  260.3 13.9 %collective-permute-start.47 = (bf16[128,2304]{1,0:T(8,128)(2,1)S(1)}, bf16[128,2304]{1,0:T(8,128)(2,1)S(1)}, u32[]{:S(2)}, u32[]{:S(2)}) collective-permute-start(bf16[128,2304]{1,0:T(8,128)(2,1)S(1)} %add_convert_fusion.16), channel_id=1, source_target_pairs={{0,4},{8,0},{16,8},{24,16},{28,24},{20,28},{12,20},{4,12},{1,5},{9... | collective-permute-start | bytes 1769480 | tf_op jit(solution)/shard_map/ppermute | solution.py:26
  274.5 15.0 %collective-permute-start.48 = (bf16[128,2304]{1,0:T(8,128)(2,1)S(1)}, bf16[128,2304]{1,0:T(8,128)(2,1)S(1)}, u32[]{:S(2)}, u32[]{:S(2)}) collective-permute-start(bf16[128,2304]{1,0:T(8,128)(2,1)S(1)} %add_convert_fusion.15), channel_id=1, source_target_pairs={{0,8},{8,16},{16,24},{24,28},{28,20},{20,12},{12,4},{4,0},{1,9},{9... | collective-permute-start | bytes 1769480 | tf_op jit(solution)/shard_map/ppermute | solution.py:26
  275.1 16.3 %collective-permute-start.49 = (bf16[128,2304]{1,0:T(8,128)(2,1)S(1)}, bf16[128,2304]{1,0:T(8,128)(2,1)S(1)}, u32[]{:S(2)}, u32[]{:S(2)}) collective-permute-start(bf16[128,2304]{1,0:T(8,128)(2,1)S(1)} %add_convert_fusion.14), channel_id=1, source_target_pairs={{0,4},{8,0},{16,8},{24,16},{28,24},{20,28},{12,20},{4,12},{1,5},{9... | collective-permute-start | bytes 1769480 | tf_op jit(solution)/shard_map/ppermute | solution.py:26
  291.8 15.9 %collective-permute-start.50 = (bf16[128,2304]{1,0:T(8,128)(2,1)S(1)}, bf16[128,2304]{1,0:T(8,128)(2,1)S(1)}, u32[]{:S(2)}, u32[]{:S(2)}) collective-permute-start(bf16[128,2304]{1,0:T(8,128)(2,1)S(1)} %add_convert_fusion.13), channel_id=1, source_target_pairs={{0,8},{8,16},{16,24},{24,28},{28,20},{20,12},{12,4},{4,0},{1,9},{9... | collective-permute-start | bytes 1769480 | tf_op jit(solution)/shard_map/ppermute | solution.py:26
  291.8 16.0 %collective-permute-start.51 = (bf16[128,2304]{1,0:T(8,128)(2,1)S(1)}, bf16[128,2304]{1,0:T(8,128)(2,1)S(1)}, u32[]{:S(2)}, u32[]{:S(2)}) collective-permute-start(bf16[128,2304]{1,0:T(8,128)(2,1)S(1)} %add_convert_fusion.12), channel_id=1, source_target_pairs={{0,4},{8,0},{16,8},{24,16},{28,24},{20,28},{12,20},{4,12},{1,5},{9... | collective-permute-start | bytes 1769480 | tf_op jit(solution)/shard_map/ppermute | solution.py:26
  309.4 14.2 %collective-permute-start.52 = (bf16[128,2304]{1,0:T(8,128)(2,1)S(1)}, bf16[128,2304]{1,0:T(8,128)(2,1)S(1)}, u32[]{:S(2)}, u32[]{:S(2)}) collective-permute-start(bf16[128,2304]{1,0:T(8,128)(2,1)S(1)} %get-tuple-element.1218.refs_0_.refs_5_), channel_id=1, source_target_pairs={{0,8},{8,16},{16,24},{24,28},{28,20},{20,12},{12,4},{4,0},{1,9},{9... | collective-permute-start | bytes 1769480 | tf_op jit(solution)/shard_map/ppermute | solution.py:26
  309.4 14.2 %collective-permute-start.53 = (bf16[128,2304]{1,0:T(8,128)(2,1)S(1)}, bf16[128,2304]{1,0:T(8,128)(2,1)S(1)}, u32[]{:S(2)}, u32[]{:S(2)}) collective-permute-start(bf16[128,2304]{1,0:T(8,128)(2,1)S(1)} %get-tuple-element.1218.refs_0_.refs_5_), channel_id=1, source_target_pairs={{0,4},{8,0},{16,8},{24,16},{28,24},{20,28},{12,20},{4,12},{1,5},{9... | collective-permute-start | bytes 1769480 | tf_op jit(solution)/shard_map/ppermute | solution.py:26
  323.6 13.4 %collective-permute-start.54 = (bf16[128,2304]{1,0:T(8,128)(2,1)S(1)}, bf16[128,2304]{1,0:T(8,128)(2,1)S(1)}, u32[]{:S(2)}, u32[]{:S(2)}) collective-permute-start(bf16[128,2304]{1,0:T(8,128)(2,1)S(1)} %collective-permute-done.52.refs_0_.refs_6_), channel_id=1, source_target_pairs={{0,8},{8,16},{16,24},{24,28},{28,20},{20,12},{12,4},{4,0},{1,9},{9... | collective-permute-start | bytes 1769480 | tf_op jit(solution)/shard_map/ppermute | solution.py:26
  323.7 13.3 %collective-permute-start.55 = (bf16[128,2304]{1,0:T(8,128)(2,1)S(1)}, bf16[128,2304]{1,0:T(8,128)(2,1)S(1)}, u32[]{:S(2)}, u32[]{:S(2)}) collective-permute-start(bf16[128,2304]{1,0:T(8,128)(2,1)S(1)} %collective-permute-done.53.refs_1_.refs_7_), channel_id=1, source_target_pairs={{0,4},{8,0},{16,8},{24,16},{28,24},{20,28},{12,20},{4,12},{1,5},{9... | collective-permute-start | bytes 1769480 | tf_op jit(solution)/shard_map/ppermute | solution.py:26
  372.7 15.1 %collective-permute-start.62 = (bf16[128,2304]{1,0:T(8,128)(2,1)}, bf16[128,2304]{1,0:T(8,128)(2,1)S(1)}, u32[]{:S(2)}, u32[]{:S(2)}) collective-permute-start(bf16[128,2304]{1,0:T(8,128)(2,1)} %add_convert_fusion.11), channel_id=1, source_target_pairs={{0,8},{8,16},{16,24},{24,28},{28,20},{20,12},{12,4},{4,0},{1,9},{9... | collective-permute-start | bytes 1769480 | tf_op jit(solution)/shard_map/ppermute | solution.py:26
  373.5 14.4 %collective-permute-start.63 = (bf16[128,2304]{1,0:T(8,128)(2,1)}, bf16[128,2304]{1,0:T(8,128)(2,1)}, u32[]{:S(2)}, u32[]{:S(2)}) collective-permute-start(bf16[128,2304]{1,0:T(8,128)(2,1)} %add_convert_fusion.10), channel_id=1, source_target_pairs={{0,4},{8,0},{16,8},{24,16},{28,24},{20,28},{12,20},{4,12},{1,5},{9... | collective-permute-start | bytes 1769480 | tf_op jit(solution)/shard_map/ppermute | solution.py:26
  390.1 11.1 %collective-permute-start.64 = (bf16[128,2304]{1,0:T(8,128)(2,1)S(1)}, bf16[128,2304]{1,0:T(8,128)(2,1)S(1)}, u32[]{:S(2)}, u32[]{:S(2)}) collective-permute-start(bf16[128,2304]{1,0:T(8,128)(2,1)S(1)} %add_convert_fusion.9), channel_id=1, source_target_pairs={{0,8},{8,16},{16,24},{24,28},{28,20},{20,12},{12,4},{4,0},{1,9},{9... | collective-permute-start | bytes 1769480 | tf_op jit(solution)/shard_map/ppermute | solution.py:26
  391.0 11.3 %collective-permute-start.65 = (bf16[128,2304]{1,0:T(8,128)(2,1)S(1)}, bf16[128,2304]{1,0:T(8,128)(2,1)S(1)}, u32[]{:S(2)}, u32[]{:S(2)}) collective-permute-start(bf16[128,2304]{1,0:T(8,128)(2,1)S(1)} %add_convert_fusion.8), channel_id=1, source_target_pairs={{0,4},{8,0},{16,8},{24,16},{28,24},{20,28},{12,20},{4,12},{1,5},{9... | collective-permute-start | bytes 1769480 | tf_op jit(solution)/shard_map/ppermute | solution.py:26
  417.2 19.1 %collective-permute-start.68 = (bf16[128,2304]{1,0:T(8,128)(2,1)}, bf16[128,2304]{1,0:T(8,128)(2,1)}, u32[]{:S(2)}, u32[]{:S(2)}) collective-permute-start(bf16[128,2304]{1,0:T(8,128)(2,1)} %get-tuple-element.1037.d_attn_ref), channel_id=1, source_target_pairs={{0,2},{1,3},{2,0},{3,1},{4,6},{5,7},{6,4},{7,5},{8,10},{9,11},{10,... | collective-permute-start | bytes 1769480 | tf_op jit(solution)/shard_map/ppermute | solution.py:133
  436.4 117.2 %reduce-scatter.6.cloned.1.call-start = ((), (), s32[]{:S(2)}) async-start(), calls=%async_computation.6 | async-start | bytes 6635520 | tf_op jit(solution)/shard_map/reduce_scatter | solution.py:908
  461.6 13.5 %collective-permute-start.73 = (bf16[2,4,128,256]{3,2,1,0:T(8,128)(2,1)}, bf16[2,4,128,256]{3,2,1,0:T(8,128)(2,1)S(1)}, u32[]{:S(2)}, u32[]{:S(2)}) collective-permute-start(bf16[2,4,128,256]{3,2,1,0:T(8,128)(2,1)} %get-tuple-element.1154), channel_id=1, source_target_pairs={{0,8},{8,16},{16,24},{24,28},{28,20},{20,12},{12,4},{4,0},{1,9},{9... | collective-permute-start | bytes 1572872 | tf_op jit(solution)/shard_map/ppermute | solution.py:26
  462.6 13.2 %collective-permute-start.74 = (bf16[2,4,128,256]{3,2,1,0:T(8,128)(2,1)}, bf16[2,4,128,256]{3,2,1,0:T(8,128)(2,1)}, u32[]{:S(2)}, u32[]{:S(2)}) collective-permute-start(bf16[2,4,128,256]{3,2,1,0:T(8,128)(2,1)} %get-tuple-element.1155), channel_id=1, source_target_pairs={{0,4},{8,0},{16,8},{24,16},{28,24},{20,28},{12,20},{4,12},{1,5},{9... | collective-permute-start | bytes 1572872 | tf_op jit(solution)/shard_map/ppermute | solution.py:26
  478.3 129.9 %reduce-scatter.8.cloned.1.call-start = ((), (), s32[]{:S(2)}) async-start(), calls=%async_computation.7 | async-start | bytes 6635520 | tf_op jit(solution)/shard_map/reduce_scatter | solution.py:908
  478.4 12.8 %collective-permute-start.75 = (bf16[2,4,128,256]{3,2,1,0:T(8,128)(2,1)}, bf16[2,4,128,256]{3,2,1,0:T(8,128)(2,1)}, u32[]{:S(2)}, u32[]{:S(2)}) collective-permute-start(bf16[2,4,128,256]{3,2,1,0:T(8,128)(2,1)} %get-tuple-element.1209), channel_id=1, source_target_pairs={{0,8},{8,16},{16,24},{24,28},{28,20},{20,12},{12,4},{4,0},{1,9},{9... | collective-permute-start | bytes 1572872 | tf_op jit(solution)/shard_map/ppermute | solution.py:26
  479.3 12.4 %collective-permute-start.76 = (bf16[2,4,128,256]{3,2,1,0:T(8,128)(2,1)}, bf16[2,4,128,256]{3,2,1,0:T(8,128)(2,1)}, u32[]{:S(2)}, u32[]{:S(2)}) collective-permute-start(bf16[2,4,128,256]{3,2,1,0:T(8,128)(2,1)} %get-tuple-element.1210), channel_id=1, source_target_pairs={{0,4},{8,0},{16,8},{24,16},{28,24},{20,28},{12,20},{4,12},{1,5},{9... | collective-permute-start | bytes 1572872 | tf_op jit(solution)/shard_map/ppermute | solution.py:26
  494.1 11.7 %collective-permute-start.77 = (bf16[2,4,128,256]{3,2,1,0:T(8,128)(2,1)}, bf16[2,4,128,256]{3,2,1,0:T(8,128)(2,1)}, u32[]{:S(2)}, u32[]{:S(2)}) collective-permute-start(bf16[2,4,128,256]{3,2,1,0:T(8,128)(2,1)} %get-tuple-element.1235), channel_id=1, source_target_pairs={{0,8},{8,16},{16,24},{24,28},{28,20},{20,12},{12,4},{4,0},{1,9},{9... | collective-permute-start | bytes 1572872 | tf_op jit(solution)/shard_map/ppermute | solution.py:26
  494.8 11.6 %collective-permute-start.78 = (bf16[2,4,128,256]{3,2,1,0:T(8,128)(2,1)}, bf16[2,4,128,256]{3,2,1,0:T(8,128)(2,1)}, u32[]{:S(2)}, u32[]{:S(2)}) collective-permute-start(bf16[2,4,128,256]{3,2,1,0:T(8,128)(2,1)} %get-tuple-element.1236), channel_id=1, source_target_pairs={{0,4},{8,0},{16,8},{24,16},{28,24},{20,28},{12,20},{4,12},{1,5},{9... | collective-permute-start | bytes 1572872 | tf_op jit(solution)/shard_map/ppermute | solution.py:26
  513.9 14.3 %collective-permute-start.79 = (bf16[96,2304]{1,0:T(8,128)(2,1)}, bf16[96,2304]{1,0:T(8,128)(2,1)S(1)}, u32[]{:S(2)}, u32[]{:S(2)}) collective-permute-start(bf16[96,2304]{1,0:T(8,128)(2,1)} %get-tuple-element.1252), channel_id=1, source_target_pairs={{0,8},{8,16},{16,24},{24,28},{28,20},{20,12},{12,4},{4,0},{1,9},{9... | collective-permute-start | bytes 1327112 | tf_op jit(solution)/shard_map/ppermute | solution.py:26
  514.9 13.3 %collective-permute-start.80 = (bf16[96,2304]{1,0:T(8,128)(2,1)}, bf16[96,2304]{1,0:T(8,128)(2,1)S(1)}, u32[]{:S(2)}, u32[]{:S(2)}) collective-permute-start(bf16[96,2304]{1,0:T(8,128)(2,1)} %get-tuple-element.1253), channel_id=1, source_target_pairs={{0,4},{8,0},{16,8},{24,16},{28,24},{20,28},{12,20},{4,12},{1,5},{9... | collective-permute-start | bytes 1327112 | tf_op jit(solution)/shard_map/ppermute | solution.py:26
  530.6 23.0 %collective-permute-start.83 = (bf16[256,2304]{1,0:T(8,128)(2,1)}, bf16[256,2304]{1,0:T(8,128)(2,1)S(1)}, u32[]{:S(2)}, u32[]{:S(2)}) collective-permute-start(bf16[256,2304]{1,0:T(8,128)(2,1)} %get-tuple-element.1290), channel_id=1, source_target_pairs={{0,1},{1,0},{2,3},{3,2},{4,5},{5,4},{6,7},{7,6},{8,9},{9,8},{10,11... | collective-permute-start | bytes 3538952 | tf_op jit(solution)/shard_map/ppermute | solution.py:138
  530.9 21.7 %collective-permute-start.81 = (bf16[192,2304]{1,0:T(8,128)(2,1)S(1)}, bf16[192,2304]{1,0:T(8,128)(2,1)S(1)}, u32[]{:S(2)}, u32[]{:S(2)}) collective-permute-start(bf16[192,2304]{1,0:T(8,128)(2,1)S(1)} %add_convert_fusion.5), channel_id=1, source_target_pairs={{0,8},{8,16},{16,24},{24,28},{28,20},{20,12},{12,4},{4,0},{1,9},{9... | collective-permute-start | bytes 2654216 | tf_op jit(solution)/shard_map/ppermute | solution.py:26
  532.0 21.6 %collective-permute-start.82 = (bf16[192,2304]{1,0:T(8,128)(2,1)S(1)}, bf16[192,2304]{1,0:T(8,128)(2,1)}, u32[]{:S(2)}, u32[]{:S(2)}) collective-permute-start(bf16[192,2304]{1,0:T(8,128)(2,1)S(1)} %add_convert_fusion.4), channel_id=1, source_target_pairs={{0,4},{8,0},{16,8},{24,16},{28,24},{20,28},{12,20},{4,12},{1,5},{9... | collective-permute-start | bytes 2654216 | tf_op jit(solution)/shard_map/ppermute | solution.py:26
  561.0 25.0 %collective-permute-start.89 = (bf16[128,2304]{1,0:T(8,128)(2,1)S(1)}, bf16[128,2304]{1,0:T(8,128)(2,1)S(1)}, u32[]{:S(2)}, u32[]{:S(2)}) collective-permute-start(bf16[128,2304]{1,0:T(8,128)(2,1)S(1)} %slice.178), channel_id=1, source_target_pairs={{0,2},{1,3},{2,0},{3,1},{4,6},{5,7},{6,4},{7,5},{8,10},{9,11},{10,... | collective-permute-start | bytes 1769480 | tf_op jit(solution)/shard_map/ppermute | solution.py:133
  562.6 23.6 %collective-permute-start.87 = (bf16[192,2304]{1,0:T(8,128)(2,1)}, bf16[192,2304]{1,0:T(8,128)(2,1)S(1)}, u32[]{:S(2)}, u32[]{:S(2)}) collective-permute-start(bf16[192,2304]{1,0:T(8,128)(2,1)} %add_convert_fusion.3), channel_id=1, source_target_pairs={{0,8},{8,16},{16,24},{24,28},{28,20},{20,12},{12,4},{4,0},{1,9},{9... | collective-permute-start | bytes 2654216 | tf_op jit(solution)/shard_map/ppermute | solution.py:26
  565.9 20.2 %collective-permute-start.88 = (bf16[192,2304]{1,0:T(8,128)(2,1)S(1)}, bf16[192,2304]{1,0:T(8,128)(2,1)S(1)}, u32[]{:S(2)}, u32[]{:S(2)}) collective-permute-start(bf16[192,2304]{1,0:T(8,128)(2,1)S(1)} %add_convert_fusion.2), channel_id=1, source_target_pairs={{0,4},{8,0},{16,8},{24,16},{28,24},{20,28},{12,20},{4,12},{1,5},{9... | collective-permute-start | bytes 2654216 | tf_op jit(solution)/shard_map/ppermute | solution.py:26
  587.6 17.7 %collective-permute-start.93 = (bf16[192,2304]{1,0:T(8,128)(2,1)S(1)}, bf16[192,2304]{1,0:T(8,128)(2,1)S(1)}, u32[]{:S(2)}, u32[]{:S(2)}) collective-permute-start(bf16[192,2304]{1,0:T(8,128)(2,1)S(1)} %add_convert_fusion.1), channel_id=1, source_target_pairs={{0,8},{8,16},{16,24},{24,28},{28,20},{20,12},{12,4},{4,0},{1,9},{9... | collective-permute-start | bytes 2654216 | tf_op jit(solution)/shard_map/ppermute | solution.py:26
  588.4 18.3 %collective-permute-start.94 = (bf16[192,2304]{1,0:T(8,128)(2,1)S(1)}, bf16[192,2304]{1,0:T(8,128)(2,1)S(1)}, u32[]{:S(2)}, u32[]{:S(2)}) collective-permute-start(bf16[192,2304]{1,0:T(8,128)(2,1)S(1)} %add_convert_fusion), channel_id=1, source_target_pairs={{0,4},{8,0},{16,8},{24,16},{28,24},{20,28},{12,20},{4,12},{1,5},{9... | collective-permute-start | bytes 2654216 | tf_op jit(solution)/shard_map/ppermute | solution.py:26
  (169 other events, 1681.2 us)
Sparse Core Ops, SparseCore 0:
  39.9 72.2 all-gather.2
  137.3 38.9 all-gather.4
  436.5 49.7 reduce-scatter.3
  488.9 53.4 reduce-scatter.5
  544.7 60.4 reduce-scatter.7

commit v4 on v3

--- a/solution.py
+++ b/solution.py
@@ -995,10 +995,14 @@
     )
     grad_fulls = [grad_query_full, grad_key_full, grad_value_full, grad_output_full]
 
+    ready = {}
+
     def weight_terms(i, fulls):
         if i == half_ring:
             member = ring_member(i)
             return member_rows([(fulls[:2], cols[:2], member), (fulls[2:], cols[2:], member)], BF16)
+        if i in ready:
+            return ready[i]
         ends = [0] if i == 0 else [-i, i]
         return member_rows([(fulls, cols, ring_member(k)) for k in ends], BF16)
 
@@ -1012,9 +1016,11 @@
         if i == half_ring - 2:
             kept, sent, sums, up = state
             sums = add_from(sums, "fsdp", low_masks())
-            return kept, near_hop(sent), sums, up.T.astype(F32), flying.pop("gate")
+            fulls, _ = tie(grad_fulls, kept)
+            ready[1], ready[0] = weight_terms(1, fulls), weight_terms(0, fulls)
+            return kept, near_hop(sent), sums, up.T.astype(F32), flying.pop("gate"), dict(ready)
         if i == half_ring - 3:
-            kept, near, sums, up, gate = state
+            kept, near, sums, up, gate, _ = state
             total = kept + near.astype(F32)
             arrived = far_hop(total[tokens:].astype(BF16))
             sums = add_from(sums, "ctx", low_masks())

time: 628 us -> 624 us (level)
    unnamed x271 -> x273, local copies, waits for them, and re-layouts: 26 us -> 25.9 us
where the time goes in v4:
time: 624 us; the launch traced here: 616 us
  waiting for transfers between devices  213 us (34%)
  Pallas kernels  206 us (33%)
  starting transfers between devices  98.5 us (16%)
  local copies, waits for them, and re-layouts  41.2 us (7%)
  other arithmetic  31 us (5%)
  between operations  15.9 us (3%)
  matrix products  9.8 us (2%)
    ppermute x72, waiting for transfers between devices, ring_hop(): lax.ppermute(block, 'ctx', [(order[i], order[(i + step) % size]) for i in...  170 us
    ppermute x72, starting transfers between devices, ring_hop(): lax.ppermute(block, 'ctx', [(order[i], order[(i + step) % size]) for i in...  75.5 us
    ppermute x4, waiting for transfers between devices, far_hop(): lax.ppermute(block, 'fsdp', [(i, i ^ size // 2) for i in range(size)])  37.6 us
    pallas_call x4, Pallas kernels, weight_grad(): pl.pallas_call(functools.partial(weight_grad_kernel, len(units), len(rows...  35.9 us
    pallas_call x10, Pallas kernels, unit_call(): pl.pallas_call(functools.partial(kernel, len(rows)), grid=(count // tile,...  34.2 us
    pallas_call x10, Pallas kernels, out_call(): pl.pallas_call(functools.partial(out_kernel, len(ins)), grid=(width // ti...  29.6 us
    pallas_call x12, Pallas kernels, place_rows(): pl.pallas_call(functools.partial(place_kernel, cols, n_blocks), grid_spec...  27.5 us
    unnamed x273, local copies, waits for them, and re-layouts  25.9 us
  transfers between devices with their start and end apart: 101, of which 52 were waited for; matrix products, arithmetic and copies ran while one was open for 8% of the time, Pallas kernels for 31%

profile of v4, /device:TPU:0, one launch (start us, length us, event | category | flops | bytes accessed | tf_op | source)
XLA Modules:
  0.0 615.7 jit_solution(956304623053941224)
XLA Ops:
  10.6 2.6 collective-permute-start.2
  15.7 3.1 pad_maximum_fusion
  26.3 7.2 %collective-permute-done.refs_0_ = bf16[64,2304]{1,0:T(8,128)(2,1)S(1)} collective-permute-done((bf16[64,2304]{1,0:T(8,128)(2,1)S(1)}, bf16[64,2304]{1,0:T(8,128)(2,1)S(1)}, u32[]{:S(2)}, u32[]{:S(2)}) %collective-permute-start) | collective-permute-done | bytes 294944 | tf_op jit(solution)/shard_map/ppermute | solution.py:26
  35.0 4.7 collective-permute-done.4
  46.6 3.2 shard_map.242
  49.8 2.7 shard_map.241
  55.1 11.2 %collective-permute-done.10.refs_1_ = bf16[64,2304]{1,0:T(8,128)(2,1)} collective-permute-done((bf16[64,2304]{1,0:T(8,128)(2,1)}, bf16[64,2304]{1,0:T(8,128)(2,1)}, u32[]{:S(2)}, u32[]{:S(2)}) %collective-permute-start.10) | collective-permute-done | bytes 294944 | tf_op jit(solution)/shard_map/ppermute | solution.py:26
  66.3 2.6 collective-permute-start.19
  72.4 2.7 shard_map.243
  75.1 3.0 shard_map.244
  85.4 2.7 shard_map.245
  99.5 4.2 shard_map.248
  113.1 3.0 shard_map.251
  116.1 4.7 collective-permute-done.26.refs_0_
  128.8 3.6 shard_map.254.queries_ref
  142.5 7.7 %collective-permute-done.30.refs_0_ = bf16[8,128,256]{2,1,0:T(8,128)(2,1)S(1)} collective-permute-done((bf16[8,128,256]{2,1,0:T(8,128)(2,1)}, bf16[8,128,256]{2,1,0:T(8,128)(2,1)S(1)}, u32[]{:S(2)}, u32[]{:S(2)}) %collective-permute-start.30) | collective-permute-done | bytes 524320 | tf_op jit(solution)/shard_map/ppermute | solution.py:26
  161.2 5.4 shard_map.259
  166.7 2.6 fusion.40
  169.5 2.8 collective-permute-done.34
  175.7 12.4 %collective-permute-done.35.moved_ref = bf16[128,2304]{1,0:T(8,128)(2,1)S(1)} collective-permute-done((bf16[128,2304]{1,0:T(8,128)(2,1)S(1)}, bf16[128,2304]{1,0:T(8,128)(2,1)S(1)}, u32[]{:S(2)}, u32[]{:S(2)}) %collective-permute-start.35) | collective-permute-done | bytes 589856 | tf_op jit(solution)/shard_map/ppermute | solution.py:133
  191.9 3.5 shard_map.261
  197.8 6.8 %collective-permute-done.36.refs_0_.refs_6_ = bf16[128,2304]{1,0:T(8,128)(2,1)S(1)} collective-permute-done((bf16[128,2304]{1,0:T(8,128)(2,1)S(1)}, bf16[128,2304]{1,0:T(8,128)(2,1)S(1)}, u32[]{:S(2)}, u32[]{:S(2)}) %collective-permute-start.36) | collective-permute-done | bytes 589856 | tf_op jit(solution)/shard_map/ppermute | solution.py:26
  206.9 4.0 copy-done
  210.9 5.6 shard_map.262
  222.2 4.5 shard_map.263
  226.8 5.9 collective-permute-done.40.refs_0_.refs_10_
  236.4 4.5 shard_map.264
  242.9 3.4 shard_map.265
  250.3 2.5 shard_map.267
  252.8 4.6 collective-permute-done.44
  261.5 2.5 shard_map.268
  264.0 9.4 %collective-permute-done.46 = bf16[128,2304]{1,0:T(8,128)(2,1)S(1)} collective-permute-done((bf16[128,2304]{1,0:T(8,128)(2,1)S(1)}, bf16[128,2304]{1,0:T(8,128)(2,1)S(1)}, u32[]{:S(2)}, u32[]{:S(2)}) %collective-permute-start.46) | collective-permute-done | bytes 589856 | tf_op jit(solution)/shard_map/ppermute | solution.py:26
  279.0 9.8 %collective-permute-done.48 = bf16[128,2304]{1,0:T(8,128)(2,1)S(1)} collective-permute-done((bf16[128,2304]{1,0:T(8,128)(2,1)S(1)}, bf16[128,2304]{1,0:T(8,128)(2,1)S(1)}, u32[]{:S(2)}, u32[]{:S(2)}) %collective-permute-start.48) | collective-permute-done | bytes 589856 | tf_op jit(solution)/shard_map/ppermute | solution.py:26
  295.4 12.1 %collective-permute-done.50.behind_ref = bf16[128,2304]{1,0:T(8,128)(2,1)S(1)} collective-permute-done((bf16[128,2304]{1,0:T(8,128)(2,1)S(1)}, bf16[128,2304]{1,0:T(8,128)(2,1)S(1)}, u32[]{:S(2)}, u32[]{:S(2)}) %collective-permute-start.50) | collective-permute-done | bytes 589856 | tf_op jit(solution)/shard_map/ppermute | solution.py:26
  314.6 9.5 %collective-permute-done.52.refs_0_.refs_6_ = bf16[128,2304]{1,0:T(8,128)(2,1)S(1)} collective-permute-done((bf16[128,2304]{1,0:T(8,128)(2,1)S(1)}, bf16[128,2304]{1,0:T(8,128)(2,1)S(1)}, u32[]{:S(2)}, u32[]{:S(2)}) %collective-permute-start.52) | collective-permute-done | bytes 589856 | tf_op jit(solution)/shard_map/ppermute | solution.py:26
  326.2 2.7 shard_map.273
  329.8 7.5 %collective-permute-done.54.refs_0_.refs_8_ = bf16[128,2304]{1,0:T(8,128)(2,1)S(1)} collective-permute-done((bf16[128,2304]{1,0:T(8,128)(2,1)S(1)}, bf16[128,2304]{1,0:T(8,128)(2,1)S(1)}, u32[]{:S(2)}, u32[]{:S(2)}) %collective-permute-start.54) | collective-permute-done | bytes 589856 | tf_op jit(solution)/shard_map/ppermute | solution.py:26
  339.4 2.7 shard_map.274
  342.1 5.1 collective-permute-done.56.refs_0_.refs_10_
  350.3 2.7 shard_map.275
  359.0 2.8 shard_map.277
  363.9 4.3 shard_map.278
  374.6 4.3 shard_map.279
  378.9 8.6 %shard_map.280.refs_14_ = bf16[1152,2304]{1,0:T(8,128)(2,1)} custom-call(bf16[128,1152]{1,0:T(8,128)(2,1)} %copy-done.25, bf16[256,1152]{1,0:T(8,128)(2,1)} %copy-done.15, bf16[256,1152]{1,0:T(8,128)(2,1)} %copy-done.17, bf16[256,1152]{1,0:T(8,128)(2,1)} %copy-done.18, bf16[128,1152]{1,0:T(8,128)(2,1)} %copy-done.27, bf16[128,2304]{1,0:T(8,128)(2,1)} %copy-done.10, ...), custom_call_target="tpu_custom_call" | custom-call | tf_op jit(solution)/shard_map/pallas_call | solution.py:415
  391.9 4.0 copy-done.1
  395.9 4.4 shard_map.281
  404.2 2.9 shard_map.282.term_ref
  407.1 5.0 collective-permute-done.66.behind_ref
  419.6 5.9 shard_map.285
  426.8 8.8 %shard_map.284 = (bf16[512,512]{1,0:T(8,128)(2,1)}, bf16[2,4,128,256]{3,2,1,0:T(8,128)(2,1)}, bf16[2,4,128,256]{3,2,1,0:T(8,128)(2,1)}, bf16[2,4,128,256]{3,2,1,...) custom-call(bf16[8,1024,256]{2,1,0:T(8,128)(2,1)} %shard_map.258.key, ...), custom_call_target="tpu_custom_call" | custom-call | tf_op jit(solution)/shard_map/pallas_call | solution.py:666
  439.0 9.6 %shard_map.286 = (bf16[512,512]{1,0:T(8,128)(2,1)}, bf16[2,4,128,256]{3,2,1,0:T(8,128)(2,1)}, bf16[2,4,128,256]{3,2,1,0:T(8,128)(2,1)}, bf16[2,4,128,256]{3,2,1,...) custom-call(bf16[8,1024,256]{2,1,0:T(8,128)(2,1)} %shard_map.258.key, ...), custom_call_target="tpu_custom_call", output_to_operand_aliasing={{0}: (10, {}), {1}: (11, {}), {2}: (12, {}), {3}: (13, {}),... | custom-call | tf_op jit(solution)/shard_map/pallas_call | solution.py:666
  450.7 6.7 %collective-permute-done.71.behind_ref = bf16[1,4,128,256]{3,2,1,0:T(8,128)(2,1)S(1)} collective-permute-done((bf16[1,4,128,256]{3,2,1,0:T(8,128)(2,1)}, bf16[1,4,128,256]{3,2,1,0:T(8,128)(2,1)S(1)}, u32[]{:S(2)}, u32[]{:S(2)}) %collective-permute-start.71) | collective-permute-done | bytes 262176 | tf_op jit(solution)/shard_map/ppermute | solution.py:26
  463.7 10.7 %shard_map.288 = bf16[1152,2304]{1,0:T(8,128)(2,1)} custom-call(bf16[128,1152]{1,0:T(8,128)(2,1)} %copy-done.55, bf16[256,1152]{1,0:T(8,128)(2,1)} %copy-done.37, bf16[256,1152]{1,0:T(8,128)(2,1)} %copy-done.38, bf16[256,1152]{1,0:T(8,128)(2,1)} %copy-done.39, bf16[128,1152]{1,0:T(8,128)(2,1)} %copy-done.57, bf16[128,2304]{1,0:T(8,128)(2,1)} %copy-done.10, ...), custom_call_target="tpu_custom_call" | custom-call | tf_op jit(solution)/shard_map/pallas_call | solution.py:415
  480.4 10.7 %shard_map.290 = bf16[1152,2304]{1,0:T(8,128)(2,1)} custom-call(bf16[128,1152]{1,0:T(8,128)(2,1)} %copy-done.46, bf16[256,1152]{1,0:T(8,128)(2,1)} %copy-done.29, bf16[256,1152]{1,0:T(8,128)(2,1)} %copy-done.30, bf16[256,1152]{1,0:T(8,128)(2,1)} %copy-done.31, bf16[128,1152]{1,0:T(8,128)(2,1)} %copy-done.48, bf16[128,2304]{1,0:T(8,128)(2,1)} %copy-done.32, ...), custom_call_target="tpu_custom_call" | custom-call | tf_op jit(solution)/shard_map/pallas_call | solution.py:415
  496.1 2.9 convolution_convert_fusion.1.refs_2_.refs_6_.refs_1_
  499.0 4.3 convolution_convert_fusion.refs_5_.refs_9_.refs_4_
  506.4 5.3 shard_map.292
  517.2 2.8 shard_map.294
  520.0 7.4 %shard_map.295 = (f32[256,2304]{1,0:T(8,128)}, bf16[256,2304]{1,0:T(8,128)(2,1)}, f32[1,2304]{1,0:T(1,128)}) custom-call(bf16[512,512]{1,0:T(8,128)(2,1)} %get-tuple-element.1256.refs_0_, bf16[512,256]{1,0:T(8,128)(2,1)} %get-tuple-element.1257.refs_1_, bf16[512,256]{1,0:T(8,128)(2,1)} %get-tuple-element.1258.refs_2_, ...), custom_call_target="tpu_custom_call" | custom-call | tf_op jit(solution)/shard_map/pallas_call | solution.py:279
  534.6 2.8 shard_map.298
  539.6 2.7 shard_map.296
  542.4 10.3 %collective-permute-done.81 = bf16[192,2304]{1,0:T(8,128)(2,1)S(1)} collective-permute-done((bf16[192,2304]{1,0:T(8,128)(2,1)S(1)}, bf16[192,2304]{1,0:T(8,128)(2,1)S(1)}, u32[]{:S(2)}, u32[]{:S(2)}) %collective-permute-start.81) | collective-permute-done | bytes 884768 | tf_op jit(solution)/shard_map/ppermute | solution.py:26
  563.9 20.5 %collective-permute-done.89 = bf16[128,2304]{1,0:T(8,128)(2,1)S(1)} collective-permute-done((bf16[128,2304]{1,0:T(8,128)(2,1)S(1)}, bf16[128,2304]{1,0:T(8,128)(2,1)S(1)}, u32[]{:S(2)}, u32[]{:S(2)}) %collective-permute-start.89) | collective-permute-done | bytes 589856 | tf_op jit(solution)/shard_map/ppermute | solution.py:133
  591.6 11.0 %collective-permute-done.93 = bf16[192,2304]{1,0:T(8,128)(2,1)S(1)} collective-permute-done((bf16[192,2304]{1,0:T(8,128)(2,1)S(1)}, bf16[192,2304]{1,0:T(8,128)(2,1)S(1)}, u32[]{:S(2)}, u32[]{:S(2)}) %collective-permute-start.93) | collective-permute-done | bytes 884768 | tf_op jit(solution)/shard_map/ppermute | solution.py:26
  (580 shorter events, 239.6 us)
Async XLA Ops:
  7.2 129.9 %all-gather.3.cloned.1.call-start = ((), (), s32[]{:S(2)}) async-start(), calls=%async_computation.3 | async-start | bytes 13271040 | tf_op jit(solution)/shard_map/all_gather | solution.py:751
  10.6 24.4 %collective-permute-start.2 = (bf16[128,2304]{1,0:T(8,128)(2,1)S(1)}, bf16[128,2304]{1,0:T(8,128)(2,1)S(1)}, u32[]{:S(2)}, u32[]{:S(2)}) collective-permute-start(bf16[128,2304]{1,0:T(8,128)(2,1)S(1)} %pad_maximum_fusion.3.refs_0_), channel_id=1, source_target_pairs={{0,8},{8,16},{16,24},{24,28},{28,20},{20,12},{12,4},{4,0},{1,9},{9... | collective-permute-start | bytes 1769480 | tf_op jit(solution)/shard_map/ppermute | solution.py:26
  13.3 21.8 %collective-permute-start.3 = (bf16[128,2304]{1,0:T(8,128)(2,1)S(1)}, bf16[128,2304]{1,0:T(8,128)(2,1)}, u32[]{:S(2)}, u32[]{:S(2)}) collective-permute-start(bf16[128,2304]{1,0:T(8,128)(2,1)S(1)} %pad_maximum_fusion.3.refs_0_), channel_id=1, source_target_pairs={{0,4},{8,0},{16,8},{24,16},{28,24},{20,28},{12,20},{4,12},{1,5},{9... | collective-permute-start | bytes 1769480 | tf_op jit(solution)/shard_map/ppermute | solution.py:26
  24.5 15.2 %collective-permute-start.4 = (bf16[128,2304]{1,0:T(8,128)(2,1)S(1)}, bf16[128,2304]{1,0:T(8,128)(2,1)S(1)}, u32[]{:S(2)}, u32[]{:S(2)}) collective-permute-start(bf16[128,2304]{1,0:T(8,128)(2,1)S(1)} %bitcast.80), channel_id=1, source_target_pairs={{0,2},{1,3},{2,0},{3,1},{4,6},{5,7},{6,4},{7,5},{8,10},{9,11},{10,... | collective-permute-start | bytes 1769480 | tf_op jit(solution)/shard_map/ppermute | solution.py:133
  39.7 165.1 %all-gather.5.cloned.1.call-start = ((), (), s32[]{:S(2)}) async-start(), calls=%async_computation.4 | async-start | bytes 6635520 | tf_op jit(solution)/shard_map/all_gather | solution.py:824
  40.5 11.9 %collective-permute-start.14 = (f32[4,2304]{1,0:T(4,128)S(1)}, f32[4,2304]{1,0:T(4,128)S(1)}, u32[]{:S(2)}, u32[]{:S(2)}) collective-permute-start(f32[4,2304]{1,0:T(4,128)S(1)} %add_add_fusion.4), channel_id=1, source_target_pairs={{0,4},{4,0},{8,12},{12,8},{16,20},{20,16},{24,28},{28,24},{1,5},{5... | collective-permute-start | bytes 110600 | tf_op jit(solution)/shard_map/ppermute | solution.py:144
  42.1 11.9 %collective-permute-start.15 = (f32[4,2304]{1,0:T(4,128)S(1)}, f32[4,2304]{1,0:T(4,128)S(1)}, u32[]{:S(2)}, u32[]{:S(2)}) collective-permute-start(f32[4,2304]{1,0:T(4,128)S(1)} %add_add_fusion.4), channel_id=1, source_target_pairs={{0,8},{4,12},{8,0},{12,4},{16,24},{20,28},{24,16},{28,20},{1,9},{5... | collective-permute-start | bytes 110600 | tf_op jit(solution)/shard_map/ppermute | solution.py:144
  44.6 21.7 %collective-permute-start.11 = (bf16[128,2304]{1,0:T(8,128)(2,1)S(1)}, bf16[128,2304]{1,0:T(8,128)(2,1)}, u32[]{:S(2)}, u32[]{:S(2)}) collective-permute-start(bf16[128,2304]{1,0:T(8,128)(2,1)S(1)} %collective-permute-done.2.refs_0_), channel_id=1, source_target_pairs={{0,8},{8,16},{16,24},{24,28},{28,20},{20,12},{12,4},{4,0},{1,9},{9... | collective-permute-start | bytes 1769480 | tf_op jit(solution)/shard_map/ppermute | solution.py:26
  46.3 20.1 %collective-permute-start.12 = (bf16[128,2304]{1,0:T(8,128)(2,1)}, bf16[128,2304]{1,0:T(8,128)(2,1)}, u32[]{:S(2)}, u32[]{:S(2)}) collective-permute-start(bf16[128,2304]{1,0:T(8,128)(2,1)} %collective-permute-done.3.refs_1_), channel_id=1, source_target_pairs={{0,4},{8,0},{16,8},{24,16},{28,24},{20,28},{12,20},{4,12},{1,5},{9... | collective-permute-start | bytes 1769480 | tf_op jit(solution)/shard_map/ppermute | solution.py:26
  52.5 13.8 %collective-permute-start.10 = (bf16[64,2304]{1,0:T(8,128)(2,1)}, bf16[64,2304]{1,0:T(8,128)(2,1)}, u32[]{:S(2)}, u32[]{:S(2)}) collective-permute-start(bf16[64,2304]{1,0:T(8,128)(2,1)} %copy-done.102), channel_id=1, source_target_pairs={{0,4},{8,0},{16,8},{24,16},{28,24},{20,28},{12,20},{4,12},{1,5},{9... | collective-permute-start | bytes 884744 | tf_op jit(solution)/shard_map/ppermute | solution.py:26
  54.0 12.3 %collective-permute-start.9 = (bf16[64,2304]{1,0:T(8,128)(2,1)}, bf16[64,2304]{1,0:T(8,128)(2,1)}, u32[]{:S(2)}, u32[]{:S(2)}) collective-permute-start(bf16[64,2304]{1,0:T(8,128)(2,1)} %copy-done.101), channel_id=1, source_target_pairs={{0,8},{8,16},{16,24},{24,28},{28,20},{20,12},{12,4},{4,0},{1,9},{9... | collective-permute-start | bytes 884744 | tf_op jit(solution)/shard_map/ppermute | solution.py:26
  54.5 11.8 %collective-permute-start.13 = (bf16[128,2304]{1,0:T(8,128)(2,1)S(1)}, bf16[128,2304]{1,0:T(8,128)(2,1)S(1)}, u32[]{:S(2)}, u32[]{:S(2)}) collective-permute-start(bf16[128,2304]{1,0:T(8,128)(2,1)S(1)} %collective-permute-done.4), channel_id=1, source_target_pairs={{0,1},{1,0},{2,3},{3,2},{4,5},{5,4},{6,7},{7,6},{8,9},{9,8},{10,11... | collective-permute-start | bytes 1769480 | tf_op jit(solution)/shard_map/ppermute | solution.py:138
  66.3 11.8 %collective-permute-start.19 = (f32[4,2304]{1,0:T(4,128)}, f32[4,2304]{1,0:T(4,128)}, u32[]{:S(2)}, u32[]{:S(2)}) collective-permute-start(f32[4,2304]{1,0:T(4,128)} %add_add_fusion.3), channel_id=1, source_target_pairs={{0,16},{4,20},{8,24},{12,28},{16,0},{20,4},{24,8},{28,12},{1,17},{... | collective-permute-start | bytes 110600 | tf_op jit(solution)/shard_map/ppermute | solution.py:144
  88.1 15.7 %collective-permute-start.22 = (bf16[128,2304]{1,0:T(8,128)(2,1)}, bf16[128,2304]{1,0:T(8,128)(2,1)}, u32[]{:S(2)}, u32[]{:S(2)}) collective-permute-start(bf16[128,2304]{1,0:T(8,128)(2,1)} %collective-permute-done.11.refs_0_), channel_id=1, source_target_pairs={{0,8},{8,16},{16,24},{24,28},{28,20},{20,12},{12,4},{4,0},{1,9},{9... | collective-permute-start | bytes 1769480 | tf_op jit(solution)/shard_map/ppermute | solution.py:26
  89.6 14.2 %collective-permute-start.23 = (bf16[128,2304]{1,0:T(8,128)(2,1)}, bf16[128,2304]{1,0:T(8,128)(2,1)}, u32[]{:S(2)}, u32[]{:S(2)}) collective-permute-start(bf16[128,2304]{1,0:T(8,128)(2,1)} %collective-permute-done.12.refs_1_), channel_id=1, source_target_pairs={{0,4},{8,0},{16,8},{24,16},{28,24},{20,28},{12,20},{4,12},{1,5},{9... | collective-permute-start | bytes 1769480 | tf_op jit(solution)/shard_map/ppermute | solution.py:26
  103.8 18.8 %collective-permute-start.24 = (bf16[8,128,256]{2,1,0:T(8,128)(2,1)}, bf16[8,128,256]{2,1,0:T(8,128)(2,1)S(1)}, u32[]{:S(2)}, u32[]{:S(2)}) collective-permute-start(bf16[8,128,256]{2,1,0:T(8,128)(2,1)} %bitcast.21.refs_0_), channel_id=1, source_target_pairs={{0,8},{8,16},{16,24},{24,28},{28,20},{20,12},{12,4},{4,0},{1,9},{9... | collective-permute-start | bytes 1572872 | tf_op jit(solution)/shard_map/ppermute | solution.py:26
  105.3 17.3 %collective-permute-start.25 = (bf16[8,128,256]{2,1,0:T(8,128)(2,1)}, bf16[8,128,256]{2,1,0:T(8,128)(2,1)S(1)}, u32[]{:S(2)}, u32[]{:S(2)}) collective-permute-start(bf16[8,128,256]{2,1,0:T(8,128)(2,1)} %bitcast.21.refs_0_), channel_id=1, source_target_pairs={{0,4},{8,0},{16,8},{24,16},{28,24},{20,28},{12,20},{4,12},{1,5},{9... | collective-permute-start | bytes 1572872 | tf_op jit(solution)/shard_map/ppermute | solution.py:26
  107.5 13.2 %collective-permute-start.26 = (bf16[64,2304]{1,0:T(8,128)(2,1)}, bf16[64,2304]{1,0:T(8,128)(2,1)}, u32[]{:S(2)}, u32[]{:S(2)}) collective-permute-start(bf16[64,2304]{1,0:T(8,128)(2,1)} %slice.111), channel_id=1, source_target_pairs={{0,8},{8,16},{16,24},{24,28},{28,20},{20,12},{12,4},{4,0},{1,9},{9... | collective-permute-start | bytes 884744 | tf_op jit(solution)/shard_map/ppermute | solution.py:26
  110.7 11.9 %collective-permute-start.27 = (bf16[64,2304]{1,0:T(8,128)(2,1)}, bf16[64,2304]{1,0:T(8,128)(2,1)}, u32[]{:S(2)}, u32[]{:S(2)}) collective-permute-start(bf16[64,2304]{1,0:T(8,128)(2,1)} %slice.112), channel_id=1, source_target_pairs={{0,4},{8,0},{16,8},{24,16},{28,24},{20,28},{12,20},{4,12},{1,5},{9... | collective-permute-start | bytes 884744 | tf_op jit(solution)/shard_map/ppermute | solution.py:26
  123.4 13.8 %collective-permute-start.28 = (bf16[8,128,256]{2,1,0:T(8,128)(2,1)S(1)}, bf16[8,128,256]{2,1,0:T(8,128)(2,1)}, u32[]{:S(2)}, u32[]{:S(2)}) collective-permute-start(bf16[8,128,256]{2,1,0:T(8,128)(2,1)S(1)} %collective-permute-done.24.refs_0_), channel_id=1, source_target_pairs={{0,8},{8,16},{16,24},{24,28},{28,20},{20,12},{12,4},{4,0},{1,9},{9... | collective-permute-start | bytes 1572872 | tf_op jit(solution)/shard_map/ppermute | solution.py:26
  123.9 13.3 %collective-permute-start.29 = (bf16[8,128,256]{2,1,0:T(8,128)(2,1)}, bf16[8,128,256]{2,1,0:T(8,128)(2,1)S(1)}, u32[]{:S(2)}, u32[]{:S(2)}) collective-permute-start(bf16[8,128,256]{2,1,0:T(8,128)(2,1)} %copy-done.99), channel_id=1, source_target_pairs={{0,4},{8,0},{16,8},{24,16},{28,24},{20,28},{12,20},{4,12},{1,5},{9... | collective-permute-start | bytes 1572872 | tf_op jit(solution)/shard_map/ppermute | solution.py:26
  137.2 369.2 %reduce-scatter.4.cloned.1.call-start = ((), (), s32[]{:S(2)}) async-start(), calls=%async_computation.5 | async-start | bytes 6635520 | tf_op jit(solution)/shard_map/reduce_scatter | solution.py:908
  138.0 12.3 %collective-permute-start.30 = (bf16[8,128,256]{2,1,0:T(8,128)(2,1)}, bf16[8,128,256]{2,1,0:T(8,128)(2,1)S(1)}, u32[]{:S(2)}, u32[]{:S(2)}) collective-permute-start(bf16[8,128,256]{2,1,0:T(8,128)(2,1)} %collective-permute-done.28.refs_0_), channel_id=1, source_target_pairs={{0,8},{8,16},{16,24},{24,28},{28,20},{20,12},{12,4},{4,0},{1,9},{9... | collective-permute-start | bytes 1572872 | tf_op jit(solution)/shard_map/ppermute | solution.py:26
  138.6 12.2 %collective-permute-start.31 = (bf16[8,128,256]{2,1,0:T(8,128)(2,1)}, bf16[8,128,256]{2,1,0:T(8,128)(2,1)S(1)}, u32[]{:S(2)}, u32[]{:S(2)}) collective-permute-start(bf16[8,128,256]{2,1,0:T(8,128)(2,1)} %copy-done.97), channel_id=1, source_target_pairs={{0,4},{8,0},{16,8},{24,16},{28,24},{20,28},{12,20},{4,12},{1,5},{9... | collective-permute-start | bytes 1572872 | tf_op jit(solution)/shard_map/ppermute | solution.py:26
  172.6 15.4 %collective-permute-start.35 = (bf16[128,2304]{1,0:T(8,128)(2,1)S(1)}, bf16[128,2304]{1,0:T(8,128)(2,1)S(1)}, u32[]{:S(2)}, u32[]{:S(2)}) collective-permute-start(bf16[128,2304]{1,0:T(8,128)(2,1)S(1)} %get-tuple-element.1346), channel_id=1, source_target_pairs={{0,2},{1,3},{2,0},{3,1},{4,6},{5,7},{6,4},{7,5},{8,10},{9,11},{10,... | collective-permute-start | bytes 1769480 | tf_op jit(solution)/shard_map/ppermute | solution.py:133
  189.9 14.7 %collective-permute-start.36 = (bf16[128,2304]{1,0:T(8,128)(2,1)S(1)}, bf16[128,2304]{1,0:T(8,128)(2,1)S(1)}, u32[]{:S(2)}, u32[]{:S(2)}) collective-permute-start(bf16[128,2304]{1,0:T(8,128)(2,1)S(1)} %get-tuple-element.1159.refs_0_.refs_5_), channel_id=1, source_target_pairs={{0,8},{8,16},{16,24},{24,28},{28,20},{20,12},{12,4},{4,0},{1,9},{9... | collective-permute-start | bytes 1769480 | tf_op jit(solution)/shard_map/ppermute | solution.py:26
  190.4 14.5 %collective-permute-start.37 = (bf16[128,2304]{1,0:T(8,128)(2,1)S(1)}, bf16[128,2304]{1,0:T(8,128)(2,1)}, u32[]{:S(2)}, u32[]{:S(2)}) collective-permute-start(bf16[128,2304]{1,0:T(8,128)(2,1)S(1)} %get-tuple-element.1159.refs_0_.refs_5_), channel_id=1, source_target_pairs={{0,4},{8,0},{16,8},{24,16},{28,24},{20,28},{12,20},{4,12},{1,5},{9... | collective-permute-start | bytes 1769480 | tf_op jit(solution)/shard_map/ppermute | solution.py:26
  204.9 13.5 %collective-permute-start.38 = (bf16[128,2304]{1,0:T(8,128)(2,1)S(1)}, bf16[128,2304]{1,0:T(8,128)(2,1)S(1)}, u32[]{:S(2)}, u32[]{:S(2)}) collective-permute-start(bf16[128,2304]{1,0:T(8,128)(2,1)S(1)} %collective-permute-done.36.refs_0_.refs_6_), channel_id=1, source_target_pairs={{0,8},{8,16},{16,24},{24,28},{28,20},{20,12},{12,4},{4,0},{1,9},{9... | collective-permute-start | bytes 1769480 | tf_op jit(solution)/shard_map/ppermute | solution.py:26
  206.6 13.6 %collective-permute-start.39 = (bf16[128,2304]{1,0:T(8,128)(2,1)}, bf16[128,2304]{1,0:T(8,128)(2,1)S(1)}, u32[]{:S(2)}, u32[]{:S(2)}) collective-permute-start(bf16[128,2304]{1,0:T(8,128)(2,1)} %collective-permute-done.37.refs_1_.refs_7_), channel_id=1, source_target_pairs={{0,4},{8,0},{16,8},{24,16},{28,24},{20,28},{12,20},{4,12},{1,5},{9... | collective-permute-start | bytes 1769480 | tf_op jit(solution)/shard_map/ppermute | solution.py:26
  220.2 12.5 %collective-permute-start.40 = (bf16[128,2304]{1,0:T(8,128)(2,1)S(1)}, bf16[128,2304]{1,0:T(8,128)(2,1)S(1)}, u32[]{:S(2)}, u32[]{:S(2)}) collective-permute-start(bf16[128,2304]{1,0:T(8,128)(2,1)S(1)} %collective-permute-done.38.refs_0_.refs_8_), channel_id=1, source_target_pairs={{0,8},{8,16},{16,24},{24,28},{28,20},{20,12},{12,4},{4,0},{1,9},{9... | collective-permute-start | bytes 1769480 | tf_op jit(solution)/shard_map/ppermute | solution.py:26
  221.8 12.4 %collective-permute-start.41 = (bf16[128,2304]{1,0:T(8,128)(2,1)S(1)}, bf16[128,2304]{1,0:T(8,128)(2,1)S(1)}, u32[]{:S(2)}, u32[]{:S(2)}) collective-permute-start(bf16[128,2304]{1,0:T(8,128)(2,1)S(1)} %collective-permute-done.39.refs_1_.refs_9_), channel_id=1, source_target_pairs={{0,4},{8,0},{16,8},{24,16},{28,24},{20,28},{12,20},{4,12},{1,5},{9... | collective-permute-start | bytes 1769480 | tf_op jit(solution)/shard_map/ppermute | solution.py:26
  259.4 13.9 %collective-permute-start.46 = (bf16[128,2304]{1,0:T(8,128)(2,1)S(1)}, bf16[128,2304]{1,0:T(8,128)(2,1)S(1)}, u32[]{:S(2)}, u32[]{:S(2)}) collective-permute-start(bf16[128,2304]{1,0:T(8,128)(2,1)S(1)} %add_convert_fusion.17), channel_id=1, source_target_pairs={{0,8},{8,16},{16,24},{24,28},{28,20},{20,12},{12,4},{4,0},{1,9},{9... | collective-permute-start | bytes 1769480 | tf_op jit(solution)/shard_map/ppermute | solution.py:26
  260.0 13.7 %collective-permute-start.47 = (bf16[128,2304]{1,0:T(8,128)(2,1)S(1)}, bf16[128,2304]{1,0:T(8,128)(2,1)S(1)}, u32[]{:S(2)}, u32[]{:S(2)}) collective-permute-start(bf16[128,2304]{1,0:T(8,128)(2,1)S(1)} %add_convert_fusion.16), channel_id=1, source_target_pairs={{0,4},{8,0},{16,8},{24,16},{28,24},{20,28},{12,20},{4,12},{1,5},{9... | collective-permute-start | bytes 1769480 | tf_op jit(solution)/shard_map/ppermute | solution.py:26
  274.0 14.8 %collective-permute-start.48 = (bf16[128,2304]{1,0:T(8,128)(2,1)S(1)}, bf16[128,2304]{1,0:T(8,128)(2,1)S(1)}, u32[]{:S(2)}, u32[]{:S(2)}) collective-permute-start(bf16[128,2304]{1,0:T(8,128)(2,1)S(1)} %add_convert_fusion.15), channel_id=1, source_target_pairs={{0,8},{8,16},{16,24},{24,28},{28,20},{20,12},{12,4},{4,0},{1,9},{9... | collective-permute-start | bytes 1769480 | tf_op jit(solution)/shard_map/ppermute | solution.py:26
  275.0 16.3 %collective-permute-start.49 = (bf16[128,2304]{1,0:T(8,128)(2,1)S(1)}, bf16[128,2304]{1,0:T(8,128)(2,1)S(1)}, u32[]{:S(2)}, u32[]{:S(2)}) collective-permute-start(bf16[128,2304]{1,0:T(8,128)(2,1)S(1)} %add_convert_fusion.14), channel_id=1, source_target_pairs={{0,4},{8,0},{16,8},{24,16},{28,24},{20,28},{12,20},{4,12},{1,5},{9... | collective-permute-start | bytes 1769480 | tf_op jit(solution)/shard_map/ppermute | solution.py:26
  291.6 16.0 %collective-permute-start.50 = (bf16[128,2304]{1,0:T(8,128)(2,1)S(1)}, bf16[128,2304]{1,0:T(8,128)(2,1)S(1)}, u32[]{:S(2)}, u32[]{:S(2)}) collective-permute-start(bf16[128,2304]{1,0:T(8,128)(2,1)S(1)} %add_convert_fusion.13), channel_id=1, source_target_pairs={{0,8},{8,16},{16,24},{24,28},{28,20},{20,12},{12,4},{4,0},{1,9},{9... | collective-permute-start | bytes 1769480 | tf_op jit(solution)/shard_map/ppermute | solution.py:26
  292.6 16.1 %collective-permute-start.51 = (bf16[128,2304]{1,0:T(8,128)(2,1)S(1)}, bf16[128,2304]{1,0:T(8,128)(2,1)S(1)}, u32[]{:S(2)}, u32[]{:S(2)}) collective-permute-start(bf16[128,2304]{1,0:T(8,128)(2,1)S(1)} %add_convert_fusion.12), channel_id=1, source_target_pairs={{0,4},{8,0},{16,8},{24,16},{28,24},{20,28},{12,20},{4,12},{1,5},{9... | collective-permute-start | bytes 1769480 | tf_op jit(solution)/shard_map/ppermute | solution.py:26
  310.3 13.8 %collective-permute-start.52 = (bf16[128,2304]{1,0:T(8,128)(2,1)S(1)}, bf16[128,2304]{1,0:T(8,128)(2,1)S(1)}, u32[]{:S(2)}, u32[]{:S(2)}) collective-permute-start(bf16[128,2304]{1,0:T(8,128)(2,1)S(1)} %get-tuple-element.1214.refs_0_.refs_5_), channel_id=1, source_target_pairs={{0,8},{8,16},{16,24},{24,28},{28,20},{20,12},{12,4},{4,0},{1,9},{9... | collective-permute-start | bytes 1769480 | tf_op jit(solution)/shard_map/ppermute | solution.py:26
  310.3 13.8 %collective-permute-start.53 = (bf16[128,2304]{1,0:T(8,128)(2,1)S(1)}, bf16[128,2304]{1,0:T(8,128)(2,1)S(1)}, u32[]{:S(2)}, u32[]{:S(2)}) collective-permute-start(bf16[128,2304]{1,0:T(8,128)(2,1)S(1)} %get-tuple-element.1214.refs_0_.refs_5_), channel_id=1, source_target_pairs={{0,4},{8,0},{16,8},{24,16},{28,24},{20,28},{12,20},{4,12},{1,5},{9... | collective-permute-start | bytes 1769480 | tf_op jit(solution)/shard_map/ppermute | solution.py:26
  324.1 13.2 %collective-permute-start.54 = (bf16[128,2304]{1,0:T(8,128)(2,1)S(1)}, bf16[128,2304]{1,0:T(8,128)(2,1)S(1)}, u32[]{:S(2)}, u32[]{:S(2)}) collective-permute-start(bf16[128,2304]{1,0:T(8,128)(2,1)S(1)} %collective-permute-done.52.refs_0_.refs_6_), channel_id=1, source_target_pairs={{0,8},{8,16},{16,24},{24,28},{28,20},{20,12},{12,4},{4,0},{1,9},{9... | collective-permute-start | bytes 1769480 | tf_op jit(solution)/shard_map/ppermute | solution.py:26
  324.4 12.9 %collective-permute-start.55 = (bf16[128,2304]{1,0:T(8,128)(2,1)S(1)}, bf16[128,2304]{1,0:T(8,128)(2,1)S(1)}, u32[]{:S(2)}, u32[]{:S(2)}) collective-permute-start(bf16[128,2304]{1,0:T(8,128)(2,1)S(1)} %collective-permute-done.53.refs_1_.refs_7_), channel_id=1, source_target_pairs={{0,4},{8,0},{16,8},{24,16},{28,24},{20,28},{12,20},{4,12},{1,5},{9... | collective-permute-start | bytes 1769480 | tf_op jit(solution)/shard_map/ppermute | solution.py:26
  372.4 15.1 %collective-permute-start.62 = (bf16[128,2304]{1,0:T(8,128)(2,1)}, bf16[128,2304]{1,0:T(8,128)(2,1)S(1)}, u32[]{:S(2)}, u32[]{:S(2)}) collective-permute-start(bf16[128,2304]{1,0:T(8,128)(2,1)} %add_convert_fusion.11), channel_id=1, source_target_pairs={{0,8},{8,16},{16,24},{24,28},{28,20},{20,12},{12,4},{4,0},{1,9},{9... | collective-permute-start | bytes 1769480 | tf_op jit(solution)/shard_map/ppermute | solution.py:26
  372.8 14.7 %collective-permute-start.63 = (bf16[128,2304]{1,0:T(8,128)(2,1)}, bf16[128,2304]{1,0:T(8,128)(2,1)}, u32[]{:S(2)}, u32[]{:S(2)}) collective-permute-start(bf16[128,2304]{1,0:T(8,128)(2,1)} %add_convert_fusion.10), channel_id=1, source_target_pairs={{0,4},{8,0},{16,8},{24,16},{28,24},{20,28},{12,20},{4,12},{1,5},{9... | collective-permute-start | bytes 1769480 | tf_op jit(solution)/shard_map/ppermute | solution.py:26
  390.3 11.5 %collective-permute-start.65 = (bf16[128,2304]{1,0:T(8,128)(2,1)S(1)}, bf16[128,2304]{1,0:T(8,128)(2,1)S(1)}, u32[]{:S(2)}, u32[]{:S(2)}) collective-permute-start(bf16[128,2304]{1,0:T(8,128)(2,1)S(1)} %add_convert_fusion.8), channel_id=1, source_target_pairs={{0,4},{8,0},{16,8},{24,16},{28,24},{20,28},{12,20},{4,12},{1,5},{9... | collective-permute-start | bytes 1769480 | tf_op jit(solution)/shard_map/ppermute | solution.py:26
  416.1 19.5 %collective-permute-start.68 = (bf16[128,2304]{1,0:T(8,128)(2,1)}, bf16[128,2304]{1,0:T(8,128)(2,1)}, u32[]{:S(2)}, u32[]{:S(2)}) collective-permute-start(bf16[128,2304]{1,0:T(8,128)(2,1)} %get-tuple-element.1033.d_attn_ref), channel_id=1, source_target_pairs={{0,2},{1,3},{2,0},{3,1},{4,6},{5,7},{6,4},{7,5},{8,10},{9,11},{10,... | collective-permute-start | bytes 1769480 | tf_op jit(solution)/shard_map/ppermute | solution.py:133
  435.6 118.0 %reduce-scatter.6.cloned.1.call-start = ((), (), s32[]{:S(2)}) async-start(), calls=%async_computation.6 | async-start | bytes 6635520 | tf_op jit(solution)/shard_map/reduce_scatter | solution.py:908
  461.6 13.2 %collective-permute-start.73 = (bf16[2,4,128,256]{3,2,1,0:T(8,128)(2,1)}, bf16[2,4,128,256]{3,2,1,0:T(8,128)(2,1)S(1)}, u32[]{:S(2)}, u32[]{:S(2)}) collective-permute-start(bf16[2,4,128,256]{3,2,1,0:T(8,128)(2,1)} %get-tuple-element.1150), channel_id=1, source_target_pairs={{0,8},{8,16},{16,24},{24,28},{28,20},{20,12},{12,4},{4,0},{1,9},{9... | collective-permute-start | bytes 1572872 | tf_op jit(solution)/shard_map/ppermute | solution.py:26
  462.6 13.2 %collective-permute-start.74 = (bf16[2,4,128,256]{3,2,1,0:T(8,128)(2,1)}, bf16[2,4,128,256]{3,2,1,0:T(8,128)(2,1)}, u32[]{:S(2)}, u32[]{:S(2)}) collective-permute-start(bf16[2,4,128,256]{3,2,1,0:T(8,128)(2,1)} %get-tuple-element.1151), channel_id=1, source_target_pairs={{0,4},{8,0},{16,8},{24,16},{28,24},{20,28},{12,20},{4,12},{1,5},{9... | collective-permute-start | bytes 1572872 | tf_op jit(solution)/shard_map/ppermute | solution.py:26
  478.3 126.2 %reduce-scatter.8.cloned.1.call-start = ((), (), s32[]{:S(2)}) async-start(), calls=%async_computation.7 | async-start | bytes 6635520 | tf_op jit(solution)/shard_map/reduce_scatter | solution.py:908
  478.3 12.8 %collective-permute-start.75 = (bf16[2,4,128,256]{3,2,1,0:T(8,128)(2,1)}, bf16[2,4,128,256]{3,2,1,0:T(8,128)(2,1)}, u32[]{:S(2)}, u32[]{:S(2)}) collective-permute-start(bf16[2,4,128,256]{3,2,1,0:T(8,128)(2,1)} %get-tuple-element.1205), channel_id=1, source_target_pairs={{0,8},{8,16},{16,24},{24,28},{28,20},{20,12},{12,4},{4,0},{1,9},{9... | collective-permute-start | bytes 1572872 | tf_op jit(solution)/shard_map/ppermute | solution.py:26
  479.4 12.3 %collective-permute-start.76 = (bf16[2,4,128,256]{3,2,1,0:T(8,128)(2,1)}, bf16[2,4,128,256]{3,2,1,0:T(8,128)(2,1)}, u32[]{:S(2)}, u32[]{:S(2)}) collective-permute-start(bf16[2,4,128,256]{3,2,1,0:T(8,128)(2,1)} %get-tuple-element.1206), channel_id=1, source_target_pairs={{0,4},{8,0},{16,8},{24,16},{28,24},{20,28},{12,20},{4,12},{1,5},{9... | collective-permute-start | bytes 1572872 | tf_op jit(solution)/shard_map/ppermute | solution.py:26
  494.1 11.4 %collective-permute-start.77 = (bf16[2,4,128,256]{3,2,1,0:T(8,128)(2,1)}, bf16[2,4,128,256]{3,2,1,0:T(8,128)(2,1)}, u32[]{:S(2)}, u32[]{:S(2)}) collective-permute-start(bf16[2,4,128,256]{3,2,1,0:T(8,128)(2,1)} %get-tuple-element.1231), channel_id=1, source_target_pairs={{0,8},{8,16},{16,24},{24,28},{28,20},{20,12},{12,4},{4,0},{1,9},{9... | collective-permute-start | bytes 1572872 | tf_op jit(solution)/shard_map/ppermute | solution.py:26
  513.8 14.3 %collective-permute-start.79 = (bf16[96,2304]{1,0:T(8,128)(2,1)}, bf16[96,2304]{1,0:T(8,128)(2,1)S(1)}, u32[]{:S(2)}, u32[]{:S(2)}) collective-permute-start(bf16[96,2304]{1,0:T(8,128)(2,1)} %get-tuple-element.1248), channel_id=1, source_target_pairs={{0,8},{8,16},{16,24},{24,28},{28,20},{20,12},{12,4},{4,0},{1,9},{9... | collective-permute-start | bytes 1327112 | tf_op jit(solution)/shard_map/ppermute | solution.py:26
  515.0 13.2 %collective-permute-start.80 = (bf16[96,2304]{1,0:T(8,128)(2,1)}, bf16[96,2304]{1,0:T(8,128)(2,1)S(1)}, u32[]{:S(2)}, u32[]{:S(2)}) collective-permute-start(bf16[96,2304]{1,0:T(8,128)(2,1)} %get-tuple-element.1249), channel_id=1, source_target_pairs={{0,4},{8,0},{16,8},{24,16},{28,24},{20,28},{12,20},{4,12},{1,5},{9... | collective-permute-start | bytes 1327112 | tf_op jit(solution)/shard_map/ppermute | solution.py:26
  528.7 13.6 %collective-permute-start.85 = (f32[4,2304]{1,0:T(4,128)S(1)}, f32[4,2304]{1,0:T(4,128)S(1)}, u32[]{:S(2)}, u32[]{:S(2)}) collective-permute-start(f32[4,2304]{1,0:T(4,128)S(1)} %pad_maximum_fusion.5), channel_id=1, source_target_pairs={{0,2},{1,3},{2,0},{3,1},{4,6},{5,7},{6,4},{7,5},{8,10},{9,11},{10,... | collective-permute-start | bytes 110600 | tf_op jit(solution)/shard_map/ppermute | solution.py:144
  530.2 12.2 %collective-permute-start.86 = (f32[4,2304]{1,0:T(4,128)S(1)}, f32[4,2304]{1,0:T(4,128)S(1)}, u32[]{:S(2)}, u32[]{:S(2)}) collective-permute-start(f32[4,2304]{1,0:T(4,128)S(1)} %pad_maximum_fusion.5), channel_id=1, source_target_pairs={{0,3},{1,2},{2,1},{3,0},{4,7},{5,6},{6,5},{7,4},{8,11},{9,10},{10,... | collective-permute-start | bytes 110600 | tf_op jit(solution)/shard_map/ppermute | solution.py:144
  530.6 23.1 %collective-permute-start.83 = (bf16[256,2304]{1,0:T(8,128)(2,1)}, bf16[256,2304]{1,0:T(8,128)(2,1)S(1)}, u32[]{:S(2)}, u32[]{:S(2)}) collective-permute-start(bf16[256,2304]{1,0:T(8,128)(2,1)} %get-tuple-element.1286), channel_id=1, source_target_pairs={{0,1},{1,0},{2,3},{3,2},{4,5},{5,4},{6,7},{7,6},{8,9},{9,8},{10,11... | collective-permute-start | bytes 3538952 | tf_op jit(solution)/shard_map/ppermute | solution.py:138
  530.9 21.7 %collective-permute-start.81 = (bf16[192,2304]{1,0:T(8,128)(2,1)S(1)}, bf16[192,2304]{1,0:T(8,128)(2,1)S(1)}, u32[]{:S(2)}, u32[]{:S(2)}) collective-permute-start(bf16[192,2304]{1,0:T(8,128)(2,1)S(1)} %add_convert_fusion.5), channel_id=1, source_target_pairs={{0,8},{8,16},{16,24},{24,28},{28,20},{20,12},{12,4},{4,0},{1,9},{9... | collective-permute-start | bytes 2654216 | tf_op jit(solution)/shard_map/ppermute | solution.py:26
  532.1 21.5 %collective-permute-start.82 = (bf16[192,2304]{1,0:T(8,128)(2,1)S(1)}, bf16[192,2304]{1,0:T(8,128)(2,1)}, u32[]{:S(2)}, u32[]{:S(2)}) collective-permute-start(bf16[192,2304]{1,0:T(8,128)(2,1)S(1)} %add_convert_fusion.4), channel_id=1, source_target_pairs={{0,4},{8,0},{16,8},{24,16},{28,24},{20,28},{12,20},{4,12},{1,5},{9... | collective-permute-start | bytes 2654216 | tf_op jit(solution)/shard_map/ppermute | solution.py:26
  560.3 24.2 %collective-permute-start.89 = (bf16[128,2304]{1,0:T(8,128)(2,1)S(1)}, bf16[128,2304]{1,0:T(8,128)(2,1)S(1)}, u32[]{:S(2)}, u32[]{:S(2)}) collective-permute-start(bf16[128,2304]{1,0:T(8,128)(2,1)S(1)} %slice.178), channel_id=1, source_target_pairs={{0,2},{1,3},{2,0},{3,1},{4,6},{5,7},{6,4},{7,5},{8,10},{9,11},{10,... | collective-permute-start | bytes 1769480 | tf_op jit(solution)/shard_map/ppermute | solution.py:133
  561.8 22.7 %collective-permute-start.87 = (bf16[192,2304]{1,0:T(8,128)(2,1)S(1)}, bf16[192,2304]{1,0:T(8,128)(2,1)S(1)}, u32[]{:S(2)}, u32[]{:S(2)}) collective-permute-start(bf16[192,2304]{1,0:T(8,128)(2,1)S(1)} %add_convert_fusion.3), channel_id=1, source_target_pairs={{0,8},{8,16},{16,24},{24,28},{28,20},{20,12},{12,4},{4,0},{1,9},{9... | collective-permute-start | bytes 2654216 | tf_op jit(solution)/shard_map/ppermute | solution.py:26
  562.6 22.0 %collective-permute-start.88 = (bf16[192,2304]{1,0:T(8,128)(2,1)S(1)}, bf16[192,2304]{1,0:T(8,128)(2,1)S(1)}, u32[]{:S(2)}, u32[]{:S(2)}) collective-permute-start(bf16[192,2304]{1,0:T(8,128)(2,1)S(1)} %add_convert_fusion.2), channel_id=1, source_target_pairs={{0,4},{8,0},{16,8},{24,16},{28,24},{20,28},{12,20},{4,12},{1,5},{9... | collective-permute-start | bytes 2654216 | tf_op jit(solution)/shard_map/ppermute | solution.py:26
  586.0 16.6 %collective-permute-start.93 = (bf16[192,2304]{1,0:T(8,128)(2,1)S(1)}, bf16[192,2304]{1,0:T(8,128)(2,1)S(1)}, u32[]{:S(2)}, u32[]{:S(2)}) collective-permute-start(bf16[192,2304]{1,0:T(8,128)(2,1)S(1)} %add_convert_fusion.1), channel_id=1, source_target_pairs={{0,8},{8,16},{16,24},{24,28},{28,20},{20,12},{12,4},{4,0},{1,9},{9... | collective-permute-start | bytes 2654216 | tf_op jit(solution)/shard_map/ppermute | solution.py:26
  587.2 17.0 %collective-permute-start.94 = (bf16[192,2304]{1,0:T(8,128)(2,1)S(1)}, bf16[192,2304]{1,0:T(8,128)(2,1)S(1)}, u32[]{:S(2)}, u32[]{:S(2)}) collective-permute-start(bf16[192,2304]{1,0:T(8,128)(2,1)S(1)} %add_convert_fusion), channel_id=1, source_target_pairs={{0,4},{8,0},{16,8},{24,16},{28,24},{20,28},{12,20},{4,12},{1,5},{9... | collective-permute-start | bytes 2654216 | tf_op jit(solution)/shard_map/ppermute | solution.py:26
  (170 other events, 1693.7 us)
Sparse Core Ops, SparseCore 0:
  39.9 72.2 all-gather.2
  137.3 38.7 all-gather.4
  435.8 50.5 reduce-scatter.3
  488.9 53.3 reduce-scatter.5
  544.8 59.6 reduce-scatter.7
